TPU v7x, 256 devices: a whole 4x4x8 slice. The times are simulated.
256 devices in a mesh: grp: 32 (over x, y, z_lo), sec: 8 (over z_hi, core).
Axes of the slice: x: 4, y: 4, z: 8 (z_hi: 4, z_lo: 2; z = z_hi * 2 + z_lo), core: 2. Of those that a mesh axis runs over, the one named last changes fastest.
Arguments:
- coefficients: bfloat16 [65536, 4096], P('sec', 'grp'), may hold values from -0.1875 to 0.1875
- energy_gaps: float32 [4096], P('grp'), may hold values from 0.1 to 10
- metric_blocks: bfloat16 [512, 2, 128, 128], P('sec'), as said below
- metric_index: int32 [512, 2], P('sec'), may hold values from -1 to 511, as said below
- coulomb_blocks: bfloat16 [512, 2, 128, 128], P('sec'), as said below
- coulomb_index: int32 [512, 2], P('sec'), may hold values from -1 to 511, as said below
Outputs:
- response_tiles: float32 [8, 8192, 256], P('sec', 'grp')
Inputs may be any that keep to these rules, and one draw needn't show every extreme that they name: `metric_index`: slot 0 of block row r is r itself; every other live slot names a block within 8 blocks of r, counted periodically over 512 blocks; padded slots hold -1 and some slot is padded; in the first block row of each run of 64 blocks every other slot is live and names a block below it, in the last one every other slot is live and names a block above it. `coulomb_index`: slot 0 of block row r is r itself; every other live slot names a block within 8 blocks of r, counted periodically over 512 blocks; padded slots hold -1 and some slot is padded; in the first block row of each run of 64 blocks every other slot is live and names a block below it, in the last one every other slot is live and names a block above it. `metric_blocks`: padded slots hold arbitrary blocks. `coulomb_blocks`: padded slots hold arbitrary blocks.
All inputs are finite; a program needn't handle non-finite values.
Results may differ from a plain program's by a relative error of at most 0.0054.
Values may be sent and summed in bfloat16 or wider, within the bound.
No kernel may reach another device: no remote copies, remote signals or barrier semaphores. Data moves between devices by JAX's collectives and lax.ppermute only.
A program may use at most 64 MiB of HBM per device.

v0:
```python
import jax
import jax.numpy as jnp
from jax import lax
from jax.sharding import PartitionSpec as P

QC = 256


frequency_sq = 1.0


def with_halo(cells, sides, width):
    for axis, dim in sides:
        count = lax.axis_size(axis)
        head = lax.slice_in_dim(cells, 0, width, axis=dim)
        tail = lax.slice_in_dim(cells, cells.shape[dim] - width, cells.shape[dim], axis=dim)
        cells = jnp.concatenate(
            [
                lax.ppermute(tail, axis, [(i, (i + 1) % count) for i in range(count)]),
                cells,
                lax.ppermute(head, axis, [((i + 1) % count, i) for i in range(count)]),
            ],
            axis=dim,
        )
    return cells


def block_positions(index):
    rows_here = index.shape[0]
    reach_blocks = rows_here // 8
    block_total = rows_here * lax.axis_size("sec")
    local_rows = jnp.arange(rows_here, dtype=jnp.int32)[:, None]
    row_global = lax.axis_index("sec") * rows_here + local_rows
    distance = (index - row_global + block_total // 2) % block_total - block_total // 2
    live_slots = index >= 0
    offsets = jnp.where(live_slots, local_rows + reach_blocks + distance, local_rows + reach_blocks)
    return (offsets, live_slots)


def prepare(blocks, index):
    offsets, live_slots = block_positions(index)
    kept = jnp.where(live_slots[:, :, None, None], blocks, jnp.zeros_like(blocks))
    return (kept, offsets)


def apply_operator(kept, offsets, field):
    rows_here = kept.shape[0]
    block_size = kept.shape[2]
    reach_blocks = rows_here // 8
    padded = with_halo(field, (("sec", 0),), reach_blocks * block_size)
    stacked = padded.reshape(rows_here + 2 * reach_blocks, block_size, field.shape[1])
    chosen = stacked[offsets]
    result = jnp.einsum("rkab,rkbc->rac", kept, chosen, preferred_element_type=jnp.float32)
    return result.reshape(rows_here * block_size, field.shape[1]).astype(jnp.bfloat16)


def on_device(
    coefficients, energy_gaps, metric_blocks, metric_index, coulomb_blocks, coulomb_index
):
    metric, metric_offsets = prepare(metric_blocks, metric_index)
    coulomb, coulomb_offsets = prepare(coulomb_blocks, coulomb_index)
    first = apply_operator(metric, metric_offsets, coefficients)
    second = apply_operator(coulomb, coulomb_offsets, first)
    pieces = apply_operator(metric, metric_offsets, second)
    pair_weight = 4.0 * energy_gaps / (energy_gaps * energy_gaps + frequency_sq)
    weighted = (pieces[:QC].astype(jnp.float32) * pair_weight[None, :]).astype(jnp.bfloat16)
    tiles = lax.psum_scatter(
        lax.dot_general(
            pieces, weighted, (((1,), (1,)), ((), ())), preferred_element_type=jnp.float32
        ),
        "grp",
        scatter_dimension=0,
        tiled=True,
    )
    return tiles[None]


def solution(mesh):
    placed = (
        P("sec", "grp"),
        P("grp"),
        P("sec", None, None, None),
        P("sec", None),
        P("sec", None, None, None),
        P("sec", None),
    )
    return jax.shard_map(
        on_device, mesh=mesh, in_specs=placed, out_specs=P("sec", "grp", None), check_vma=False
    )
```

profile of v0, /device:TPU:64, one launch (start us, length us, event | category | flops | bytes accessed | tf_op | source)
XLA Modules:
  0.0 300.8 jit_solution(5648532059439215960)
XLA Ops:
  6.5 1.1 fusion.27
  7.6 0.1 collective-permute-start
  7.7 2.6 collective-permute-start.1
  10.3 0.7 broadcast_compare_fusion.1
  11.0 0.1 copy.11
  11.1 0.7 compare_select_fusion
  11.8 0.1 copy.13
  11.9 0.1 reshape.41
  12.1 2.9 collective-permute-done
  15.0 2.0 collective-permute-done.1
  17.0 7.3 %pad_maximum_fusion = bf16[10240,128]{1,0:T(8,128)(2,1)S(1)} fusion(bf16[1024,128]{1,0:T(8,128)(2,1)S(1)} %collective-permute-done.1, bf16[8192,128]{1,0:T(8,128)(2,1)} %param.6, bf16[1024,128]{1,0:T(8,128)(2,1)S(1)} %collective-permute-done), kind=kLoop, calls=%fused_computation.12 | loop fusion | flops 7864320 | bytes 5242880 | tf_op jit(solution)/shard_map/concatenate | solution.py:17
  24.3 3.0 %gather_fusion = bf16[128,128,128]{2,1,0:T(8,128)(2,1)} fusion(bf16[80,128,128]{2,1,0:T(8,128)(2,1)S(1)} %bitcast.31, s32[1024]{0:T(1024)S(1)} %pad_clamp_fusion.1), kind=kCustom, calls=%fused_computation | custom fusion | bytes 8389120 | tf_op jit(solution)/shard_map/gather | solution.py:52
  27.3 4.8 %bitcast_convert_fusion.2 = bf16[64,128,128]{2,1,0:T(8,128)(2,1)S(1)} fusion(bf16[64,2,128,128]{3,2,1,0:T(8,128)(2,1)} %bitcast.34, bf16[64,2,128,128]{3,2,1,0:T(8,128)(2,1)} %param.8, pred[64,2]{1,0:T(8,128)(4,1)S(1)} %copy.11), kind=kOutput, calls=%fused_computation.5 | convolution fusion | flops 540016640 | bytes 10485888 | tf_op jit(solution)/shard_map/rkab,rkbc->rac/dot_general | solution.py:53
  32.2 2.9 collective-permute-start.3
  35.1 3.4 %collective-permute-start.2 = (bf16[1024,128]{1,0:T(8,128)(2,1)S(1)}, bf16[1024,128]{1,0:T(8,128)(2,1)S(1)}, u32[]{:S(2)}, u32[]{:S(2)}) collective-permute-start(bf16[1024,128]{1,0:T(8,128)(2,1)S(1)} %bitcast.39), channel_id=1, source_target_pairs={{0,1},{1,2},{2,3},{3,4},{4,5},{5,6},{6,7},{7,0},{8,9},{9,10},{10,1... | collective-permute-start | bytes 786440 | tf_op jit(solution)/shard_map/ppermute | solution.py:19
  38.5 0.1 copy.12
  38.6 0.1 copy.14
  38.7 0.1 reshape.49
  38.9 1.8 collective-permute-done.3
  40.7 4.0 %collective-permute-done.2 = bf16[1024,128]{1,0:T(8,128)(2,1)S(1)} collective-permute-done((bf16[1024,128]{1,0:T(8,128)(2,1)S(1)}, bf16[1024,128]{1,0:T(8,128)(2,1)S(1)}, u32[]{:S(2)}, u32[]{:S(2)}) %collective-permute-start.2) | collective-permute-done | bytes 262176 | tf_op jit(solution)/shard_map/ppermute | solution.py:19
  44.7 7.3 %pad_maximum_fusion.1 = bf16[10240,128]{1,0:T(8,128)(2,1)S(1)} fusion(bf16[1024,128]{1,0:T(8,128)(2,1)S(1)} %collective-permute-done.3, bf16[8192,128]{1,0:T(8,128)(2,1)} %bitcast.36, bf16[1024,128]{1,0:T(8,128)(2,1)S(1)} %collective-permute-done.2), kind=kLoop, calls=%fused_computation.13 | loop fusion | flops 7864320 | bytes 5242880 | tf_op jit(solution)/shard_map/concatenate | solution.py:17
  51.9 3.0 %gather_fusion.1 = bf16[128,128,128]{2,1,0:T(8,128)(2,1)} fusion(bf16[80,128,128]{2,1,0:T(8,128)(2,1)S(1)} %bitcast.29, s32[1024]{0:T(1024)S(1)} %pad_clamp_fusion), kind=kCustom, calls=%fused_computation.1 | custom fusion | bytes 8389120 | tf_op jit(solution)/shard_map/gather | solution.py:52
  55.0 4.8 %bitcast_convert_fusion.1 = bf16[64,128,128]{2,1,0:T(8,128)(2,1)S(1)} fusion(bf16[64,2,128,128]{3,2,1,0:T(8,128)(2,1)} %bitcast.32, bf16[64,2,128,128]{3,2,1,0:T(8,128)(2,1)} %param.10, pred[64,2]{1,0:T(8,128)(4,1)S(1)} %copy.12), kind=kOutput, calls=%fused_computation.4 | convolution fusion | flops 540016640 | bytes 10485888 | tf_op jit(solution)/shard_map/rkab,rkbc->rac/dot_general | solution.py:53
  59.8 0.1 collective-permute-start.5
  59.9 2.1 collective-permute-start.4
  62.0 2.7 collective-permute-done.5
  64.7 2.2 collective-permute-done.4
  66.9 7.7 %pad_maximum_fusion.2 = bf16[10240,128]{1,0:T(8,128)(2,1)S(1)} fusion(bf16[1024,128]{1,0:T(8,128)(2,1)S(1)} %collective-permute-done.5, bf16[8192,128]{1,0:T(8,128)(2,1)S(1)} %bitcast.37, bf16[1024,128]{1,0:T(8,128)(2,1)S(1)} %collective-permute-done.4), kind=kLoop, calls=%fused_computation.14 | loop fusion | flops 7864320 | bytes 5242880 | tf_op jit(solution)/shard_map/concatenate | solution.py:17
  74.6 3.0 %gather_fusion.2 = bf16[128,128,128]{2,1,0:T(8,128)(2,1)} fusion(bf16[80,128,128]{2,1,0:T(8,128)(2,1)S(1)} %bitcast.30, s32[1024]{0:T(1024)S(1)} %pad_clamp_fusion.1), kind=kCustom, calls=%fused_computation.2 | custom fusion | bytes 8389120 | tf_op jit(solution)/shard_map/gather | solution.py:52
  77.6 4.8 %bitcast_convert_fusion = bf16[64,128,128]{2,1,0:T(8,128)(2,1)S(1)} fusion(bf16[64,2,128,128]{3,2,1,0:T(8,128)(2,1)} %bitcast.33, bf16[64,2,128,128]{3,2,1,0:T(8,128)(2,1)} %param.8, pred[64,2]{1,0:T(8,128)(4,1)S(1)} %copy.11), kind=kOutput, calls=%fused_computation.3 | convolution fusion | flops 540016640 | bytes 10485888 | tf_op jit(solution)/shard_map/rkab,rkbc->rac/dot_general | solution.py:53
  82.4 4.5 %fusion.11 = f32[8192,256]{1,0:T(8,128)} fusion(bf16[8192,128]{1,0:T(8,128)(2,1)S(1)} %bitcast.35, bf16[256,128]{1,0:T(8,128)(2,1)S(1)} %bitcast.38, f32[128]{0:T(128)S(1)} %add_divide_fusion), kind=kOutput, calls=%fused_computation.20 | convolution fusion | flops 536969216 | bytes 10551808 | tf_op jit(solution)/shard_map/dot_general | solution.py:68
  86.9 207.1 %reduce-scatter.2.cloned.1.call-done = f32[256,256]{1,0:T(8,128)} async-done(((f32[8192,256]{1,0:T(8,128)}), f32[256,256]{1,0:T(8,128)}) %reduce-scatter.2.cloned.1.call-update) | async-done | bytes 262160 | tf_op jit(solution)/shard_map/reduce_scatter | solution.py:67
  (16 shorter events, 0.1 us)
Async XLA Ops:
  6.5 287.4 %reduce-scatter.2.cloned.1.call-start = ((), (), s32[]{:S(2)}) async-start(), calls=%async_computation.1 | async-start | bytes 8650752 | tf_op jit(solution)/shard_map/reduce_scatter | solution.py:67
  7.6 7.4 %collective-permute-start = (bf16[1024,128]{1,0:T(8,128)(2,1)S(1)}, bf16[1024,128]{1,0:T(8,128)(2,1)S(1)}, u32[]{:S(2)}, u32[]{:S(2)}) collective-permute-start(bf16[1024,128]{1,0:T(8,128)(2,1)S(1)} %get-tuple-element.9), channel_id=1, source_target_pairs={{0,1},{1,2},{2,3},{3,4},{4,5},{5,6},{6,7},{7,0},{8,9},{9,10},{10,1... | collective-permute-start | bytes 786440 | tf_op jit(solution)/shard_map/ppermute | solution.py:19
  7.7 9.3 %collective-permute-start.1 = (bf16[1024,128]{1,0:T(8,128)(2,1)S(1)}, bf16[1024,128]{1,0:T(8,128)(2,1)S(1)}, u32[]{:S(2)}, u32[]{:S(2)}) collective-permute-start(bf16[1024,128]{1,0:T(8,128)(2,1)S(1)} %get-tuple-element.10), channel_id=1, source_target_pairs={{1,0},{2,1},{3,2},{4,3},{5,4},{6,5},{7,6},{0,7},{9,8},{10,9},{11,1... | collective-permute-start | bytes 786440 | tf_op jit(solution)/shard_map/ppermute | solution.py:21
  27.3 11.2 %copy-start.1 = (s32[64,2]{0,1:T(2,128)S(1)}, s32[64,2]{0,1:T(2,128)}, u32[]{:S(2)}) copy-start(s32[64,2]{0,1:T(2,128)} %param.11) | copy-start | bytes 1540
  32.1 12.5 %copy-start = (bf16[64,128,128]{2,1,0:T(8,128)(2,1)}, bf16[64,128,128]{2,1,0:T(8,128)(2,1)S(1)}, u32[]{:S(2)}) copy-start(bf16[64,128,128]{2,1,0:T(8,128)(2,1)S(1)} %bitcast_convert_fusion.2) | copy-start | bytes 6291460
  32.2 8.5 %collective-permute-start.3 = (bf16[1024,128]{1,0:T(8,128)(2,1)S(1)}, bf16[1024,128]{1,0:T(8,128)(2,1)S(1)}, u32[]{:S(2)}, u32[]{:S(2)}) collective-permute-start(bf16[1024,128]{1,0:T(8,128)(2,1)S(1)} %bitcast.40), channel_id=1, source_target_pairs={{1,0},{2,1},{3,2},{4,3},{5,4},{6,5},{7,6},{0,7},{9,8},{10,9},{11,1... | collective-permute-start | bytes 786440 | tf_op jit(solution)/shard_map/ppermute | solution.py:21
  35.1 9.6 %collective-permute-start.2 = (bf16[1024,128]{1,0:T(8,128)(2,1)S(1)}, bf16[1024,128]{1,0:T(8,128)(2,1)S(1)}, u32[]{:S(2)}, u32[]{:S(2)}) collective-permute-start(bf16[1024,128]{1,0:T(8,128)(2,1)S(1)} %bitcast.39), channel_id=1, source_target_pairs={{0,1},{1,2},{2,3},{3,4},{4,5},{5,6},{6,7},{7,0},{8,9},{9,10},{10,1... | collective-permute-start | bytes 786440 | tf_op jit(solution)/shard_map/ppermute | solution.py:19
  55.0 7.0 %copy-start.2 = (f32[128]{0:T(128)S(1)}, f32[128]{0:T(128)}, u32[]{:S(2)}) copy-start(f32[128]{0:T(128)} %param.7) | copy-start | bytes 1540
  59.8 4.9 %collective-permute-start.5 = (bf16[1024,128]{1,0:T(8,128)(2,1)S(1)}, bf16[1024,128]{1,0:T(8,128)(2,1)S(1)}, u32[]{:S(2)}, u32[]{:S(2)}) collective-permute-start(bf16[1024,128]{1,0:T(8,128)(2,1)S(1)} %bitcast.42), channel_id=1, source_target_pairs={{1,0},{2,1},{3,2},{4,3},{5,4},{6,5},{7,6},{0,7},{9,8},{10,9},{11,1... | collective-permute-start | bytes 786440 | tf_op jit(solution)/shard_map/ppermute | solution.py:21
  59.9 7.0 %collective-permute-start.4 = (bf16[1024,128]{1,0:T(8,128)(2,1)S(1)}, bf16[1024,128]{1,0:T(8,128)(2,1)S(1)}, u32[]{:S(2)}, u32[]{:S(2)}) collective-permute-start(bf16[1024,128]{1,0:T(8,128)(2,1)S(1)} %bitcast.41), channel_id=1, source_target_pairs={{0,1},{1,2},{2,3},{3,4},{4,5},{5,6},{6,7},{7,0},{8,9},{9,10},{10,1... | collective-permute-start | bytes 786440 | tf_op jit(solution)/shard_map/ppermute | solution.py:19
Sparse Core Ops, SparseCore 0:
  87.0 206.8 reduce-scatter.1
where the time goes:
time: 301 us
  waiting for transfers between devices  223 us (74%)
  other arithmetic  23.6 us (8%)
  matrix products  18.8 us (6%)
  between operations  13.5 us (4%)
  starting transfers between devices  11.2 us (4%)
  local copies, waits for them, and re-layouts  11 us (4%)
    reduce_scatter x1, waiting for transfers between devices, on_device(): lax.psum_scatter(lax.dot_general(pieces, weighted, (((1,), (1,)), ((), ()...  207 us
    concatenate x3, other arithmetic, with_halo(): jnp.concatenate([lax.ppermute(tail, axis, [(i, (i + 1) % count) for i in...  22.2 us
    dot_general x3, matrix products, apply_operator(): jnp.einsum('rkab,rkbc->rac', kept, chosen, preferred_element_type=jnp.flo...  14.3 us
    ppermute x3, waiting for transfers between devices, with_halo(): lax.ppermute(tail, axis, [(i, (i + 1) % count) for i in range(count)])  9.1 us
    gather x3, local copies, waits for them, and re-layouts, apply_operator(): chosen = stacked[offsets]  9.1 us
    ppermute x3, waiting for transfers between devices, with_halo(): lax.ppermute(head, axis, [((i + 1) % count, i) for i in range(count)])  6.5 us
  transfers between devices with their start and end apart: 7, of which 7 were waited for; matrix products, arithmetic and copies ran while one was open for 1% of the time, Pallas kernels for 0%

commit v1 on v0

v1 whole, which is shorter than its diff:
```python
import functools

import jax
import jax.numpy as jnp
from jax import lax
from jax.experimental import pallas as pl
from jax.experimental.pallas import tpu as pltpu
from jax.sharding import PartitionSpec as P

BS = 128
ROWS = 64
REACH = 8
NBLK = 512
QC = 256
NX, NY, NZ = 4, 4, 2

frequency_sq = 1.0

VMEM = pl.BlockSpec(memory_space=pltpu.VMEM)
SMEM = pl.BlockSpec(memory_space=pltpu.SMEM)
ANY = pl.BlockSpec(memory_space=pl.ANY)
BF = jnp.bfloat16
F32 = jnp.float32


def blocks_of(count):
    return jax.ShapeDtypeStruct((count, BS, BS), BF)


def params(mib):
    return pltpu.CompilerParams(vmem_limit_bytes=mib * 2**20)


def cost(row_ops, nbytes):
    return pl.CostEstimate(
        flops=row_ops * 4 * BS**3, bytes_accessed=nbytes, transcendentals=0
    )


def coords():
    grp = lax.axis_index("grp")
    return grp // (NY * NZ), (grp // NZ) % NY, grp % NZ


def neighbour(index_ref, row):
    named = index_ref[1, row]
    distance = named - (lax.axis_index("sec") * ROWS + row)
    distance = jnp.where(distance >= NBLK // 2, distance - NBLK, distance)
    distance = jnp.where(distance < -(NBLK // 2), distance + NBLK, distance)
    live = named >= 0
    return jnp.where(live, row + distance, row), live


def row_product(x, field_ref, base, row, index_ref):
    other, live = neighbour(index_ref, row)
    own = field_ref[row - base]
    far = jnp.where(live, field_ref[other - base], jnp.zeros((BS, BS), BF))
    return jnp.dot(
        jnp.concatenate([x[0], x[1]], axis=1),
        jnp.concatenate([own, far], axis=0),
        preferred_element_type=F32,
    ).astype(BF)


def rows_loop(first, count, body):
    def step(k, carry):
        body(first + k)
        return carry

    lax.fori_loop(0, count, step, 0, unroll=4)


def layer_start(layer, y):
    low, high = 8 * (4 - layer), 64 - 8 * (4 - layer) - 8
    if layer % 2 == 0:
        return jnp.where(y < 2, low + 4 * y, high + 4 * (y - 2))
    return jnp.where(y < 2, high + 4 * y, low + 4 * (y - 2))


def layer_rows(layer, outs, body):
    _, y, _ = coords()
    for step in range(NY):
        start = layer_start(layer, (y + step) % NY)
        for k in range(4):
            outs[step][k] = body(start + k)


def inner_kernel(s_index, v_index, c_hbm, s_hbm, v_hbm, first, second, b0, b1, b2, b3, c, s, v, sems):
    copies = [
        pltpu.make_async_copy(c_hbm, c, sems.at[0]),
        pltpu.make_async_copy(s_hbm.at[pl.ds(8, 48)], s, sems.at[1]),
        pltpu.make_async_copy(v_hbm.at[pl.ds(16, 32)], v, sems.at[2]),
    ]
    for copy in copies:
        copy.start()
    copies[0].wait()
    copies[1].wait()

    def one(row):
        first[row - 8] = row_product(s[row - 8], c, 0, row, s_index)

    rows_loop(8, 48, one)
    copies[2].wait()

    def two(row):
        second[row - 16] = row_product(v[row - 16], first, 8, row, v_index)

    rows_loop(16, 32, two)
    layer_rows(1, (b0, b1, b2, b3), lambda row: row_product(s[row - 8], second, 16, row, s_index))


def inner(s_index, v_index, c, s, v):
    return pl.pallas_call(
        inner_kernel,
        out_shape=[blocks_of(48), blocks_of(32)] + [blocks_of(4)] * 4,
        in_specs=[SMEM, SMEM, ANY, ANY, ANY],
        out_specs=[VMEM] * 6,
        scratch_shapes=[
            pltpu.VMEM((64, BS, BS), BF),
            pltpu.VMEM((48, 2, BS, BS), BF),
            pltpu.VMEM((32, 2, BS, BS), BF),
            pltpu.SemaphoreType.DMA((3,)),
        ],
        compiler_params=params(24),
        cost_estimate=cost(96, 14 * 2**20),
    )(s_index, v_index, c, s, v)


def edge_rows(index, low_halo, low, high, high_halo, x_low, x_high, ext, emit):
    ext[0:8] = low_halo[...]
    ext[8:24] = low[...]
    for k in range(8):
        emit(0, k, row_product(x_low[k], ext, -8, k, index))
    ext[0:16] = high[...]
    ext[16:24] = high_halo[...]
    for k in range(8):
        emit(1, k, row_product(x_high[k], ext, 48, 56 + k, index))


def edge_specs(low_block, high_block, low_at, high_at):
    return [
        SMEM,
        VMEM,
        VMEM,
        pl.BlockSpec((low_block, BS, BS), lambda i: (low_at, 0, 0)),
        pl.BlockSpec((high_block, BS, BS), lambda i: (high_at, 0, 0)),
        pl.BlockSpec((8, 2, BS, BS), lambda i: (0, 0, 0, 0)),
        pl.BlockSpec((8, 2, BS, BS), lambda i: (7, 0, 0, 0)),
    ]


def first_edges_kernel(index, low_halo, high_halo, low, high, x_low, x_high, head, tail, ext):
    def emit(side, k, value):
        (head, tail)[side][k] = value

    edge_rows(index, low_halo, low, high, high_halo, x_low, x_high, ext, emit)


def first_edges(index, low_halo, high_halo, field, x):
    return pl.pallas_call(
        first_edges_kernel,
        grid=(1,),
        out_shape=[blocks_of(8)] * 2,
        in_specs=edge_specs(16, 16, 0, 3),
        out_specs=[VMEM] * 2,
        scratch_shapes=[pltpu.VMEM((24, BS, BS), BF)],
        compiler_params=params(16),
        cost_estimate=cost(16, 4 * 2**20),
    )(index, low_halo, high_halo, field, field, x, x)


def middle_kernel(
    s_index, v_index, head, tail, first, second, v_low, v_high, s_low, s_high,
    low_out, high_out, b0, b1, b2, b3, f_low, f_high, e,
):
    f_low[0:8] = head[...]
    f_low[8:24] = first[0:16]
    f_high[0:16] = first[32:48]
    f_high[16:24] = tail[...]
    for k in range(8):
        low_out[k] = row_product(v_low[k], f_low, 0, 8 + k, v_index)
        high_out[k] = row_product(v_high[k], f_high, 40, 48 + k, v_index)
    e[0:8] = low_out[...]
    e[8:40] = second[...]
    e[40:48] = high_out[...]

    def body(row):
        x = jnp.where(row < 32, s_low[row % 8], s_high[row % 8])
        return row_product(x, e, 8, row, s_index)

    layer_rows(2, (b0, b1, b2, b3), body)


def middle(s_index, v_index, head, tail, first, second, v, s):
    def rows_at(at):
        return pl.BlockSpec((8, 2, BS, BS), lambda i: (at, 0, 0, 0))

    return pl.pallas_call(
        middle_kernel,
        grid=(1,),
        out_shape=[blocks_of(8)] * 2 + [blocks_of(4)] * 4,
        in_specs=[SMEM, SMEM] + [VMEM] * 4 + [rows_at(1), rows_at(6), rows_at(2), rows_at(5)],
        out_specs=[VMEM] * 6,
        scratch_shapes=[
            pltpu.VMEM((24, BS, BS), BF),
            pltpu.VMEM((24, BS, BS), BF),
            pltpu.VMEM((48, BS, BS), BF),
        ],
        compiler_params=params(24),
        cost_estimate=cost(32, 8 * 2**20),
    )(s_index, v_index, head, tail, first, second, v, v, s, s)


def second_edges_kernel(
    index, low_halo, high_halo, head, tail, first_low, first_high, x_low, x_high,
    out_head, out_tail, ext,
):
    ext[0:8] = low_halo[...]
    ext[8:16] = head[...]
    ext[16:24] = first_low[...]
    for k in range(8):
        out_head[k] = row_product(x_low[k], ext, -8, k, index)
    ext[0:8] = first_high[...]
    ext[8:16] = tail[...]
    ext[16:24] = high_halo[...]
    for k in range(8):
        out_tail[k] = row_product(x_high[k], ext, 48, 56 + k, index)


def second_edges(index, low_halo, high_halo, head, tail, first, x):
    return pl.pallas_call(
        second_edges_kernel,
        grid=(1,),
        out_shape=[blocks_of(8)] * 2,
        in_specs=[SMEM] + [VMEM] * 4 + edge_specs(8, 8, 0, 5)[3:],
        out_specs=[VMEM] * 2,
        scratch_shapes=[pltpu.VMEM((24, BS, BS), BF)],
        compiler_params=params(16),
        cost_estimate=cost(16, 4 * 2**20),
    )(index, low_halo, high_halo, head, tail, first, first, x, x)


def outer_kernel(index, head, tail, low, high, second, s_low, s_high, b0, b1, b2, b3, e):
    e[0:8] = head[...]
    e[8:16] = low[...]
    e[16:24] = second[0:8]
    e[24:32] = second[24:32]
    e[32:40] = high[...]
    e[40:48] = tail[...]

    def body(row):
        x = jnp.where(row < 32, s_low[row % 8], s_high[row % 8])
        return row_product(x, e, jnp.where(row < 32, 0, 16), row, index)

    layer_rows(3, (b0, b1, b2, b3), body)


def outer(index, head, tail, low, high, second, s):
    def rows_at(at):
        return pl.BlockSpec((8, 2, BS, BS), lambda i: (at, 0, 0, 0))

    return pl.pallas_call(
        outer_kernel,
        grid=(1,),
        out_shape=[blocks_of(4)] * 4,
        in_specs=[SMEM] + [VMEM] * 5 + [rows_at(1), rows_at(6)],
        out_specs=[VMEM] * 4,
        scratch_shapes=[pltpu.VMEM((48, BS, BS), BF)],
        compiler_params=params(16),
        cost_estimate=cost(16, 4 * 2**20),
    )(index, head, tail, low, high, second, s, s)


def last_kernel(
    index, low_halo, high_halo, head, tail, low, high, s_low, s_high, gaps,
    b0, b1, b2, b3, weighted, e,
):
    e[0:8] = low_halo[...]
    e[8:16] = head[...]
    e[16:24] = low[...]
    e[24:32] = high[...]
    e[32:40] = tail[...]
    e[40:48] = high_halo[...]
    gap = gaps[...]
    weight = 4.0 * gap / (gap * gap + frequency_sq)
    for k in range(2):
        value = row_product(s_low[k], e, -8, k, index)
        weighted[k] = (value.astype(F32) * weight).astype(BF)

    def body(row):
        x = jnp.where(row < 32, s_low[row % 8], s_high[row % 8])
        return row_product(x, e, jnp.where(row < 32, -8, 24), row, index)

    layer_rows(4, (b0, b1, b2, b3), body)


def last(index, low_halo, high_halo, head, tail, low, high, s, gaps):
    def rows_at(at):
        return pl.BlockSpec((8, 2, BS, BS), lambda i: (at, 0, 0, 0))

    return pl.pallas_call(
        last_kernel,
        grid=(1,),
        out_shape=[blocks_of(4)] * 4 + [blocks_of(2)],
        in_specs=[SMEM] + [VMEM] * 6 + [rows_at(0), rows_at(7), VMEM],
        out_specs=[VMEM] * 5,
        scratch_shapes=[pltpu.VMEM((48, BS, BS), BF)],
        compiler_params=params(16),
        cost_estimate=cost(18, 4 * 2**20),
    )(index, low_halo, high_halo, head, tail, low, high, s, s, gaps)


def product_kernel(*refs):
    pieces, w_refs = refs[:16], refs[16:20]
    own, outs, b, w = refs[20], refs[21:28], refs[28], refs[29]
    for layer in range(4):
        for source in range(4):
            b[layer, :, source * BS : (source + 1) * BS] = pieces[layer * 4 + source][...].reshape(4 * BS, BS)
    for source in range(4):
        w[:, source * BS : (source + 1) * BS] = w_refs[source][...].reshape(QC, BS)
    x, y, z = coords()
    for step in range(NX):
        to = (x + step) % NX
        near = jnp.where(to == 2, 0, jnp.where(to == 1, 1, jnp.where(to == 3, 2, 3)))
        away = jnp.where(to == 1, 0, jnp.where(to == 2, 1, jnp.where(to == 0, 2, 3)))
        layer = jnp.where(y < 2, near, away)
        for flip in range(NZ):
            half = (z + flip) % NZ
            tile = lax.dot_general(
                b[layer, pl.ds(pl.multiple_of(half * QC, QC), QC), :],
                w[...],
                (((1,), (1,)), ((), ())),
                preferred_element_type=F32,
            )
            if step == 0 and flip == 0:
                own[...] = tile
            else:
                outs[step * NZ + flip - 1][...] = tile.astype(BF)


def product(pieces, weights):
    tile = jax.ShapeDtypeStruct((QC, QC), BF)
    return pl.pallas_call(
        product_kernel,
        out_shape=[jax.ShapeDtypeStruct((QC, QC), F32)] + [tile] * 7,
        in_specs=[VMEM] * 20,
        out_specs=[VMEM] * 8,
        scratch_shapes=[pltpu.VMEM((4, 4 * BS, 4 * BS), BF), pltpu.VMEM((QC, 4 * BS), BF)],
        compiler_params=params(24),
        cost_estimate=pl.CostEstimate(
            flops=2 * 2048 * 512 * 256, bytes_accessed=8 * 2**20, transcendentals=0
        ),
    )(*pieces, *weights)


def add_kernel(*refs):
    total = refs[0][...]
    for ref in refs[1:8]:
        total += ref[...].astype(F32)
    refs[8][0] = total


def add_up(own, others):
    return pl.pallas_call(
        add_kernel,
        out_shape=jax.ShapeDtypeStruct((1, QC, QC), F32),
        in_specs=[VMEM] * 8,
        out_specs=VMEM,
        compiler_params=params(8),
        cost_estimate=pl.CostEstimate(flops=8 * QC * QC, bytes_accessed=2**20, transcendentals=0),
    )(own, *others)


def grp_shift(value, dx, dy, dz):
    pairs = []
    for x in range(NX):
        for y in range(NY):
            for z in range(NZ):
                to = ((x + dx) % NX * NY + (y + dy) % NY) * NZ + (z + dz) % NZ
                pairs.append(((x * NY + y) * NZ + z, to))
    return lax.ppermute(value, "grp", pairs)


def halo(head, tail):
    count = lax.axis_size("sec")
    up = [(i, (i + 1) % count) for i in range(count)]
    down = [((i + 1) % count, i) for i in range(count)]
    return lax.ppermute(tail, "sec", up), lax.ppermute(head, "sec", down)


def spread_y(parts):
    return [parts[0]] + [grp_shift(parts[d], 0, d, 0) for d in (1, 2, 3)]


def on_device(coefficients, energy_gaps, metric_blocks, metric_index, coulomb_blocks, coulomb_index):
    c = coefficients.reshape(ROWS, BS, BS)
    s, v = metric_blocks, coulomb_blocks
    s_index, v_index = metric_index.T, coulomb_index.T
    gaps = energy_gaps.reshape(1, BS)

    c_low, c_high = halo(c[:8], c[56:])
    first, second, *layer1 = inner(s_index, v_index, c, s, v)
    layer1 = spread_y(layer1)
    f_head, f_tail = first_edges(s_index, c_low, c_high, c, s)
    f_low, f_high = halo(f_head, f_tail)
    e_low, e_high, *layer2 = middle(s_index, v_index, f_head, f_tail, first, second, v, s)
    layer2 = spread_y(layer2)
    e_head, e_tail = second_edges(v_index, f_low, f_high, f_head, f_tail, first, v)
    g_low, g_high = halo(e_head, e_tail)
    layer3 = outer(s_index, e_head, e_tail, e_low, e_high, second, s)
    layer3 = spread_y(layer3)
    *layer4, weighted = last(s_index, g_low, g_high, e_head, e_tail, e_low, e_high, s, gaps)
    weights = spread_y([weighted] * 4)
    layer4 = spread_y(layer4)
    own, *others = product([*layer1, *layer2, *layer3, *layer4], weights)
    sent = [
        grp_shift(others[step * NZ + flip - 1], step, 0, flip)
        for step in range(NX)
        for flip in range(NZ)
        if step or flip
    ]
    return add_up(own, sent)


def solution(mesh):
    placed = (
        P("sec", "grp"),
        P("grp"),
        P("sec", None, None, None),
        P("sec", None),
        P("sec", None, None, None),
        P("sec", None),
    )
    return jax.shard_map(
        on_device, mesh=mesh, in_specs=placed, out_specs=P("sec", "grp", None), check_vma=False
    )
```

time: 301 us -> 88.5 us (0.29)
  waiting for transfers between devices: 223 us -> 17.1 us
  starting transfers between devices: 11.2 us -> 50.1 us
  other arithmetic: 23.6 us -> 0 us
  matrix products: 18.8 us -> 0 us
  Pallas kernels: 0 us -> 14.4 us
  between operations: 13.5 us -> 0.15 us
  local copies, waits for them, and re-layouts: 11 us -> 5.54 us
    reduce_scatter x1 -> x0, waiting for transfers between devices: 207 us -> none  [on_device(): lax.psum_scatter(lax.dot_general(pieces, weighted, (((1,), (1,)), ((), ()...]
    ppermute x6 -> x28, starting transfers between devices: 11.2 us -> 50.1 us  [the longest x22 37.6 us: grp_shift(): return lax.ppermute(value, 'grp', pairs)]
    concatenate x3 -> x0, other arithmetic: 22.2 us -> none  [with_halo(): jnp.concatenate([lax.ppermute(tail, axis, [(i, (i + 1) % count) for i in...]
    dot_general x4 -> x0, matrix products: 18.8 us -> none  [the longest x3 14.3 us: apply_operator(): jnp.einsum('rkab,rkbc->rac', kept, chosen, preferred_element_type=jnp.flo...]
    pallas_call x0 -> x8, Pallas kernels: none -> 14.4 us  [the longest x1 6.23 us: inner(): pl.pallas_call(inner_kernel, out_shape=[blocks_of(48), blocks_of(32)] + [...]
    gather x3 -> x0, local copies, waits for them, and re-layouts: 9.1 us -> none  [apply_operator(): chosen = stacked[offsets]]
    unnamed x6 -> x18, local copies, waits for them, and re-layouts: 0.01 us -> 4.48 us
    ppermute x6 -> x28, waiting for transfers between devices: 15.6 us -> 17.1 us  [the longest x22 10.4 us: grp_shift(): return lax.ppermute(value, 'grp', pairs)]
  transfers between devices with their start and end apart: 7 -> 28, of which waited for: 7 -> 10; matrix products, arithmetic and copies ran while one was open for 1% -> 0% of each run, Pallas kernels for 0% -> 13%
where the time goes in v1:
time: 88.5 us; the launch traced here: 87.3 us
  starting transfers between devices  50.1 us (57%)
  waiting for transfers between devices  17.1 us (19%)
  Pallas kernels  14.4 us (16%)
  local copies, waits for them, and re-layouts  5.54 us (6%)
    ppermute x22, starting transfers between devices, grp_shift(): return lax.ppermute(value, 'grp', pairs)  37.6 us
    ppermute x6, starting transfers between devices, halo(): return (lax.ppermute(tail, 'sec', up), lax.ppermute(head, 'sec', down))  12.5 us
    ppermute x22, waiting for transfers between devices, grp_shift(): return lax.ppermute(value, 'grp', pairs)  10.4 us
    ppermute x6, waiting for transfers between devices, halo(): return (lax.ppermute(tail, 'sec', up), lax.ppermute(head, 'sec', down))  6.71 us
    pallas_call x1, Pallas kernels, inner(): pl.pallas_call(inner_kernel, out_shape=[blocks_of(48), blocks_of(32)] + [...  6.23 us
    unnamed x18, local copies, waits for them, and re-layouts  4.48 us
  transfers between devices with their start and end apart: 28, of which 10 were waited for; matrix products, arithmetic and copies ran while one was open for 0% of the time, Pallas kernels for 13%

profile of v1, /device:TPU:64, one launch (start us, length us, event | category | flops | bytes accessed | tf_op | source)
XLA Modules:
  0.0 87.3 jit_solution(1414758590127732485)
XLA Ops:
  1.2 2.6 %collective-permute-start.4 = (bf16[8,128,128]{2,1,0:T(8,128)(2,1)S(1)}, bf16[8,128,128]{2,1,0:T(8,128)(2,1)S(1)}, u32[]{:S(2)}, u32[]{:S(2)}) collective-permute-start(bf16[8,128,128]{2,1,0:T(8,128)(2,1)S(1)} %bitcast.18), channel_id=1, source_target_pairs={{1,0},{2,1},{3,2},{4,3},{5,4},{6,5},{7,6},{0,7},{9,8},{10,9},{11,1... | collective-permute-start | bytes 786440 | tf_op jit(solution)/shard_map/ppermute | solution.py:388
  3.8 4.7 %collective-permute-done.3.low_halo = bf16[8,128,128]{2,1,0:T(8,128)(2,1)S(1)} collective-permute-done((bf16[8,128,128]{2,1,0:T(8,128)(2,1)S(1)}, bf16[8,128,128]{2,1,0:T(8,128)(2,1)S(1)}, u32[]{:S(2)}, u32[]{:S(2)}) %collective-permute-start.3) | collective-permute-done | bytes 262176 | tf_op jit(solution)/shard_map/ppermute | solution.py:388
  8.5 2.0 %collective-permute-done.4.high_halo = bf16[8,128,128]{2,1,0:T(8,128)(2,1)S(1)} collective-permute-done((bf16[8,128,128]{2,1,0:T(8,128)(2,1)S(1)}, bf16[8,128,128]{2,1,0:T(8,128)(2,1)S(1)}, u32[]{:S(2)}, u32[]{:S(2)}) %collective-permute-start.4) | collective-permute-done | bytes 262176 | tf_op jit(solution)/shard_map/ppermute | solution.py:388
  10.5 2.2 %copy-done = bf16[64,2,128,128]{3,2,1,0:T(8,128)(2,1)S(1)} copy-done((bf16[64,2,128,128]{3,2,1,0:T(8,128)(2,1)S(1)}, bf16[64,2,128,128]{3,2,1,0:T(8,128)(2,1)}, u32[]{:S(2)}) %copy-start) | copy-done | bytes 4194328
  12.7 1.6 %copy-done.3 = bf16[8192,128]{1,0:T(8,128)(2,1)S(1)} copy-done((bf16[8192,128]{1,0:T(8,128)(2,1)S(1)}, bf16[8192,128]{1,0:T(8,128)(2,1)}, u32[]{:S(2)}) %copy-start.3) | copy-done | bytes 2097176
  16.1 2.9 %collective-permute-start.9 = (bf16[8,128,128]{2,1,0:T(8,128)(2,1)S(1)}, bf16[8,128,128]{2,1,0:T(8,128)(2,1)S(1)}, u32[]{:S(2)}, u32[]{:S(2)}) collective-permute-start(bf16[8,128,128]{2,1,0:T(8,128)(2,1)S(1)} %get-tuple-element.42.head), channel_id=1, source_target_pairs={{1,0},{2,1},{3,2},{4,3},{5,4},{6,5},{7,6},{0,7},{9,8},{10,9},{11,1... | collective-permute-start | bytes 786440 | tf_op jit(solution)/shard_map/ppermute | solution.py:388
  19.0 3.2 %collective-permute-start.8 = (bf16[8,128,128]{2,1,0:T(8,128)(2,1)S(1)}, bf16[8,128,128]{2,1,0:T(8,128)(2,1)S(1)}, u32[]{:S(2)}, u32[]{:S(2)}) collective-permute-start(bf16[8,128,128]{2,1,0:T(8,128)(2,1)S(1)} %get-tuple-element.43.tail), channel_id=1, source_target_pairs={{0,1},{1,2},{2,3},{3,4},{4,5},{5,6},{6,7},{7,0},{8,9},{9,10},{10,1... | collective-permute-start | bytes 786440 | tf_op jit(solution)/shard_map/ppermute | solution.py:388
  22.2 6.2 %shard_map.64 = (bf16[48,128,128]{2,1,0:T(8,128)(2,1)S(1)}, bf16[32,128,128]{2,1,0:T(8,128)(2,1)S(1)}, bf16[4,128,128]{2,1,0:T(8,128)(2,1)S(1)}, bf16[4,128,128]...) custom-call(s32[2,64]{1,0:T(2,128)S(1)} %bitcast.10, s32[2,64]{1,0:T(2,128)S(1)} %bitcast.14, ...), custom_call_target="tpu_custom_call" | custom-call | flops 805306368 | bytes 14680064 | tf_op jit(solution)/shard_map/pallas_call | solution.py:113
  28.5 1.6 %collective-permute-start = (bf16[4,128,128]{2,1,0:T(8,128)(2,1)S(1)}, bf16[4,128,128]{2,1,0:T(8,128)(2,1)S(1)}, u32[]{:S(2)}, u32[]{:S(2)}) collective-permute-start(bf16[4,128,128]{2,1,0:T(8,128)(2,1)S(1)} %get-tuple-element.39), channel_id=1, source_target_pairs={{0,16},{8,24},{16,32},{24,40},{32,48},{40,56},{48,0},{56,8},{64,80... | collective-permute-start | bytes 393224 | tf_op jit(solution)/shard_map/ppermute | solution.py:381
  31.3 3.6 %collective-permute-start.13 = (bf16[8,128,128]{2,1,0:T(8,128)(2,1)S(1)}, bf16[8,128,128]{2,1,0:T(8,128)(2,1)S(1)}, u32[]{:S(2)}, u32[]{:S(2)}) collective-permute-start(bf16[8,128,128]{2,1,0:T(8,128)(2,1)S(1)} %get-tuple-element.51.tail), channel_id=1, source_target_pairs={{0,1},{1,2},{2,3},{3,4},{4,5},{5,6},{6,7},{7,0},{8,9},{9,10},{10,1... | collective-permute-start | bytes 786440 | tf_op jit(solution)/shard_map/ppermute | solution.py:388
  34.9 2.9 %collective-permute-start.1 = (bf16[4,128,128]{2,1,0:T(8,128)(2,1)S(1)}, bf16[4,128,128]{2,1,0:T(8,128)(2,1)S(1)}, u32[]{:S(2)}, u32[]{:S(2)}) collective-permute-start(bf16[4,128,128]{2,1,0:T(8,128)(2,1)S(1)} %get-tuple-element.40), channel_id=1, source_target_pairs={{0,32},{8,40},{16,48},{24,56},{32,0},{40,8},{48,16},{56,24},{64,96... | collective-permute-start | bytes 393224 | tf_op jit(solution)/shard_map/ppermute | solution.py:381
  37.8 1.3 %collective-permute-start.2 = (bf16[4,128,128]{2,1,0:T(8,128)(2,1)S(1)}, bf16[4,128,128]{2,1,0:T(8,128)(2,1)S(1)}, u32[]{:S(2)}, u32[]{:S(2)}) collective-permute-start(bf16[4,128,128]{2,1,0:T(8,128)(2,1)S(1)} %get-tuple-element.41), channel_id=1, source_target_pairs={{0,48},{8,56},{16,0},{24,8},{32,16},{40,24},{48,32},{56,40},{64,11... | collective-permute-start | bytes 393224 | tf_op jit(solution)/shard_map/ppermute | solution.py:381
  39.1 1.7 %shard_map.66 = (bf16[8,128,128]{2,1,0:T(8,128)(2,1)S(1)}, bf16[8,128,128]{2,1,0:T(8,128)(2,1)S(1)}, bf16[4,128,128]{2,1,0:T(8,128)(2,1)S(1)}, bf16[4,128,128]{2...) custom-call(s32[2,64]{1,0:T(2,128)S(1)} %bitcast.11, s32[2,64]{1,0:T(2,128)S(1)} %bitcast.16, ...), custom_call_target="tpu_custom_call" | custom-call | flops 268435456 | bytes 8388608 | tf_op jit(solution)/shard_map/pallas_call | solution.py:198
  41.6 1.1 %shard_map.68 = (bf16[4,128,128]{2,1,0:T(8,128)(2,1)S(1)}, bf16[4,128,128]{2,1,0:T(8,128)(2,1)S(1)}, bf16[4,128,128]{2,1,0:T(8,128)(2,1)S(1)}, bf16[4,128,128]{2,1,0:T(8,128)(2,1)S(1)}) custom-call(s32[2,64]{1,0:T(2,128)S(1)} %bitcast.12, bf16[8,128,128]{2,1,0:T(8,128)(2,1)S(1)} %get-tuple-element.50.head, bf16[8,128,128]{2,1,0:T(8,128)(2,1)S(1)} %get-tuple-element.51.tail, ...), custom_call_target="tpu_custom_call" | custom-call | flops 134217728 | bytes 4194304 | tf_op jit(solution)/shard_map/pallas_call | solution.py:262
  42.8 1.5 %collective-permute-start.6 = (bf16[4,128,128]{2,1,0:T(8,128)(2,1)S(1)}, bf16[4,128,128]{2,1,0:T(8,128)(2,1)S(1)}, u32[]{:S(2)}, u32[]{:S(2)}) collective-permute-start(bf16[4,128,128]{2,1,0:T(8,128)(2,1)S(1)} %get-tuple-element.48), channel_id=1, source_target_pairs={{0,32},{8,40},{16,48},{24,56},{32,0},{40,8},{48,16},{56,24},{64,96... | collective-permute-start | bytes 393224 | tf_op jit(solution)/shard_map/ppermute | solution.py:381
  44.2 1.9 %collective-permute-start.7 = (bf16[4,128,128]{2,1,0:T(8,128)(2,1)S(1)}, bf16[4,128,128]{2,1,0:T(8,128)(2,1)S(1)}, u32[]{:S(2)}, u32[]{:S(2)}) collective-permute-start(bf16[4,128,128]{2,1,0:T(8,128)(2,1)S(1)} %get-tuple-element.49), channel_id=1, source_target_pairs={{0,48},{8,56},{16,0},{24,8},{32,16},{40,24},{48,32},{56,40},{64,11... | collective-permute-start | bytes 393224 | tf_op jit(solution)/shard_map/ppermute | solution.py:381
  47.1 1.3 %collective-permute-start.11 = (bf16[4,128,128]{2,1,0:T(8,128)(2,1)S(1)}, bf16[4,128,128]{2,1,0:T(8,128)(2,1)S(1)}, u32[]{:S(2)}, u32[]{:S(2)}) collective-permute-start(bf16[4,128,128]{2,1,0:T(8,128)(2,1)S(1)} %get-tuple-element.56), channel_id=1, source_target_pairs={{0,32},{8,40},{16,48},{24,56},{32,0},{40,8},{48,16},{56,24},{64,96... | collective-permute-start | bytes 393224 | tf_op jit(solution)/shard_map/ppermute | solution.py:381
  48.5 2.5 %collective-permute-start.12 = (bf16[4,128,128]{2,1,0:T(8,128)(2,1)S(1)}, bf16[4,128,128]{2,1,0:T(8,128)(2,1)S(1)}, u32[]{:S(2)}, u32[]{:S(2)}) collective-permute-start(bf16[4,128,128]{2,1,0:T(8,128)(2,1)S(1)} %get-tuple-element.57), channel_id=1, source_target_pairs={{0,48},{8,56},{16,0},{24,8},{32,16},{40,24},{48,32},{56,40},{64,11... | collective-permute-start | bytes 393224 | tf_op jit(solution)/shard_map/ppermute | solution.py:381
  51.0 1.2 %shard_map.69 = (bf16[4,128,128]{2,1,0:T(8,128)(2,1)S(1)}, bf16[4,128,128]{2,1,0:T(8,128)(2,1)S(1)}, bf16[4,128,128]{2,1,0:T(8,128)(2,1)S(1)}, bf16[4,128,128]{2,1,0:T(8,128)(2,1)S(1)}, bf16[2,128,128]{2,1,0:T(8,128)(2,1)S(1)}) custom-call(s32[2,64]{1,0:T(2,128)S(1)} %bitcast.13, bf16[8,128,128]{2,1,0:T(8,128)(2,1)S(1)} %collective-permute-done.13.low_halo, ...), custom_call_target="tpu_custom_call" | custom-call | flops 150994944 | bytes 4194304 | tf_op jit(solution)/shard_map/pallas_call | solution.py:301
  52.5 1.8 %collective-permute-start.15 = (bf16[4,128,128]{2,1,0:T(8,128)(2,1)S(1)}, bf16[4,128,128]{2,1,0:T(8,128)(2,1)S(1)}, u32[]{:S(2)}, u32[]{:S(2)}) collective-permute-start(bf16[4,128,128]{2,1,0:T(8,128)(2,1)S(1)} %get-tuple-element.59), channel_id=1, source_target_pairs={{0,16},{8,24},{16,32},{24,40},{32,48},{40,56},{48,0},{56,8},{64,80... | collective-permute-start | bytes 393224 | tf_op jit(solution)/shard_map/ppermute | solution.py:381
  55.1 1.9 %collective-permute-start.16 = (bf16[4,128,128]{2,1,0:T(8,128)(2,1)S(1)}, bf16[4,128,128]{2,1,0:T(8,128)(2,1)S(1)}, u32[]{:S(2)}, u32[]{:S(2)}) collective-permute-start(bf16[4,128,128]{2,1,0:T(8,128)(2,1)S(1)} %get-tuple-element.60), channel_id=1, source_target_pairs={{0,32},{8,40},{16,48},{24,56},{32,0},{40,8},{48,16},{56,24},{64,96... | collective-permute-start | bytes 393224 | tf_op jit(solution)/shard_map/ppermute | solution.py:381
  57.6 1.1 %collective-permute-start.19 = (bf16[2,128,128]{2,1,0:T(8,128)(2,1)S(1)}, bf16[2,128,128]{2,1,0:T(8,128)(2,1)S(1)}, u32[]{:S(2)}, u32[]{:S(2)}) collective-permute-start(bf16[2,128,128]{2,1,0:T(8,128)(2,1)S(1)} %get-tuple-element.62.refs_16_), channel_id=1, source_target_pairs={{0,32},{8,40},{16,48},{24,56},{32,0},{40,8},{48,16},{56,24},{64,96... | collective-permute-start | bytes 196616 | tf_op jit(solution)/shard_map/ppermute | solution.py:381
  59.4 1.7 %collective-permute-start.18 = (bf16[2,128,128]{2,1,0:T(8,128)(2,1)S(1)}, bf16[2,128,128]{2,1,0:T(8,128)(2,1)S(1)}, u32[]{:S(2)}, u32[]{:S(2)}) collective-permute-start(bf16[2,128,128]{2,1,0:T(8,128)(2,1)S(1)} %get-tuple-element.62.refs_16_), channel_id=1, source_target_pairs={{0,16},{8,24},{16,32},{24,40},{32,48},{40,56},{48,0},{56,8},{64,80... | collective-permute-start | bytes 196616 | tf_op jit(solution)/shard_map/ppermute | solution.py:381
  61.1 2.9 %collective-permute-done.19.refs_18_ = bf16[2,128,128]{2,1,0:T(8,128)(2,1)S(1)} collective-permute-done((bf16[2,128,128]{2,1,0:T(8,128)(2,1)S(1)}, bf16[2,128,128]{2,1,0:T(8,128)(2,1)S(1)}, u32[]{:S(2)}, u32[]{:S(2)}) %collective-permute-start.19) | collective-permute-done | bytes 65568 | tf_op jit(solution)/shard_map/ppermute | solution.py:381
  64.1 2.5 %collective-permute-done.18.refs_17_ = bf16[2,128,128]{2,1,0:T(8,128)(2,1)S(1)} collective-permute-done((bf16[2,128,128]{2,1,0:T(8,128)(2,1)S(1)}, bf16[2,128,128]{2,1,0:T(8,128)(2,1)S(1)}, u32[]{:S(2)}, u32[]{:S(2)}) %collective-permute-start.18) | collective-permute-done | bytes 65568 | tf_op jit(solution)/shard_map/ppermute | solution.py:381
  68.1 1.5 %collective-permute-start.22 = (bf16[256,256]{1,0:T(8,128)(2,1)S(1)}, bf16[256,256]{1,0:T(8,128)(2,1)S(1)}, u32[]{:S(2)}, u32[]{:S(2)}) collective-permute-start(bf16[256,256]{1,0:T(8,128)(2,1)S(1)} %get-tuple-element.65), channel_id=1, source_target_pairs={{0,64},{8,72},{16,80},{24,88},{32,96},{40,104},{48,112},{56,120},{... | collective-permute-start | bytes 393224 | tf_op jit(solution)/shard_map/ppermute | solution.py:381
  69.6 2.6 %collective-permute-start.23 = (bf16[256,256]{1,0:T(8,128)(2,1)S(1)}, bf16[256,256]{1,0:T(8,128)(2,1)S(1)}, u32[]{:S(2)}, u32[]{:S(2)}) collective-permute-start(bf16[256,256]{1,0:T(8,128)(2,1)S(1)} %get-tuple-element.66), channel_id=1, source_target_pairs={{0,72},{8,64},{16,88},{24,80},{32,104},{40,96},{48,120},{56,112},{... | collective-permute-start | bytes 393224 | tf_op jit(solution)/shard_map/ppermute | solution.py:381
  72.2 1.7 %collective-permute-start.24 = (bf16[256,256]{1,0:T(8,128)(2,1)S(1)}, bf16[256,256]{1,0:T(8,128)(2,1)S(1)}, u32[]{:S(2)}, u32[]{:S(2)}) collective-permute-start(bf16[256,256]{1,0:T(8,128)(2,1)S(1)} %get-tuple-element.67), channel_id=1, source_target_pairs={{0,128},{8,136},{16,144},{24,152},{32,160},{40,168},{48,176},{56,1... | collective-permute-start | bytes 393224 | tf_op jit(solution)/shard_map/ppermute | solution.py:381
  73.9 1.6 %collective-permute-start.25 = (bf16[256,256]{1,0:T(8,128)(2,1)S(1)}, bf16[256,256]{1,0:T(8,128)(2,1)S(1)}, u32[]{:S(2)}, u32[]{:S(2)}) collective-permute-start(bf16[256,256]{1,0:T(8,128)(2,1)S(1)} %get-tuple-element.68), channel_id=1, source_target_pairs={{0,136},{8,128},{16,152},{24,144},{32,168},{40,160},{48,184},{56,1... | collective-permute-start | bytes 393224 | tf_op jit(solution)/shard_map/ppermute | solution.py:381
  75.5 1.7 %collective-permute-start.26 = (bf16[256,256]{1,0:T(8,128)(2,1)S(1)}, bf16[256,256]{1,0:T(8,128)(2,1)S(1)}, u32[]{:S(2)}, u32[]{:S(2)}) collective-permute-start(bf16[256,256]{1,0:T(8,128)(2,1)S(1)} %get-tuple-element.69), channel_id=1, source_target_pairs={{0,192},{8,200},{16,208},{24,216},{32,224},{40,232},{48,240},{56,2... | collective-permute-start | bytes 393224 | tf_op jit(solution)/shard_map/ppermute | solution.py:381
  77.3 6.7 %collective-permute-start.27 = (bf16[256,256]{1,0:T(8,128)(2,1)S(1)}, bf16[256,256]{1,0:T(8,128)(2,1)S(1)}, u32[]{:S(2)}, u32[]{:S(2)}) collective-permute-start(bf16[256,256]{1,0:T(8,128)(2,1)S(1)} %get-tuple-element.70), channel_id=1, source_target_pairs={{0,200},{8,192},{16,216},{24,208},{32,232},{40,224},{48,248},{56,2... | collective-permute-start | bytes 393224 | tf_op jit(solution)/shard_map/ppermute | solution.py:381
  85.0 1.4 %collective-permute-done.26.refs_6_ = bf16[256,256]{1,0:T(8,128)(2,1)S(1)} collective-permute-done((bf16[256,256]{1,0:T(8,128)(2,1)S(1)}, bf16[256,256]{1,0:T(8,128)(2,1)S(1)}, u32[]{:S(2)}, u32[]{:S(2)}) %collective-permute-start.26) | collective-permute-done | bytes 131104 | tf_op jit(solution)/shard_map/ppermute | solution.py:381
  (51 shorter events, 11.7 us)
Async XLA Ops:
  1.1 7.4 %collective-permute-start.3 = (bf16[8,128,128]{2,1,0:T(8,128)(2,1)S(1)}, bf16[8,128,128]{2,1,0:T(8,128)(2,1)S(1)}, u32[]{:S(2)}, u32[]{:S(2)}) collective-permute-start(bf16[8,128,128]{2,1,0:T(8,128)(2,1)S(1)} %bitcast.19), channel_id=1, source_target_pairs={{0,1},{1,2},{2,3},{3,4},{4,5},{5,6},{6,7},{7,0},{8,9},{9,10},{10,1... | collective-permute-start | bytes 786440 | tf_op jit(solution)/shard_map/ppermute | solution.py:388
  1.2 9.3 %collective-permute-start.4 = (bf16[8,128,128]{2,1,0:T(8,128)(2,1)S(1)}, bf16[8,128,128]{2,1,0:T(8,128)(2,1)S(1)}, u32[]{:S(2)}, u32[]{:S(2)}) collective-permute-start(bf16[8,128,128]{2,1,0:T(8,128)(2,1)S(1)} %bitcast.18), channel_id=1, source_target_pairs={{1,0},{2,1},{3,2},{4,3},{5,4},{6,5},{7,6},{0,7},{9,8},{10,9},{11,1... | collective-permute-start | bytes 786440 | tf_op jit(solution)/shard_map/ppermute | solution.py:388
  15.0 7.3 %copy-start.4 = (bf16[8192,128]{1,0:T(8,128)(2,1)S(1)}, bf16[8192,128]{1,0:T(8,128)(2,1)}, u32[]{:S(2)}) copy-start(bf16[8192,128]{1,0:T(8,128)(2,1)} %param.6) | copy-start | bytes 6291460
  15.0 7.3 %copy-start.6 = (s32[64,2]{0,1:T(2,128)S(1)}, s32[64,2]{0,1:T(2,128)}, u32[]{:S(2)}) copy-start(s32[64,2]{0,1:T(2,128)} %param.9) | copy-start | bytes 1540
  15.0 7.3 %copy-start.7 = (s32[64,2]{0,1:T(2,128)S(1)}, s32[64,2]{0,1:T(2,128)}, u32[]{:S(2)}) copy-start(s32[64,2]{0,1:T(2,128)} %param.11) | copy-start | bytes 1540
  16.1 14.0 %collective-permute-start.9 = (bf16[8,128,128]{2,1,0:T(8,128)(2,1)S(1)}, bf16[8,128,128]{2,1,0:T(8,128)(2,1)S(1)}, u32[]{:S(2)}, u32[]{:S(2)}) collective-permute-start(bf16[8,128,128]{2,1,0:T(8,128)(2,1)S(1)} %get-tuple-element.42.head), channel_id=1, source_target_pairs={{1,0},{2,1},{3,2},{4,3},{5,4},{6,5},{7,6},{0,7},{9,8},{10,9},{11,1... | collective-permute-start | bytes 786440 | tf_op jit(solution)/shard_map/ppermute | solution.py:388
  19.0 11.1 %collective-permute-start.8 = (bf16[8,128,128]{2,1,0:T(8,128)(2,1)S(1)}, bf16[8,128,128]{2,1,0:T(8,128)(2,1)S(1)}, u32[]{:S(2)}, u32[]{:S(2)}) collective-permute-start(bf16[8,128,128]{2,1,0:T(8,128)(2,1)S(1)} %get-tuple-element.43.tail), channel_id=1, source_target_pairs={{0,1},{1,2},{2,3},{3,4},{4,5},{5,6},{6,7},{7,0},{8,9},{9,10},{10,1... | collective-permute-start | bytes 786440 | tf_op jit(solution)/shard_map/ppermute | solution.py:388
  28.5 12.4 %collective-permute-start = (bf16[4,128,128]{2,1,0:T(8,128)(2,1)S(1)}, bf16[4,128,128]{2,1,0:T(8,128)(2,1)S(1)}, u32[]{:S(2)}, u32[]{:S(2)}) collective-permute-start(bf16[4,128,128]{2,1,0:T(8,128)(2,1)S(1)} %get-tuple-element.39), channel_id=1, source_target_pairs={{0,16},{8,24},{16,32},{24,40},{32,48},{40,56},{48,0},{56,8},{64,80... | collective-permute-start | bytes 393224 | tf_op jit(solution)/shard_map/ppermute | solution.py:381
  31.2 15.9 %collective-permute-start.14 = (bf16[8,128,128]{2,1,0:T(8,128)(2,1)S(1)}, bf16[8,128,128]{2,1,0:T(8,128)(2,1)S(1)}, u32[]{:S(2)}, u32[]{:S(2)}) collective-permute-start(bf16[8,128,128]{2,1,0:T(8,128)(2,1)S(1)} %get-tuple-element.50.head), channel_id=1, source_target_pairs={{1,0},{2,1},{3,2},{4,3},{5,4},{6,5},{7,6},{0,7},{9,8},{10,9},{11,1... | collective-permute-start | bytes 786440 | tf_op jit(solution)/shard_map/ppermute | solution.py:388
  31.3 17.2 %collective-permute-start.13 = (bf16[8,128,128]{2,1,0:T(8,128)(2,1)S(1)}, bf16[8,128,128]{2,1,0:T(8,128)(2,1)S(1)}, u32[]{:S(2)}, u32[]{:S(2)}) collective-permute-start(bf16[8,128,128]{2,1,0:T(8,128)(2,1)S(1)} %get-tuple-element.51.tail), channel_id=1, source_target_pairs={{0,1},{1,2},{2,3},{3,4},{4,5},{5,6},{6,7},{7,0},{8,9},{9,10},{10,1... | collective-permute-start | bytes 786440 | tf_op jit(solution)/shard_map/ppermute | solution.py:388
  34.9 7.9 %collective-permute-start.1 = (bf16[4,128,128]{2,1,0:T(8,128)(2,1)S(1)}, bf16[4,128,128]{2,1,0:T(8,128)(2,1)S(1)}, u32[]{:S(2)}, u32[]{:S(2)}) collective-permute-start(bf16[4,128,128]{2,1,0:T(8,128)(2,1)S(1)} %get-tuple-element.40), channel_id=1, source_target_pairs={{0,32},{8,40},{16,48},{24,56},{32,0},{40,8},{48,16},{56,24},{64,96... | collective-permute-start | bytes 393224 | tf_op jit(solution)/shard_map/ppermute | solution.py:381
  37.8 6.5 %collective-permute-start.2 = (bf16[4,128,128]{2,1,0:T(8,128)(2,1)S(1)}, bf16[4,128,128]{2,1,0:T(8,128)(2,1)S(1)}, u32[]{:S(2)}, u32[]{:S(2)}) collective-permute-start(bf16[4,128,128]{2,1,0:T(8,128)(2,1)S(1)} %get-tuple-element.41), channel_id=1, source_target_pairs={{0,48},{8,56},{16,0},{24,8},{32,16},{40,24},{48,32},{56,40},{64,11... | collective-permute-start | bytes 393224 | tf_op jit(solution)/shard_map/ppermute | solution.py:381
  40.9 6.3 %collective-permute-start.5 = (bf16[4,128,128]{2,1,0:T(8,128)(2,1)S(1)}, bf16[4,128,128]{2,1,0:T(8,128)(2,1)S(1)}, u32[]{:S(2)}, u32[]{:S(2)}) collective-permute-start(bf16[4,128,128]{2,1,0:T(8,128)(2,1)S(1)} %get-tuple-element.47), channel_id=1, source_target_pairs={{0,16},{8,24},{16,32},{24,40},{32,48},{40,56},{48,0},{56,8},{64,80... | collective-permute-start | bytes 393224 | tf_op jit(solution)/shard_map/ppermute | solution.py:381
  41.6 9.4 %copy-start.8 = (f32[128]{0:T(128)S(1)}, f32[128]{0:T(128)}, u32[]{:S(2)}) copy-start(f32[128]{0:T(128)} %param.7) | copy-start | bytes 1540
  42.8 9.4 %collective-permute-start.6 = (bf16[4,128,128]{2,1,0:T(8,128)(2,1)S(1)}, bf16[4,128,128]{2,1,0:T(8,128)(2,1)S(1)}, u32[]{:S(2)}, u32[]{:S(2)}) collective-permute-start(bf16[4,128,128]{2,1,0:T(8,128)(2,1)S(1)} %get-tuple-element.48), channel_id=1, source_target_pairs={{0,32},{8,40},{16,48},{24,56},{32,0},{40,8},{48,16},{56,24},{64,96... | collective-permute-start | bytes 393224 | tf_op jit(solution)/shard_map/ppermute | solution.py:381
  44.2 8.3 %collective-permute-start.7 = (bf16[4,128,128]{2,1,0:T(8,128)(2,1)S(1)}, bf16[4,128,128]{2,1,0:T(8,128)(2,1)S(1)}, u32[]{:S(2)}, u32[]{:S(2)}) collective-permute-start(bf16[4,128,128]{2,1,0:T(8,128)(2,1)S(1)} %get-tuple-element.49), channel_id=1, source_target_pairs={{0,48},{8,56},{16,0},{24,8},{32,16},{40,24},{48,32},{56,40},{64,11... | collective-permute-start | bytes 393224 | tf_op jit(solution)/shard_map/ppermute | solution.py:381
  47.1 7.9 %collective-permute-start.10 = (bf16[4,128,128]{2,1,0:T(8,128)(2,1)S(1)}, bf16[4,128,128]{2,1,0:T(8,128)(2,1)S(1)}, u32[]{:S(2)}, u32[]{:S(2)}) collective-permute-start(bf16[4,128,128]{2,1,0:T(8,128)(2,1)S(1)} %get-tuple-element.55), channel_id=1, source_target_pairs={{0,16},{8,24},{16,32},{24,40},{32,48},{40,56},{48,0},{56,8},{64,80... | collective-permute-start | bytes 393224 | tf_op jit(solution)/shard_map/ppermute | solution.py:381
  47.1 9.8 %collective-permute-start.11 = (bf16[4,128,128]{2,1,0:T(8,128)(2,1)S(1)}, bf16[4,128,128]{2,1,0:T(8,128)(2,1)S(1)}, u32[]{:S(2)}, u32[]{:S(2)}) collective-permute-start(bf16[4,128,128]{2,1,0:T(8,128)(2,1)S(1)} %get-tuple-element.56), channel_id=1, source_target_pairs={{0,32},{8,40},{16,48},{24,56},{32,0},{40,8},{48,16},{56,24},{64,96... | collective-permute-start | bytes 393224 | tf_op jit(solution)/shard_map/ppermute | solution.py:381
  48.5 9.1 %collective-permute-start.12 = (bf16[4,128,128]{2,1,0:T(8,128)(2,1)S(1)}, bf16[4,128,128]{2,1,0:T(8,128)(2,1)S(1)}, u32[]{:S(2)}, u32[]{:S(2)}) collective-permute-start(bf16[4,128,128]{2,1,0:T(8,128)(2,1)S(1)} %get-tuple-element.57), channel_id=1, source_target_pairs={{0,48},{8,56},{16,0},{24,8},{32,16},{40,24},{48,32},{56,40},{64,11... | collective-permute-start | bytes 393224 | tf_op jit(solution)/shard_map/ppermute | solution.py:381
  52.2 7.2 %collective-permute-start.20 = (bf16[2,128,128]{2,1,0:T(8,128)(2,1)S(1)}, bf16[2,128,128]{2,1,0:T(8,128)(2,1)S(1)}, u32[]{:S(2)}, u32[]{:S(2)}) collective-permute-start(bf16[2,128,128]{2,1,0:T(8,128)(2,1)S(1)} %get-tuple-element.62.refs_16_), channel_id=1, source_target_pairs={{0,48},{8,56},{16,0},{24,8},{32,16},{40,24},{48,32},{56,40},{64,11... | collective-permute-start | bytes 196616 | tf_op jit(solution)/shard_map/ppermute | solution.py:381
  52.5 14.0 %collective-permute-start.15 = (bf16[4,128,128]{2,1,0:T(8,128)(2,1)S(1)}, bf16[4,128,128]{2,1,0:T(8,128)(2,1)S(1)}, u32[]{:S(2)}, u32[]{:S(2)}) collective-permute-start(bf16[4,128,128]{2,1,0:T(8,128)(2,1)S(1)} %get-tuple-element.59), channel_id=1, source_target_pairs={{0,16},{8,24},{16,32},{24,40},{32,48},{40,56},{48,0},{56,8},{64,80... | collective-permute-start | bytes 393224 | tf_op jit(solution)/shard_map/ppermute | solution.py:381
  55.1 11.5 %collective-permute-start.16 = (bf16[4,128,128]{2,1,0:T(8,128)(2,1)S(1)}, bf16[4,128,128]{2,1,0:T(8,128)(2,1)S(1)}, u32[]{:S(2)}, u32[]{:S(2)}) collective-permute-start(bf16[4,128,128]{2,1,0:T(8,128)(2,1)S(1)} %get-tuple-element.60), channel_id=1, source_target_pairs={{0,32},{8,40},{16,48},{24,56},{32,0},{40,8},{48,16},{56,24},{64,96... | collective-permute-start | bytes 393224 | tf_op jit(solution)/shard_map/ppermute | solution.py:381
  57.0 9.6 %collective-permute-start.17 = (bf16[4,128,128]{2,1,0:T(8,128)(2,1)S(1)}, bf16[4,128,128]{2,1,0:T(8,128)(2,1)S(1)}, u32[]{:S(2)}, u32[]{:S(2)}) collective-permute-start(bf16[4,128,128]{2,1,0:T(8,128)(2,1)S(1)} %get-tuple-element.61), channel_id=1, source_target_pairs={{0,48},{8,56},{16,0},{24,8},{32,16},{40,24},{48,32},{56,40},{64,11... | collective-permute-start | bytes 393224 | tf_op jit(solution)/shard_map/ppermute | solution.py:381
  57.6 6.5 %collective-permute-start.19 = (bf16[2,128,128]{2,1,0:T(8,128)(2,1)S(1)}, bf16[2,128,128]{2,1,0:T(8,128)(2,1)S(1)}, u32[]{:S(2)}, u32[]{:S(2)}) collective-permute-start(bf16[2,128,128]{2,1,0:T(8,128)(2,1)S(1)} %get-tuple-element.62.refs_16_), channel_id=1, source_target_pairs={{0,32},{8,40},{16,48},{24,56},{32,0},{40,8},{48,16},{56,24},{64,96... | collective-permute-start | bytes 196616 | tf_op jit(solution)/shard_map/ppermute | solution.py:381
  59.4 7.1 %collective-permute-start.18 = (bf16[2,128,128]{2,1,0:T(8,128)(2,1)S(1)}, bf16[2,128,128]{2,1,0:T(8,128)(2,1)S(1)}, u32[]{:S(2)}, u32[]{:S(2)}) collective-permute-start(bf16[2,128,128]{2,1,0:T(8,128)(2,1)S(1)} %get-tuple-element.62.refs_16_), channel_id=1, source_target_pairs={{0,16},{8,24},{16,32},{24,40},{32,48},{40,56},{48,0},{56,8},{64,80... | collective-permute-start | bytes 196616 | tf_op jit(solution)/shard_map/ppermute | solution.py:381
  67.7 7.8 %collective-permute-start.21 = (bf16[256,256]{1,0:T(8,128)(2,1)S(1)}, bf16[256,256]{1,0:T(8,128)(2,1)S(1)}, u32[]{:S(2)}, u32[]{:S(2)}) collective-permute-start(bf16[256,256]{1,0:T(8,128)(2,1)S(1)} %get-tuple-element.64), channel_id=1, source_target_pairs={{0,8},{8,0},{16,24},{24,16},{32,40},{40,32},{48,56},{56,48},{64,72... | collective-permute-start | bytes 393224 | tf_op jit(solution)/shard_map/ppermute | solution.py:381
  68.1 9.2 %collective-permute-start.22 = (bf16[256,256]{1,0:T(8,128)(2,1)S(1)}, bf16[256,256]{1,0:T(8,128)(2,1)S(1)}, u32[]{:S(2)}, u32[]{:S(2)}) collective-permute-start(bf16[256,256]{1,0:T(8,128)(2,1)S(1)} %get-tuple-element.65), channel_id=1, source_target_pairs={{0,64},{8,72},{16,80},{24,88},{32,96},{40,104},{48,112},{56,120},{... | collective-permute-start | bytes 393224 | tf_op jit(solution)/shard_map/ppermute | solution.py:381
  69.6 14.4 %collective-permute-start.23 = (bf16[256,256]{1,0:T(8,128)(2,1)S(1)}, bf16[256,256]{1,0:T(8,128)(2,1)S(1)}, u32[]{:S(2)}, u32[]{:S(2)}) collective-permute-start(bf16[256,256]{1,0:T(8,128)(2,1)S(1)} %get-tuple-element.66), channel_id=1, source_target_pairs={{0,72},{8,64},{16,88},{24,80},{32,104},{40,96},{48,120},{56,112},{... | collective-permute-start | bytes 393224 | tf_op jit(solution)/shard_map/ppermute | solution.py:381
  72.2 12.7 %collective-permute-start.24 = (bf16[256,256]{1,0:T(8,128)(2,1)S(1)}, bf16[256,256]{1,0:T(8,128)(2,1)S(1)}, u32[]{:S(2)}, u32[]{:S(2)}) collective-permute-start(bf16[256,256]{1,0:T(8,128)(2,1)S(1)} %get-tuple-element.67), channel_id=1, source_target_pairs={{0,128},{8,136},{16,144},{24,152},{32,160},{40,168},{48,176},{56,1... | collective-permute-start | bytes 393224 | tf_op jit(solution)/shard_map/ppermute | solution.py:381
  73.9 11.0 %collective-permute-start.25 = (bf16[256,256]{1,0:T(8,128)(2,1)S(1)}, bf16[256,256]{1,0:T(8,128)(2,1)S(1)}, u32[]{:S(2)}, u32[]{:S(2)}) collective-permute-start(bf16[256,256]{1,0:T(8,128)(2,1)S(1)} %get-tuple-element.68), channel_id=1, source_target_pairs={{0,136},{8,128},{16,152},{24,144},{32,168},{40,160},{48,184},{56,1... | collective-permute-start | bytes 393224 | tf_op jit(solution)/shard_map/ppermute | solution.py:381
  75.5 10.9 %collective-permute-start.26 = (bf16[256,256]{1,0:T(8,128)(2,1)S(1)}, bf16[256,256]{1,0:T(8,128)(2,1)S(1)}, u32[]{:S(2)}, u32[]{:S(2)}) collective-permute-start(bf16[256,256]{1,0:T(8,128)(2,1)S(1)} %get-tuple-element.69), channel_id=1, source_target_pairs={{0,192},{8,200},{16,208},{24,216},{32,224},{40,232},{48,240},{56,2... | collective-permute-start | bytes 393224 | tf_op jit(solution)/shard_map/ppermute | solution.py:381
  77.3 9.2 %collective-permute-start.27 = (bf16[256,256]{1,0:T(8,128)(2,1)S(1)}, bf16[256,256]{1,0:T(8,128)(2,1)S(1)}, u32[]{:S(2)}, u32[]{:S(2)}) collective-permute-start(bf16[256,256]{1,0:T(8,128)(2,1)S(1)} %get-tuple-element.70), channel_id=1, source_target_pairs={{0,200},{8,192},{16,216},{24,208},{32,232},{40,224},{48,248},{56,2... | collective-permute-start | bytes 393224 | tf_op jit(solution)/shard_map/ppermute | solution.py:381
  (5 other events, 19.0 us)

commit v2 on v1

v2 whole, which is shorter than its diff:
```python
import jax
import jax.numpy as jnp
from jax import lax
from jax.experimental import pallas as pl
from jax.experimental.pallas import tpu as pltpu
from jax.sharding import PartitionSpec as P

BS = 128
ROWS = 64
REACH = 8
NBLK = 512
QC = 256
NX, NY, NZ = 4, 4, 2

frequency_sq = 1.0

VMEM = pl.BlockSpec(memory_space=pltpu.VMEM)
SMEM = pl.BlockSpec(memory_space=pltpu.SMEM)
HBM = pl.BlockSpec(memory_space=pltpu.HBM)
BF = jnp.bfloat16
F32 = jnp.float32


def blocks_of(count):
    return jax.ShapeDtypeStruct((count, BS, BS), BF)


def params(mib):
    return pltpu.CompilerParams(vmem_limit_bytes=mib * 2**20)


def cost(row_ops, nbytes):
    return pl.CostEstimate(
        flops=row_ops * 4 * BS**3, bytes_accessed=nbytes, transcendentals=0
    )


def coords():
    grp = lax.axis_index("grp")
    return grp // (NY * NZ), (grp // NZ) % NY, grp % NZ


def positions(index, first_row):
    rows = lax.broadcasted_iota(jnp.int32, (ROWS,), 0)
    distance = index[:, 1] - (first_row + rows)
    distance = jnp.where(distance >= NBLK // 2, distance - NBLK, distance)
    distance = jnp.where(distance < -(NBLK // 2), distance + NBLK, distance)
    return jnp.where(index[:, 1] >= 0, rows + distance, -NBLK)


def neighbour(index_ref, row):
    other = index_ref[row]
    live = other > -NBLK
    return jnp.where(live, other, row), live


def row_product(x, field_ref, base, row, index_ref):
    other, live = neighbour(index_ref, row)
    own = field_ref[row - base]
    far = jnp.where(live, field_ref[other - base], jnp.zeros((BS, BS), BF))
    return jnp.dot(
        jnp.concatenate([x[0], x[1]], axis=1),
        jnp.concatenate([own, far], axis=0),
        preferred_element_type=F32,
    ).astype(BF)


def rows_loop(first, count, body):
    def step(k, carry):
        body(first + k)
        return carry

    lax.fori_loop(0, count, step, 0, unroll=16)


def layer_start(layer, y):
    low, high = 8 * (4 - layer), 64 - 8 * (4 - layer) - 8
    if layer % 2 == 0:
        return jnp.where(y < 2, low + 4 * y, high + 4 * (y - 2))
    return jnp.where(y < 2, high + 4 * y, low + 4 * (y - 2))


def stored_slot(layer, start):
    low = 8 * (4 - layer)
    return jnp.where(start < 32, start - low, start + low - 48)


def inner_kernel(
    s_index, v_index, c_hbm, s_hbm, v_hbm,
    first, second, layer1, c_edge, s_edge, v_edge, v_mid, s_mid, s_out,
    c, s, v, sems,
):
    def load(k, source, target, at, to, count):
        return pltpu.make_async_copy(source.at[pl.ds(at, count)], target.at[pl.ds(to, count)], sems.at[k])

    copies = [
        load(0, c_hbm, c, 0, 0, 64),
        load(1, s_hbm, s, 8, 0, 16),
        load(2, s_hbm, s, 24, 16, 16),
        load(3, s_hbm, s, 40, 32, 16),
        load(4, v_hbm, v, 16, 0, 32),
        load(5, c_hbm, c_edge, 0, 0, 16),
        load(6, c_hbm, c_edge, 48, 16, 16),
    ]
    pieces = ((s_hbm, s_edge, 0), (v_hbm, v_edge, 0), (v_hbm, v_mid, 8), (s_hbm, s_mid, 16), (s_hbm, s_out, 8))
    for source, target, at in pieces:
        copies.append(load(len(copies), source, target, at, 0, 8))
        copies.append(load(len(copies), source, target, 56 - at, 8, 8))
    for copy in copies[:5]:
        copy.start()
    copies[0].wait()

    def one(row):
        first[row - 8] = row_product(s[row - 8], c, 0, row, s_index)

    for k in range(3):
        copies[1 + k].wait()
        rows_loop(8 + 16 * k, 16, one)
        if k == 0:
            for copy in copies[5:]:
                copy.start()
    copies[4].wait()

    def two(row):
        second[row - 16] = row_product(v[row - 16], first, 8, row, v_index)

    rows_loop(16, 32, two)
    _, y, _ = coords()
    for step in range(NY):
        start = layer_start(1, (y + step) % NY)
        for k in range(4):
            layer1[4 * step + k] = row_product(s[start + k - 8], second, 16, start + k, s_index)
    for copy in copies[5:]:
        copy.wait()


def inner(s_index, v_index, c, s, v):
    stored = jax.ShapeDtypeStruct((16, 2, BS, BS), BF)
    return pl.pallas_call(
        inner_kernel,
        out_shape=[blocks_of(48), blocks_of(32), blocks_of(16), blocks_of(32)] + [stored] * 5,
        in_specs=[SMEM, SMEM, HBM, HBM, HBM],
        out_specs=[VMEM] * 9,
        scratch_shapes=[
            pltpu.VMEM((64, BS, BS), BF),
            pltpu.VMEM((48, 2, BS, BS), BF),
            pltpu.VMEM((32, 2, BS, BS), BF),
            pltpu.SemaphoreType.DMA((17,)),
        ],
        compiler_params=params(44),
        cost_estimate=cost(96, 14 * 2**20),
    )(s_index, v_index, c, s, v)


def place(ref, far, near, head_at, tail_at):
    odd = lax.axis_index("sec") % 2
    ref[pl.ds(jnp.where(odd == 1, tail_at, head_at), 8)] = far[...]
    ref[pl.ds(jnp.where(odd == 1, head_at, tail_at), 8)] = near[...]


def edge_rows(index, ext, x, far, near):
    odd = lax.axis_index("sec") % 2
    for out, high in ((far, odd), (near, 1 - odd)):
        for k in range(8):
            out[k] = row_product(x[8 * high + k], ext, 32 * high - 8, 56 * high + k, index)


def first_edges_kernel(index, far_halo, near_halo, c, x, far, near, ext):
    place(ext, far_halo, near_halo, 0, 40)
    ext[8:40] = c[...]
    edge_rows(index, ext, x, far, near)


def second_edges_kernel(
    index, far_halo, near_halo, f_far, f_near, first, x, after, far, near, ext
):
    place(ext, far_halo, near_halo, 0, 40)
    place(ext, f_far, f_near, 8, 32)
    ext[16:24] = first[0:8]
    ext[24:32] = first[40:48]
    edge_rows(index, ext, x, far, near)


def edges(kernel, *operands):
    return pl.pallas_call(
        kernel,
        out_shape=[blocks_of(8)] * 2,
        in_specs=[SMEM] + [VMEM] * (len(operands) - 1),
        out_specs=[VMEM] * 2,
        scratch_shapes=[pltpu.VMEM((48, BS, BS), BF)],
        compiler_params=params(4),
        cost_estimate=cost(16, 3 * 2**20),
    )(*operands)


def middle_kernel(
    s_index, v_index, far, near, first, second, layer1, v, s, low_out, high_out, b0, b1, b2, b3, f, e
):
    place(f, far, near, 0, 40)
    f[8:24] = first[0:16]
    f[24:40] = first[32:48]
    for k in range(8):
        low_out[k] = row_product(v[k], f, 0, 8 + k, v_index)
        high_out[k] = row_product(v[8 + k], f, 16, 48 + k, v_index)
    e[0:8] = low_out[...]
    e[8:40] = second[...]
    e[40:48] = high_out[...]
    _, y, _ = coords()
    for step, out in enumerate((b0, b1, b2, b3)):
        out[0:4] = layer1[4 * step : 4 * step + 4]
        start = layer_start(2, (y + step) % NY)
        slot = stored_slot(2, start)
        for k in range(4):
            out[4 + k] = row_product(s[slot + k], e, 8, start + k, s_index)


def middle(*operands):
    return pl.pallas_call(
        middle_kernel,
        out_shape=[blocks_of(8)] * 6,
        in_specs=[SMEM, SMEM] + [VMEM] * 7,
        out_specs=[VMEM] * 6,
        scratch_shapes=[pltpu.VMEM((48, BS, BS), BF), pltpu.VMEM((48, BS, BS), BF)],
        compiler_params=params(4),
        cost_estimate=cost(32, 8 * 2**20),
    )(*operands)


def outer_kernel(index, far, near, low, high, second, s, layer3, e):
    place(e, far, near, 0, 40)
    e[8:16] = low[...]
    e[16:24] = second[0:8]
    e[24:32] = second[24:32]
    e[32:40] = high[...]
    _, y, _ = coords()
    for step in range(NY):
        start = layer_start(3, (y + step) % NY)
        slot = stored_slot(3, start)
        base = jnp.where(start < 32, 0, 16)
        for k in range(4):
            layer3[4 * step + k] = row_product(s[slot + k], e, base, start + k, index)


def outer(*operands):
    return pl.pallas_call(
        outer_kernel,
        out_shape=blocks_of(16),
        in_specs=[SMEM] + [VMEM] * 6,
        out_specs=VMEM,
        scratch_shapes=[pltpu.VMEM((48, BS, BS), BF)],
        compiler_params=params(4),
        cost_estimate=cost(16, 4 * 2**20),
    )(*operands)


def last_kernel(
    index, far_halo, near_halo, far, near, low, high, s, gaps, layer3, after1, after2, after3,
    b0, b1, b2, b3, e,
):
    place(e, far_halo, near_halo, 0, 40)
    place(e, far, near, 8, 32)
    e[16:24] = low[...]
    e[24:32] = high[...]
    gap = gaps[...]
    weight = 4.0 * gap / (gap * gap + frequency_sq)
    _, y, _ = coords()
    for k in range(2):
        value = row_product(s[k], e, -8, k, index)
        weighted = (value.astype(F32) * weight).astype(BF)
        for out in (b0, b1, b2, b3):
            out[8 + k] = weighted
    for step, out in enumerate((b0, b1, b2, b3)):
        out[0:4] = layer3[4 * step : 4 * step + 4]
        start = layer_start(4, (y + step) % NY)
        slot = stored_slot(4, start)
        base = jnp.where(start < 32, -8, 24)
        for k in range(4):
            out[4 + k] = row_product(s[slot + k], e, base, start + k, index)


def last(*operands):
    return pl.pallas_call(
        last_kernel,
        out_shape=[blocks_of(10)] * 4,
        in_specs=[SMEM] + [VMEM] * 12,
        out_specs=[VMEM] * 4,
        scratch_shapes=[pltpu.VMEM((48, BS, BS), BF)],
        compiler_params=params(4),
        cost_estimate=cost(18, 4 * 2**20),
    )(*operands)


def product_kernel(*refs):
    inside, outside = refs[:4], refs[4:8]
    own, outs, b, w = refs[8], refs[9:16], refs[16], refs[17]
    for source in range(4):
        lanes = slice(source * BS, (source + 1) * BS)
        for k in range(2):
            b[k, :, lanes] = inside[source][4 * k : 4 * k + 4].reshape(4 * BS, BS)
            b[2 + k, :, lanes] = outside[source][4 * k : 4 * k + 4].reshape(4 * BS, BS)
        w[:, lanes] = outside[source][8:10].reshape(QC, BS)
    x, y, z = coords()
    for step in range(NX):
        to = x ^ step
        near = jnp.where(to == 2, 0, jnp.where(to == 1, 1, jnp.where(to == 3, 2, 3)))
        away = jnp.where(to == 1, 0, jnp.where(to == 2, 1, jnp.where(to == 0, 2, 3)))
        layer = jnp.where(y < 2, near, away)
        for flip in range(NZ):
            half = z ^ flip
            tile = lax.dot_general(
                b[layer, pl.ds(pl.multiple_of(half * QC, QC), QC), :],
                w[...],
                (((1,), (1,)), ((), ())),
                preferred_element_type=F32,
            )
            if step == 0 and flip == 0:
                own[...] = tile
            else:
                outs[step * NZ + flip - 1][...] = tile.astype(BF)


def product(*operands):
    tile = jax.ShapeDtypeStruct((QC, QC), BF)
    return pl.pallas_call(
        product_kernel,
        out_shape=[jax.ShapeDtypeStruct((QC, QC), F32)] + [tile] * 7,
        in_specs=[VMEM] * 8,
        out_specs=[VMEM] * 8,
        scratch_shapes=[pltpu.VMEM((4, 4 * BS, 4 * BS), BF), pltpu.VMEM((QC, 4 * BS), BF)],
        compiler_params=params(8),
        cost_estimate=pl.CostEstimate(
            flops=2 * 2048 * 512 * 256, bytes_accessed=8 * 2**20, transcendentals=0
        ),
    )(*operands)


def add_kernel(*refs):
    total = refs[0][...]
    for ref in refs[1:8]:
        total += ref[...].astype(F32)
    refs[8][0] = total


def add_up(own, others):
    return pl.pallas_call(
        add_kernel,
        out_shape=jax.ShapeDtypeStruct((1, QC, QC), F32),
        in_specs=[VMEM] * 8,
        out_specs=VMEM,
        compiler_params=params(8),
        cost_estimate=pl.CostEstimate(flops=8 * QC * QC, bytes_accessed=2**20, transcendentals=0),
    )(own, *others)


def swap(value, dx, dy, dz):
    pairs = []
    for x in range(NX):
        for y in range(NY):
            for z in range(NZ):
                pairs.append(((x * NY + y) * NZ + z, ((x ^ dx) * NY + (y ^ dy)) * NZ + (z ^ dz)))
    return lax.ppermute(value, "grp", pairs)


def halo(far, near):
    count = lax.axis_size("sec")
    far_pairs = [(i, (i + 1 if i % 2 else i - 1) % count) for i in range(count)]
    near_pairs = [(i, i ^ 1) for i in range(count)]
    return lax.ppermute(far, "sec", far_pairs), lax.ppermute(near, "sec", near_pairs)


def spread_y(parts):
    out = [parts[0]]
    for d in range(1, NY):
        pairs = []
        for k in range(NX * NY * NZ):
            x, y, z = k // (NY * NZ), k // NZ % NY, k % NZ
            pairs.append((k, (x * NY + (y + d) % NY) * NZ + z))
        out.append(lax.ppermute(parts[d], "grp", pairs))
    return out


def on_device(coefficients, energy_gaps, metric_blocks, metric_index, coulomb_blocks, coulomb_index):
    c = coefficients.reshape(ROWS, BS, BS)
    s, v = metric_blocks, coulomb_blocks
    first_row = lax.axis_index("sec") * ROWS
    s_index, v_index = positions(metric_index, first_row), positions(coulomb_index, first_row)
    gaps = energy_gaps.reshape(1, BS)

    odd = lax.axis_index("sec") % 2 == 1
    c_far, c_near = halo(jnp.where(odd, c[56:], c[:8]), jnp.where(odd, c[:8], c[56:]))
    first, second, layer1, c_edge, s_edge, v_edge, v_mid, s_mid, s_out = inner(s_index, v_index, c, s, v)
    f_sends = edges(first_edges_kernel, s_index, c_far, c_near, c_edge, s_edge)
    f_halos = halo(*f_sends)
    e_low, e_high, *inside = middle(s_index, v_index, *f_sends, first, second, layer1, v_mid, s_mid)
    inside = spread_y(inside)
    e_sends = edges(second_edges_kernel, v_index, *f_halos, *f_sends, first, v_edge, e_low)
    e_halos = halo(*e_sends)
    layer3 = outer(s_index, *e_sends, e_low, e_high, second, s_out)
    outside = last(
        s_index, *e_halos, *e_sends, e_low, e_high, s_edge, gaps, layer3, *inside[1:]
    )
    outside = spread_y(outside)
    own, *others = product(*inside, *outside)
    sent = [
        swap(others[step * NZ + flip - 1], step, 0, flip)
        for step in range(NX)
        for flip in range(NZ)
        if step or flip
    ]
    return add_up(own, sent)


def solution(mesh):
    placed = (
        P("sec", "grp"),
        P("grp"),
        P("sec", None, None, None),
        P("sec", None),
        P("sec", None, None, None),
        P("sec", None),
    )
    return jax.shard_map(
        on_device, mesh=mesh, in_specs=placed, out_specs=P("sec", "grp", None), check_vma=False
    )
```

time: 88.5 us -> 79.1 us (0.89)
  the two profiles are of different devices: /device:TPU:64 before, /device:TPU:40 now
where the time goes in v2:
time: 79.1 us; the launch traced here: 79 us
  starting transfers between devices  33.8 us (43%)
  waiting for transfers between devices  29.5 us (37%)
  Pallas kernels  13.8 us (17%)
  other arithmetic  1.77 us (2%)
    ppermute x6, waiting for transfers between devices, spread_y(): out.append(lax.ppermute(parts[d], 'grp', pairs))  17.8 us
    ppermute x7, starting transfers between devices, swap(): return lax.ppermute(value, 'grp', pairs)  13.8 us
    ppermute x6, starting transfers between devices, spread_y(): out.append(lax.ppermute(parts[d], 'grp', pairs))  10 us
    ppermute x3, starting transfers between devices, halo(): lax.ppermute(far, 'sec', far_pairs)  9.99 us
    ppermute x7, waiting for transfers between devices, swap(): return lax.ppermute(value, 'grp', pairs)  8.72 us
    pallas_call x1, Pallas kernels, inner(): pl.pallas_call(inner_kernel, out_shape=[blocks_of(48), blocks_of(32), blo...  5.77 us
    ppermute x3, waiting for transfers between devices, halo(): lax.ppermute(far, 'sec', far_pairs)  2.93 us
    pallas_call x2, Pallas kernels, edges(): pl.pallas_call(kernel, out_shape=[blocks_of(8)] * 2, in_specs=[SMEM] + [V...  2.19 us
  transfers between devices with their start and end apart: 19, of which 11 were waited for; matrix products, arithmetic and copies ran while one was open for 1% of the time, Pallas kernels for 12%

profile of v2, /device:TPU:40, one launch (start us, length us, event | category | flops | bytes accessed | tf_op | source)
XLA Modules:
  0.0 79.0 jit_solution(13188709515781517467)
XLA Ops:
  0.0 1.1 %broadcast_select_fusion = (bf16[1024,128]{1,0:T(8,128)(2,1)S(1)}, bf16[1024,128]{1,0:T(8,128)(2,1)S(1)}) fusion(pred[]{:T(512)S(6)} %eq.5, bf16[8192,128]{1,0:T(8,128)(2,1)} %param.6), kind=kLoop, calls=%fused_computation | loop fusion | flops 262144 | bytes 1048577 | tf_op jit(solution)/shard_map/jit(_where)/select_n | solution.py:390
  1.1 4.9 %collective-permute-start = (bf16[8,128,128]{2,1,0:T(8,128)(2,1)S(1)}, bf16[8,128,128]{2,1,0:T(8,128)(2,1)S(1)}, u32[]{:S(2)}, u32[]{:S(2)}) collective-permute-start(bf16[8,128,128]{2,1,0:T(8,128)(2,1)S(1)} %bitcast.17), channel_id=1, source_target_pairs={{0,7},{1,2},{2,1},{3,4},{4,3},{5,6},{6,5},{7,0},{8,15},{9,10},{10,... | collective-permute-start | bytes 786440 | tf_op jit(solution)/shard_map/ppermute | solution.py:368
  6.7 5.8 %shard_map.64 = (bf16[48,128,128]{2,1,0:T(8,128)(2,1)S(1)}, bf16[32,128,128]{2,1,0:T(8,128)(2,1)S(1)}, bf16[16,128,128]{2,1,0:T(8,128)(2,1)S(1)}, bf16[32,128,12...) custom-call(s32[64]{0:T(128)S(1)} %get-tuple-element.70.s_index.inde, ...), custom_call_target="tpu_custom_call" | custom-call | flops 805306368 | bytes 14680064 | tf_op jit(solution)/shard_map/pallas_call | solution.py:139
  12.9 1.1 %shard_map.65 = (bf16[8,128,128]{2,1,0:T(8,128)(2,1)S(1)}, bf16[8,128,128]{2,1,0:T(8,128)(2,1)S(1)}) custom-call(s32[64]{0:T(128)S(1)} %get-tuple-element.70.s_index.index, bf16[8,128,128]{2,1,0:T(8,128)(2,1)S(1)} %collective-permute-done.far_halo, bf16[8,128,128]{2,1,0:T(8,128)(2,1)S(1)} %collective-permute-done.1.near_halo, ...), custom_call_target="tpu_custom_call" | custom-call | flops 134217728 | bytes 3145728 | tf_op jit(solution)/shard_map/pallas_call | solution.py:185
  14.0 2.5 %collective-permute-start.5 = (bf16[8,128,128]{2,1,0:T(8,128)(2,1)S(1)}, bf16[8,128,128]{2,1,0:T(8,128)(2,1)S(1)}, u32[]{:S(2)}, u32[]{:S(2)}) collective-permute-start(bf16[8,128,128]{2,1,0:T(8,128)(2,1)S(1)} %get-tuple-element.38.far.f_far), channel_id=1, source_target_pairs={{0,7},{1,2},{2,1},{3,4},{4,3},{5,6},{6,5},{7,0},{8,15},{9,10},{10,... | collective-permute-start | bytes 786440 | tf_op jit(solution)/shard_map/ppermute | solution.py:368
  16.5 1.7 %shard_map.66 = (bf16[8,128,128]{2,1,0:T(8,128)(2,1)S(1)}, bf16[8,128,128]{2,1,0:T(8,128)(2,1)S(1)}, bf16[8,128,128]{2,1,0:T(8,128)(2,1)S(1)}, bf16[8,128,128]{2...) custom-call(s32[64]{0:T(128)S(1)} %get-tuple-element.70.s_index.index, ...), custom_call_target="tpu_custom_call" | custom-call | flops 268435456 | bytes 8388608 | tf_op jit(solution)/shard_map/pallas_call | solution.py:218
  18.1 1.7 %collective-permute-start.2 = (bf16[8,128,128]{2,1,0:T(8,128)(2,1)S(1)}, bf16[8,128,128]{2,1,0:T(8,128)(2,1)S(1)}, u32[]{:S(2)}, u32[]{:S(2)}) collective-permute-start(bf16[8,128,128]{2,1,0:T(8,128)(2,1)S(1)} %get-tuple-element.46), channel_id=1, source_target_pairs={{0,16},{8,24},{16,32},{24,40},{32,48},{40,56},{48,0},{56,8},{64,80... | collective-permute-start | bytes 786440 | tf_op jit(solution)/shard_map/ppermute | solution.py:378
  20.8 2.4 %collective-permute-start.4 = (bf16[8,128,128]{2,1,0:T(8,128)(2,1)S(1)}, bf16[8,128,128]{2,1,0:T(8,128)(2,1)S(1)}, u32[]{:S(2)}, u32[]{:S(2)}) collective-permute-start(bf16[8,128,128]{2,1,0:T(8,128)(2,1)S(1)} %get-tuple-element.48), channel_id=1, source_target_pairs={{0,48},{8,56},{16,0},{24,8},{32,16},{40,24},{48,32},{56,40},{64,11... | collective-permute-start | bytes 786440 | tf_op jit(solution)/shard_map/ppermute | solution.py:378
  23.1 1.1 %collective-permute-done.5.far_halo = bf16[8,128,128]{2,1,0:T(8,128)(2,1)S(1)} collective-permute-done((bf16[8,128,128]{2,1,0:T(8,128)(2,1)S(1)}, bf16[8,128,128]{2,1,0:T(8,128)(2,1)S(1)}, u32[]{:S(2)}, u32[]{:S(2)}) %collective-permute-start.5) | collective-permute-done | bytes 262176 | tf_op jit(solution)/shard_map/ppermute | solution.py:368
  24.2 1.1 %shard_map.67 = (bf16[8,128,128]{2,1,0:T(8,128)(2,1)S(1)}, bf16[8,128,128]{2,1,0:T(8,128)(2,1)S(1)}) custom-call(s32[64]{0:T(128)S(1)} %get-tuple-element.69.v_index.index, bf16[8,128,128]{2,1,0:T(8,128)(2,1)S(1)} %collective-permute-done.5.far_halo, bf16[8,128,128]{2,1,0:T(8,128)(2,1)S(1)} %collective-permute-done.6.near_halo, ...), custom_call_target="tpu_custom_call" | custom-call | flops 134217728 | bytes 3145728 | tf_op jit(solution)/shard_map/pallas_call | solution.py:185
  25.3 2.6 %collective-permute-start.7 = (bf16[8,128,128]{2,1,0:T(8,128)(2,1)S(1)}, bf16[8,128,128]{2,1,0:T(8,128)(2,1)S(1)}, u32[]{:S(2)}, u32[]{:S(2)}) collective-permute-start(bf16[8,128,128]{2,1,0:T(8,128)(2,1)S(1)} %get-tuple-element.51.far), channel_id=1, source_target_pairs={{0,7},{1,2},{2,1},{3,4},{4,3},{5,6},{6,5},{7,0},{8,15},{9,10},{10,... | collective-permute-start | bytes 786440 | tf_op jit(solution)/shard_map/ppermute | solution.py:368
  27.9 1.1 %shard_map.68.layer3 = bf16[16,128,128]{2,1,0:T(8,128)(2,1)S(1)} custom-call(s32[64]{0:T(128)S(1)} %get-tuple-element.70.s_index.index, bf16[8,128,128]{2,1,0:T(8,128)(2,1)S(1)} %get-tuple-element.51.far, bf16[8,128,128]{2,1,0:T(8,128)(2,1)S(1)} %get-tuple-element.52.near, bf16[8,128,128]{2,1,0:T(8,128)(2,1)S(1)} %get-tuple-element.50.after.low, ...), custom_call_target="tpu_custom_call" | custom-call | flops 134217728 | bytes 4194304 | tf_op jit(solution)/shard_map/pallas_call | solution.py:245
  29.0 1.4 %collective-permute-done.3.after2.refs_2_ = bf16[8,128,128]{2,1,0:T(8,128)(2,1)S(1)} collective-permute-done((bf16[8,128,128]{2,1,0:T(8,128)(2,1)S(1)}, bf16[8,128,128]{2,1,0:T(8,128)(2,1)S(1)}, u32[]{:S(2)}, u32[]{:S(2)}) %collective-permute-start.3) | collective-permute-done | bytes 262176 | tf_op jit(solution)/shard_map/ppermute | solution.py:378
  30.5 4.2 %collective-permute-done.4.after3.refs_3_ = bf16[8,128,128]{2,1,0:T(8,128)(2,1)S(1)} collective-permute-done((bf16[8,128,128]{2,1,0:T(8,128)(2,1)S(1)}, bf16[8,128,128]{2,1,0:T(8,128)(2,1)S(1)}, u32[]{:S(2)}, u32[]{:S(2)}) %collective-permute-start.4) | collective-permute-done | bytes 262176 | tf_op jit(solution)/shard_map/ppermute | solution.py:378
  34.7 1.5 %collective-permute-done.7.far_halo = bf16[8,128,128]{2,1,0:T(8,128)(2,1)S(1)} collective-permute-done((bf16[8,128,128]{2,1,0:T(8,128)(2,1)S(1)}, bf16[8,128,128]{2,1,0:T(8,128)(2,1)S(1)}, u32[]{:S(2)}, u32[]{:S(2)}) %collective-permute-start.7) | collective-permute-done | bytes 262176 | tf_op jit(solution)/shard_map/ppermute | solution.py:368
  36.2 1.1 %shard_map.69 = (bf16[10,128,128]{2,1,0:T(8,128)(2,1)S(1)}, bf16[10,128,128]{2,1,0:T(8,128)(2,1)S(1)}, bf16[10,128,128]{2,1,0:T(8,128)(2,1)S(1)}, bf16[10,128,128]{2,1,0:T(8,128)(2,1)S(1)}) custom-call(s32[64]{0:T(128)S(1)} %get-tuple-element.70.s_index.index, bf16[8,128,128]{2,1,0:T(8,128)(2,1)S(1)} %collective-permute-done.7.far_halo, ...), custom_call_target="tpu_custom_call" | custom-call | flops 150994944 | bytes 4194304 | tf_op jit(solution)/shard_map/pallas_call | solution.py:282
  37.3 1.7 %collective-permute-start.9 = (bf16[10,128,128]{2,1,0:T(8,128)(2,1)S(1)}, bf16[10,128,128]{2,1,0:T(8,128)(2,1)S(1)}, u32[]{:S(2)}, u32[]{:S(2)}) collective-permute-start(bf16[10,128,128]{2,1,0:T(8,128)(2,1)S(1)} %get-tuple-element.56), channel_id=1, source_target_pairs={{0,16},{8,24},{16,32},{24,40},{32,48},{40,56},{48,0},{56,8},{64,80... | collective-permute-start | bytes 983048 | tf_op jit(solution)/shard_map/ppermute | solution.py:378
  39.0 1.0 %collective-permute-start.10 = (bf16[10,128,128]{2,1,0:T(8,128)(2,1)S(1)}, bf16[10,128,128]{2,1,0:T(8,128)(2,1)S(1)}, u32[]{:S(2)}, u32[]{:S(2)}) collective-permute-start(bf16[10,128,128]{2,1,0:T(8,128)(2,1)S(1)} %get-tuple-element.57), channel_id=1, source_target_pairs={{0,32},{8,40},{16,48},{24,56},{32,0},{40,8},{48,16},{56,24},{64,96... | collective-permute-start | bytes 983048 | tf_op jit(solution)/shard_map/ppermute | solution.py:378
  40.0 2.4 %collective-permute-start.11 = (bf16[10,128,128]{2,1,0:T(8,128)(2,1)S(1)}, bf16[10,128,128]{2,1,0:T(8,128)(2,1)S(1)}, u32[]{:S(2)}, u32[]{:S(2)}) collective-permute-start(bf16[10,128,128]{2,1,0:T(8,128)(2,1)S(1)} %get-tuple-element.58), channel_id=1, source_target_pairs={{0,48},{8,56},{16,0},{24,8},{32,16},{40,24},{48,32},{56,40},{64,11... | collective-permute-start | bytes 983048 | tf_op jit(solution)/shard_map/ppermute | solution.py:378
  42.3 5.7 %collective-permute-done.9.refs_5_ = bf16[10,128,128]{2,1,0:T(8,128)(2,1)S(1)} collective-permute-done((bf16[10,128,128]{2,1,0:T(8,128)(2,1)S(1)}, bf16[10,128,128]{2,1,0:T(8,128)(2,1)S(1)}, u32[]{:S(2)}, u32[]{:S(2)}) %collective-permute-start.9) | collective-permute-done | bytes 327712 | tf_op jit(solution)/shard_map/ppermute | solution.py:378
  48.0 3.0 %collective-permute-done.10.refs_6_ = bf16[10,128,128]{2,1,0:T(8,128)(2,1)S(1)} collective-permute-done((bf16[10,128,128]{2,1,0:T(8,128)(2,1)S(1)}, bf16[10,128,128]{2,1,0:T(8,128)(2,1)S(1)}, u32[]{:S(2)}, u32[]{:S(2)}) %collective-permute-start.10) | collective-permute-done | bytes 327712 | tf_op jit(solution)/shard_map/ppermute | solution.py:378
  51.0 3.5 %collective-permute-done.11.refs_7_ = bf16[10,128,128]{2,1,0:T(8,128)(2,1)S(1)} collective-permute-done((bf16[10,128,128]{2,1,0:T(8,128)(2,1)S(1)}, bf16[10,128,128]{2,1,0:T(8,128)(2,1)S(1)}, u32[]{:S(2)}, u32[]{:S(2)}) %collective-permute-start.11) | collective-permute-done | bytes 327712 | tf_op jit(solution)/shard_map/ppermute | solution.py:378
  54.5 1.1 %shard_map.70 = (f32[256,256]{1,0:T(8,128)S(1)}, bf16[256,256]{1,0:T(8,128)(2,1)S(1)}, bf16[256,256]{1,0:T(8,128)(2,1)S(1)}, bf16[256,256]{1,0:T(8,128)(2,1)S(1)...) custom-call(bf16[8,128,128]{2,1,0:T(8,128)(2,1)S(1)} %get-tuple-elem, ...), custom_call_target="tpu_custom_call" | custom-call | flops 536870912 | bytes 8388608 | tf_op jit(solution)/shard_map/pallas_call | solution.py:324
  55.6 2.5 %collective-permute-start.12 = (bf16[256,256]{1,0:T(8,128)(2,1)S(1)}, bf16[256,256]{1,0:T(8,128)(2,1)S(1)}, u32[]{:S(2)}, u32[]{:S(2)}) collective-permute-start(bf16[256,256]{1,0:T(8,128)(2,1)S(1)} %get-tuple-element.60), channel_id=1, source_target_pairs={{0,8},{8,0},{16,24},{24,16},{32,40},{40,32},{48,56},{56,48},{64,72... | collective-permute-start | bytes 393224 | tf_op jit(solution)/shard_map/ppermute | solution.py:361
  58.1 1.5 %collective-permute-start.13 = (bf16[256,256]{1,0:T(8,128)(2,1)S(1)}, bf16[256,256]{1,0:T(8,128)(2,1)S(1)}, u32[]{:S(2)}, u32[]{:S(2)}) collective-permute-start(bf16[256,256]{1,0:T(8,128)(2,1)S(1)} %get-tuple-element.61), channel_id=1, source_target_pairs={{0,64},{8,72},{16,80},{24,88},{32,96},{40,104},{48,112},{56,120},{... | collective-permute-start | bytes 393224 | tf_op jit(solution)/shard_map/ppermute | solution.py:361
  59.7 3.0 %collective-permute-start.15 = (bf16[256,256]{1,0:T(8,128)(2,1)S(1)}, bf16[256,256]{1,0:T(8,128)(2,1)S(1)}, u32[]{:S(2)}, u32[]{:S(2)}) collective-permute-start(bf16[256,256]{1,0:T(8,128)(2,1)S(1)} %get-tuple-element.63), channel_id=1, source_target_pairs={{0,128},{8,136},{16,144},{24,152},{32,160},{40,168},{48,176},{56,1... | collective-permute-start | bytes 393224 | tf_op jit(solution)/shard_map/ppermute | solution.py:361
  62.7 1.9 %collective-permute-start.16 = (bf16[256,256]{1,0:T(8,128)(2,1)S(1)}, bf16[256,256]{1,0:T(8,128)(2,1)S(1)}, u32[]{:S(2)}, u32[]{:S(2)}) collective-permute-start(bf16[256,256]{1,0:T(8,128)(2,1)S(1)} %get-tuple-element.64), channel_id=1, source_target_pairs={{0,136},{8,128},{16,152},{24,144},{32,168},{40,160},{48,184},{56,1... | collective-permute-start | bytes 393224 | tf_op jit(solution)/shard_map/ppermute | solution.py:361
  64.6 2.8 %collective-permute-start.17 = (bf16[256,256]{1,0:T(8,128)(2,1)S(1)}, bf16[256,256]{1,0:T(8,128)(2,1)S(1)}, u32[]{:S(2)}, u32[]{:S(2)}) collective-permute-start(bf16[256,256]{1,0:T(8,128)(2,1)S(1)} %get-tuple-element.65), channel_id=1, source_target_pairs={{0,192},{8,200},{16,208},{24,216},{32,224},{40,232},{48,240},{56,2... | collective-permute-start | bytes 393224 | tf_op jit(solution)/shard_map/ppermute | solution.py:361
  67.4 1.9 %collective-permute-done.13.refs_2_ = bf16[256,256]{1,0:T(8,128)(2,1)S(1)} collective-permute-done((bf16[256,256]{1,0:T(8,128)(2,1)S(1)}, bf16[256,256]{1,0:T(8,128)(2,1)S(1)}, u32[]{:S(2)}, u32[]{:S(2)}) %collective-permute-start.13) | collective-permute-done | bytes 131104 | tf_op jit(solution)/shard_map/ppermute | solution.py:361
  69.2 2.1 %collective-permute-start.18 = (bf16[256,256]{1,0:T(8,128)(2,1)S(1)}, bf16[256,256]{1,0:T(8,128)(2,1)S(1)}, u32[]{:S(2)}, u32[]{:S(2)}) collective-permute-start(bf16[256,256]{1,0:T(8,128)(2,1)S(1)} %get-tuple-element.66), channel_id=1, source_target_pairs={{0,200},{8,192},{16,216},{24,208},{32,232},{40,224},{48,248},{56,2... | collective-permute-start | bytes 393224 | tf_op jit(solution)/shard_map/ppermute | solution.py:361
  71.3 3.0 %collective-permute-done.15.refs_4_ = bf16[256,256]{1,0:T(8,128)(2,1)S(1)} collective-permute-done((bf16[256,256]{1,0:T(8,128)(2,1)S(1)}, bf16[256,256]{1,0:T(8,128)(2,1)S(1)}, u32[]{:S(2)}, u32[]{:S(2)}) %collective-permute-start.15) | collective-permute-done | bytes 131104 | tf_op jit(solution)/shard_map/ppermute | solution.py:361
  74.3 3.8 %collective-permute-done.17.refs_6_ = bf16[256,256]{1,0:T(8,128)(2,1)S(1)} collective-permute-done((bf16[256,256]{1,0:T(8,128)(2,1)S(1)}, bf16[256,256]{1,0:T(8,128)(2,1)S(1)}, u32[]{:S(2)}, u32[]{:S(2)}) %collective-permute-start.17) | collective-permute-done | bytes 131104 | tf_op jit(solution)/shard_map/ppermute | solution.py:361
  (18 shorter events, 3.0 us)
Async XLA Ops:
  1.1 11.8 %collective-permute-start = (bf16[8,128,128]{2,1,0:T(8,128)(2,1)S(1)}, bf16[8,128,128]{2,1,0:T(8,128)(2,1)S(1)}, u32[]{:S(2)}, u32[]{:S(2)}) collective-permute-start(bf16[8,128,128]{2,1,0:T(8,128)(2,1)S(1)} %bitcast.17), channel_id=1, source_target_pairs={{0,7},{1,2},{2,1},{3,4},{4,3},{5,6},{6,5},{7,0},{8,15},{9,10},{10,... | collective-permute-start | bytes 786440 | tf_op jit(solution)/shard_map/ppermute | solution.py:368
  6.0 6.9 %collective-permute-start.1 = (bf16[8,128,128]{2,1,0:T(8,128)(2,1)S(1)}, bf16[8,128,128]{2,1,0:T(8,128)(2,1)S(1)}, u32[]{:S(2)}, u32[]{:S(2)}) collective-permute-start(bf16[8,128,128]{2,1,0:T(8,128)(2,1)S(1)} %bitcast.16), channel_id=1, source_target_pairs={{0,1},{1,0},{2,3},{3,2},{4,5},{5,4},{6,7},{7,6},{8,9},{9,8},{10,11... | collective-permute-start | bytes 786440 | tf_op jit(solution)/shard_map/ppermute | solution.py:368
  14.0 10.3 %collective-permute-start.5 = (bf16[8,128,128]{2,1,0:T(8,128)(2,1)S(1)}, bf16[8,128,128]{2,1,0:T(8,128)(2,1)S(1)}, u32[]{:S(2)}, u32[]{:S(2)}) collective-permute-start(bf16[8,128,128]{2,1,0:T(8,128)(2,1)S(1)} %get-tuple-element.38.far.f_far), channel_id=1, source_target_pairs={{0,7},{1,2},{2,1},{3,4},{4,3},{5,6},{6,5},{7,0},{8,15},{9,10},{10,... | collective-permute-start | bytes 786440 | tf_op jit(solution)/shard_map/ppermute | solution.py:368
  16.5 7.8 %collective-permute-start.6 = (bf16[8,128,128]{2,1,0:T(8,128)(2,1)S(1)}, bf16[8,128,128]{2,1,0:T(8,128)(2,1)S(1)}, u32[]{:S(2)}, u32[]{:S(2)}) collective-permute-start(bf16[8,128,128]{2,1,0:T(8,128)(2,1)S(1)} %get-tuple-element.39.near.f_near), channel_id=1, source_target_pairs={{0,1},{1,0},{2,3},{3,2},{4,5},{5,4},{6,7},{7,6},{8,9},{9,8},{10,11... | collective-permute-start | bytes 786440 | tf_op jit(solution)/shard_map/ppermute | solution.py:368
  18.1 10.9 %collective-permute-start.2 = (bf16[8,128,128]{2,1,0:T(8,128)(2,1)S(1)}, bf16[8,128,128]{2,1,0:T(8,128)(2,1)S(1)}, u32[]{:S(2)}, u32[]{:S(2)}) collective-permute-start(bf16[8,128,128]{2,1,0:T(8,128)(2,1)S(1)} %get-tuple-element.46), channel_id=1, source_target_pairs={{0,16},{8,24},{16,32},{24,40},{32,48},{40,56},{48,0},{56,8},{64,80... | collective-permute-start | bytes 786440 | tf_op jit(solution)/shard_map/ppermute | solution.py:378
  19.8 10.7 %collective-permute-start.3 = (bf16[8,128,128]{2,1,0:T(8,128)(2,1)S(1)}, bf16[8,128,128]{2,1,0:T(8,128)(2,1)S(1)}, u32[]{:S(2)}, u32[]{:S(2)}) collective-permute-start(bf16[8,128,128]{2,1,0:T(8,128)(2,1)S(1)} %get-tuple-element.47), channel_id=1, source_target_pairs={{0,32},{8,40},{16,48},{24,56},{32,0},{40,8},{48,16},{56,24},{64,96... | collective-permute-start | bytes 786440 | tf_op jit(solution)/shard_map/ppermute | solution.py:378
  20.8 13.9 %collective-permute-start.4 = (bf16[8,128,128]{2,1,0:T(8,128)(2,1)S(1)}, bf16[8,128,128]{2,1,0:T(8,128)(2,1)S(1)}, u32[]{:S(2)}, u32[]{:S(2)}) collective-permute-start(bf16[8,128,128]{2,1,0:T(8,128)(2,1)S(1)} %get-tuple-element.48), channel_id=1, source_target_pairs={{0,48},{8,56},{16,0},{24,8},{32,16},{40,24},{48,32},{56,40},{64,11... | collective-permute-start | bytes 786440 | tf_op jit(solution)/shard_map/ppermute | solution.py:378
  25.3 10.8 %copy-start = (f32[128]{0:T(128)S(1)}, f32[128]{0:T(128)}, u32[]{:S(2)}) copy-start(f32[128]{0:T(128)} %param.7) | copy-start | bytes 1540
  25.3 10.8 %collective-permute-start.7 = (bf16[8,128,128]{2,1,0:T(8,128)(2,1)S(1)}, bf16[8,128,128]{2,1,0:T(8,128)(2,1)S(1)}, u32[]{:S(2)}, u32[]{:S(2)}) collective-permute-start(bf16[8,128,128]{2,1,0:T(8,128)(2,1)S(1)} %get-tuple-element.51.far), channel_id=1, source_target_pairs={{0,7},{1,2},{2,1},{3,4},{4,3},{5,6},{6,5},{7,0},{8,15},{9,10},{10,... | collective-permute-start | bytes 786440 | tf_op jit(solution)/shard_map/ppermute | solution.py:368
  27.9 8.2 %collective-permute-start.8 = (bf16[8,128,128]{2,1,0:T(8,128)(2,1)S(1)}, bf16[8,128,128]{2,1,0:T(8,128)(2,1)S(1)}, u32[]{:S(2)}, u32[]{:S(2)}) collective-permute-start(bf16[8,128,128]{2,1,0:T(8,128)(2,1)S(1)} %get-tuple-element.52.near), channel_id=1, source_target_pairs={{0,1},{1,0},{2,3},{3,2},{4,5},{5,4},{6,7},{7,6},{8,9},{9,8},{10,11... | collective-permute-start | bytes 786440 | tf_op jit(solution)/shard_map/ppermute | solution.py:368
  37.3 10.7 %collective-permute-start.9 = (bf16[10,128,128]{2,1,0:T(8,128)(2,1)S(1)}, bf16[10,128,128]{2,1,0:T(8,128)(2,1)S(1)}, u32[]{:S(2)}, u32[]{:S(2)}) collective-permute-start(bf16[10,128,128]{2,1,0:T(8,128)(2,1)S(1)} %get-tuple-element.56), channel_id=1, source_target_pairs={{0,16},{8,24},{16,32},{24,40},{32,48},{40,56},{48,0},{56,8},{64,80... | collective-permute-start | bytes 983048 | tf_op jit(solution)/shard_map/ppermute | solution.py:378
  39.0 12.1 %collective-permute-start.10 = (bf16[10,128,128]{2,1,0:T(8,128)(2,1)S(1)}, bf16[10,128,128]{2,1,0:T(8,128)(2,1)S(1)}, u32[]{:S(2)}, u32[]{:S(2)}) collective-permute-start(bf16[10,128,128]{2,1,0:T(8,128)(2,1)S(1)} %get-tuple-element.57), channel_id=1, source_target_pairs={{0,32},{8,40},{16,48},{24,56},{32,0},{40,8},{48,16},{56,24},{64,96... | collective-permute-start | bytes 983048 | tf_op jit(solution)/shard_map/ppermute | solution.py:378
  40.0 14.5 %collective-permute-start.11 = (bf16[10,128,128]{2,1,0:T(8,128)(2,1)S(1)}, bf16[10,128,128]{2,1,0:T(8,128)(2,1)S(1)}, u32[]{:S(2)}, u32[]{:S(2)}) collective-permute-start(bf16[10,128,128]{2,1,0:T(8,128)(2,1)S(1)} %get-tuple-element.58), channel_id=1, source_target_pairs={{0,48},{8,56},{16,0},{24,8},{32,16},{40,24},{48,32},{56,40},{64,11... | collective-permute-start | bytes 983048 | tf_op jit(solution)/shard_map/ppermute | solution.py:378
  55.6 9.0 %collective-permute-start.12 = (bf16[256,256]{1,0:T(8,128)(2,1)S(1)}, bf16[256,256]{1,0:T(8,128)(2,1)S(1)}, u32[]{:S(2)}, u32[]{:S(2)}) collective-permute-start(bf16[256,256]{1,0:T(8,128)(2,1)S(1)} %get-tuple-element.60), channel_id=1, source_target_pairs={{0,8},{8,0},{16,24},{24,16},{32,40},{40,32},{48,56},{56,48},{64,72... | collective-permute-start | bytes 393224 | tf_op jit(solution)/shard_map/ppermute | solution.py:361
  58.1 11.1 %collective-permute-start.13 = (bf16[256,256]{1,0:T(8,128)(2,1)S(1)}, bf16[256,256]{1,0:T(8,128)(2,1)S(1)}, u32[]{:S(2)}, u32[]{:S(2)}) collective-permute-start(bf16[256,256]{1,0:T(8,128)(2,1)S(1)} %get-tuple-element.61), channel_id=1, source_target_pairs={{0,64},{8,72},{16,80},{24,88},{32,96},{40,104},{48,112},{56,120},{... | collective-permute-start | bytes 393224 | tf_op jit(solution)/shard_map/ppermute | solution.py:361
  59.6 11.7 %collective-permute-start.14 = (bf16[256,256]{1,0:T(8,128)(2,1)S(1)}, bf16[256,256]{1,0:T(8,128)(2,1)S(1)}, u32[]{:S(2)}, u32[]{:S(2)}) collective-permute-start(bf16[256,256]{1,0:T(8,128)(2,1)S(1)} %get-tuple-element.62), channel_id=1, source_target_pairs={{0,72},{8,64},{16,88},{24,80},{32,104},{40,96},{48,120},{56,112},{... | collective-permute-start | bytes 393224 | tf_op jit(solution)/shard_map/ppermute | solution.py:361
  59.7 14.7 %collective-permute-start.15 = (bf16[256,256]{1,0:T(8,128)(2,1)S(1)}, bf16[256,256]{1,0:T(8,128)(2,1)S(1)}, u32[]{:S(2)}, u32[]{:S(2)}) collective-permute-start(bf16[256,256]{1,0:T(8,128)(2,1)S(1)} %get-tuple-element.63), channel_id=1, source_target_pairs={{0,128},{8,136},{16,144},{24,152},{32,160},{40,168},{48,176},{56,1... | collective-permute-start | bytes 393224 | tf_op jit(solution)/shard_map/ppermute | solution.py:361
  62.7 11.6 %collective-permute-start.16 = (bf16[256,256]{1,0:T(8,128)(2,1)S(1)}, bf16[256,256]{1,0:T(8,128)(2,1)S(1)}, u32[]{:S(2)}, u32[]{:S(2)}) collective-permute-start(bf16[256,256]{1,0:T(8,128)(2,1)S(1)} %get-tuple-element.64), channel_id=1, source_target_pairs={{0,136},{8,128},{16,152},{24,144},{32,168},{40,160},{48,184},{56,1... | collective-permute-start | bytes 393224 | tf_op jit(solution)/shard_map/ppermute | solution.py:361
  64.6 13.6 %collective-permute-start.17 = (bf16[256,256]{1,0:T(8,128)(2,1)S(1)}, bf16[256,256]{1,0:T(8,128)(2,1)S(1)}, u32[]{:S(2)}, u32[]{:S(2)}) collective-permute-start(bf16[256,256]{1,0:T(8,128)(2,1)S(1)} %get-tuple-element.65), channel_id=1, source_target_pairs={{0,192},{8,200},{16,208},{24,216},{32,224},{40,232},{48,240},{56,2... | collective-permute-start | bytes 393224 | tf_op jit(solution)/shard_map/ppermute | solution.py:361
  69.2 8.9 %collective-permute-start.18 = (bf16[256,256]{1,0:T(8,128)(2,1)S(1)}, bf16[256,256]{1,0:T(8,128)(2,1)S(1)}, u32[]{:S(2)}, u32[]{:S(2)}) collective-permute-start(bf16[256,256]{1,0:T(8,128)(2,1)S(1)} %get-tuple-element.66), channel_id=1, source_target_pairs={{0,200},{8,192},{16,216},{24,208},{32,232},{40,224},{48,248},{56,2... | collective-permute-start | bytes 393224 | tf_op jit(solution)/shard_map/ppermute | solution.py:361

commit v3 on v2

--- a/solution.py
+++ b/solution.py
@@ -368,15 +368,15 @@
     return lax.ppermute(far, "sec", far_pairs), lax.ppermute(near, "sec", near_pairs)
 
 
-def spread_y(parts):
-    out = [parts[0]]
-    for d in range(1, NY):
+def spread_y(parts, order=(1, 3, 2)):
+    out = {0: parts[0]}
+    for d in order:
         pairs = []
         for k in range(NX * NY * NZ):
             x, y, z = k // (NY * NZ), k // NZ % NY, k % NZ
             pairs.append((k, (x * NY + (y + d) % NY) * NZ + z))
-        out.append(lax.ppermute(parts[d], "grp", pairs))
-    return out
+        out[d] = lax.ppermute(parts[d], "grp", pairs)
+    return list(out.values())
 
 
 def on_device(coefficients, energy_gaps, metric_blocks, metric_index, coulomb_blocks, coulomb_index):
@@ -401,12 +401,7 @@
     )
     outside = spread_y(outside)
     own, *others = product(*inside, *outside)
-    sent = [
-        swap(others[step * NZ + flip - 1], step, 0, flip)
-        for step in range(NX)
-        for flip in range(NZ)
-        if step or flip
-    ]
+    sent = [swap(others[step * NZ + flip - 1], step, 0, flip) for step, flip in ((0, 1), (1, 0), (3, 0), (2, 0), (1, 1), (3, 1), (2, 1))]
     return add_up(own, sent)
 
 

time: 79.1 us -> 74.9 us (0.947)
  the two profiles are of different devices: /device:TPU:40 before, /device:TPU:64 now
where the time goes in v3:
time: 74.9 us; the launch traced here: 74.3 us
  starting transfers between devices  31.6 us (42%)
  waiting for transfers between devices  27 us (36%)
  Pallas kernels  13.8 us (18%)
  other arithmetic  1.77 us (2%)
    ppermute x6, waiting for transfers between devices, spread_y(): out[d] = lax.ppermute(parts[d], 'grp', pairs)  20.5 us
    ppermute x7, starting transfers between devices, swap(): return lax.ppermute(value, 'grp', pairs)  10.8 us
    ppermute x3, starting transfers between devices, halo(): lax.ppermute(near, 'sec', near_pairs)  10.5 us
    ppermute x6, starting transfers between devices, spread_y(): out[d] = lax.ppermute(parts[d], 'grp', pairs)  8.85 us
    ppermute x7, waiting for transfers between devices, swap(): return lax.ppermute(value, 'grp', pairs)  6.52 us
    pallas_call x1, Pallas kernels, inner(): pl.pallas_call(inner_kernel, out_shape=[blocks_of(48), blocks_of(32), blo...  5.77 us
    pallas_call x2, Pallas kernels, edges(): pl.pallas_call(kernel, out_shape=[blocks_of(8)] * 2, in_specs=[SMEM] + [V...  2.2 us
    pallas_call x1, Pallas kernels, middle(): pl.pallas_call(middle_kernel, out_shape=[blocks_of(8)] * 6, in_specs=[SME...  1.68 us
  transfers between devices with their start and end apart: 19, of which 8 were waited for; matrix products, arithmetic and copies ran while one was open for 1% of the time, Pallas kernels for 13%

profile of v3, /device:TPU:64, one launch (start us, length us, event | category | flops | bytes accessed | tf_op | source)
XLA Modules:
  0.0 74.3 jit_solution(6279228928962824866)
XLA Ops:
  0.0 1.1 %broadcast_select_fusion = (bf16[1024,128]{1,0:T(8,128)(2,1)S(1)}, bf16[1024,128]{1,0:T(8,128)(2,1)S(1)}) fusion(pred[]{:T(512)S(6)} %eq.5, bf16[8192,128]{1,0:T(8,128)(2,1)} %param.6), kind=kLoop, calls=%fused_computation | loop fusion | flops 262144 | bytes 1048577 | tf_op jit(solution)/shard_map/jit(_where)/select_n | solution.py:390
  1.2 4.6 %collective-permute-start.1 = (bf16[8,128,128]{2,1,0:T(8,128)(2,1)S(1)}, bf16[8,128,128]{2,1,0:T(8,128)(2,1)S(1)}, u32[]{:S(2)}, u32[]{:S(2)}) collective-permute-start(bf16[8,128,128]{2,1,0:T(8,128)(2,1)S(1)} %bitcast.16), channel_id=1, source_target_pairs={{0,1},{1,0},{2,3},{3,2},{4,5},{5,4},{6,7},{7,6},{8,9},{9,8},{10,11... | collective-permute-start | bytes 786440 | tf_op jit(solution)/shard_map/ppermute | solution.py:368
  5.8 0.7 compare_select_fusion.4
  6.5 5.8 %shard_map.64 = (bf16[48,128,128]{2,1,0:T(8,128)(2,1)S(1)}, bf16[32,128,128]{2,1,0:T(8,128)(2,1)S(1)}, bf16[16,128,128]{2,1,0:T(8,128)(2,1)S(1)}, bf16[32,128,12...) custom-call(s32[64]{0:T(128)S(1)} %get-tuple-element.70.s_index.inde, ...), custom_call_target="tpu_custom_call" | custom-call | flops 805306368 | bytes 14680064 | tf_op jit(solution)/shard_map/pallas_call | solution.py:139
  12.3 1.1 %shard_map.65 = (bf16[8,128,128]{2,1,0:T(8,128)(2,1)S(1)}, bf16[8,128,128]{2,1,0:T(8,128)(2,1)S(1)}) custom-call(s32[64]{0:T(128)S(1)} %get-tuple-element.70.s_index.index, bf16[8,128,128]{2,1,0:T(8,128)(2,1)S(1)} %collective-permute-done.far_halo, bf16[8,128,128]{2,1,0:T(8,128)(2,1)S(1)} %collective-permute-done.1.near_halo, ...), custom_call_target="tpu_custom_call" | custom-call | flops 134217728 | bytes 3145728 | tf_op jit(solution)/shard_map/pallas_call | solution.py:185
  13.4 1.0 %collective-permute-start.5 = (bf16[8,128,128]{2,1,0:T(8,128)(2,1)S(1)}, bf16[8,128,128]{2,1,0:T(8,128)(2,1)S(1)}, u32[]{:S(2)}, u32[]{:S(2)}) collective-permute-start(bf16[8,128,128]{2,1,0:T(8,128)(2,1)S(1)} %get-tuple-element.38.far.f_far), channel_id=1, source_target_pairs={{0,7},{1,2},{2,1},{3,4},{4,3},{5,6},{6,5},{7,0},{8,15},{9,10},{10,... | collective-permute-start | bytes 786440 | tf_op jit(solution)/shard_map/ppermute | solution.py:368
  14.4 3.0 %collective-permute-start.6 = (bf16[8,128,128]{2,1,0:T(8,128)(2,1)S(1)}, bf16[8,128,128]{2,1,0:T(8,128)(2,1)S(1)}, u32[]{:S(2)}, u32[]{:S(2)}) collective-permute-start(bf16[8,128,128]{2,1,0:T(8,128)(2,1)S(1)} %get-tuple-element.39.near.f_near), channel_id=1, source_target_pairs={{0,1},{1,0},{2,3},{3,2},{4,5},{5,4},{6,7},{7,6},{8,9},{9,8},{10,11... | collective-permute-start | bytes 786440 | tf_op jit(solution)/shard_map/ppermute | solution.py:368
  17.4 1.7 %shard_map.66 = (bf16[8,128,128]{2,1,0:T(8,128)(2,1)S(1)}, bf16[8,128,128]{2,1,0:T(8,128)(2,1)S(1)}, bf16[8,128,128]{2,1,0:T(8,128)(2,1)S(1)}, bf16[8,128,128]{2...) custom-call(s32[64]{0:T(128)S(1)} %get-tuple-element.70.s_index.index, ...), custom_call_target="tpu_custom_call" | custom-call | flops 268435456 | bytes 8388608 | tf_op jit(solution)/shard_map/pallas_call | solution.py:218
  19.1 1.7 %collective-permute-start.2 = (bf16[8,128,128]{2,1,0:T(8,128)(2,1)S(1)}, bf16[8,128,128]{2,1,0:T(8,128)(2,1)S(1)}, u32[]{:S(2)}, u32[]{:S(2)}) collective-permute-start(bf16[8,128,128]{2,1,0:T(8,128)(2,1)S(1)} %get-tuple-element.46), channel_id=1, source_target_pairs={{0,16},{8,24},{16,32},{24,40},{32,48},{40,56},{48,0},{56,8},{64,80... | collective-permute-start | bytes 786440 | tf_op jit(solution)/shard_map/ppermute | solution.py:378
  20.7 1.7 %collective-permute-start.3 = (bf16[8,128,128]{2,1,0:T(8,128)(2,1)S(1)}, bf16[8,128,128]{2,1,0:T(8,128)(2,1)S(1)}, u32[]{:S(2)}, u32[]{:S(2)}) collective-permute-start(bf16[8,128,128]{2,1,0:T(8,128)(2,1)S(1)} %get-tuple-element.47), channel_id=1, source_target_pairs={{0,48},{8,56},{16,0},{24,8},{32,16},{40,24},{48,32},{56,40},{64,11... | collective-permute-start | bytes 786440 | tf_op jit(solution)/shard_map/ppermute | solution.py:378
  22.4 2.0 %collective-permute-start.4 = (bf16[8,128,128]{2,1,0:T(8,128)(2,1)S(1)}, bf16[8,128,128]{2,1,0:T(8,128)(2,1)S(1)}, u32[]{:S(2)}, u32[]{:S(2)}) collective-permute-start(bf16[8,128,128]{2,1,0:T(8,128)(2,1)S(1)} %get-tuple-element.48), channel_id=1, source_target_pairs={{0,32},{8,40},{16,48},{24,56},{32,0},{40,8},{48,16},{56,24},{64,96... | collective-permute-start | bytes 786440 | tf_op jit(solution)/shard_map/ppermute | solution.py:378
  24.4 1.1 %shard_map.67 = (bf16[8,128,128]{2,1,0:T(8,128)(2,1)S(1)}, bf16[8,128,128]{2,1,0:T(8,128)(2,1)S(1)}) custom-call(s32[64]{0:T(128)S(1)} %get-tuple-element.69.v_index.index, bf16[8,128,128]{2,1,0:T(8,128)(2,1)S(1)} %collective-permute-done.5.far_halo, bf16[8,128,128]{2,1,0:T(8,128)(2,1)S(1)} %collective-permute-done.6.near_halo, ...), custom_call_target="tpu_custom_call" | custom-call | flops 134217728 | bytes 3145728 | tf_op jit(solution)/shard_map/pallas_call | solution.py:185
  25.9 2.8 %collective-permute-start.8 = (bf16[8,128,128]{2,1,0:T(8,128)(2,1)S(1)}, bf16[8,128,128]{2,1,0:T(8,128)(2,1)S(1)}, u32[]{:S(2)}, u32[]{:S(2)}) collective-permute-start(bf16[8,128,128]{2,1,0:T(8,128)(2,1)S(1)} %get-tuple-element.52.near), channel_id=1, source_target_pairs={{0,1},{1,0},{2,3},{3,2},{4,5},{5,4},{6,7},{7,6},{8,9},{9,8},{10,11... | collective-permute-start | bytes 786440 | tf_op jit(solution)/shard_map/ppermute | solution.py:368
  28.8 1.1 %shard_map.68.layer3 = bf16[16,128,128]{2,1,0:T(8,128)(2,1)S(1)} custom-call(s32[64]{0:T(128)S(1)} %get-tuple-element.70.s_index.index, bf16[8,128,128]{2,1,0:T(8,128)(2,1)S(1)} %get-tuple-element.51.far, bf16[8,128,128]{2,1,0:T(8,128)(2,1)S(1)} %get-tuple-element.52.near, bf16[8,128,128]{2,1,0:T(8,128)(2,1)S(1)} %get-tuple-element.50.after.low, ...), custom_call_target="tpu_custom_call" | custom-call | flops 134217728 | bytes 4194304 | tf_op jit(solution)/shard_map/pallas_call | solution.py:245
  29.9 3.8 %collective-permute-done.3.after2.refs_2_ = bf16[8,128,128]{2,1,0:T(8,128)(2,1)S(1)} collective-permute-done((bf16[8,128,128]{2,1,0:T(8,128)(2,1)S(1)}, bf16[8,128,128]{2,1,0:T(8,128)(2,1)S(1)}, u32[]{:S(2)}, u32[]{:S(2)}) %collective-permute-start.3) | collective-permute-done | bytes 262176 | tf_op jit(solution)/shard_map/ppermute | solution.py:378
  33.6 1.8 %collective-permute-done.4.after3.refs_3_ = bf16[8,128,128]{2,1,0:T(8,128)(2,1)S(1)} collective-permute-done((bf16[8,128,128]{2,1,0:T(8,128)(2,1)S(1)}, bf16[8,128,128]{2,1,0:T(8,128)(2,1)S(1)}, u32[]{:S(2)}, u32[]{:S(2)}) %collective-permute-start.4) | collective-permute-done | bytes 262176 | tf_op jit(solution)/shard_map/ppermute | solution.py:378
  35.4 1.1 %shard_map.69 = (bf16[10,128,128]{2,1,0:T(8,128)(2,1)S(1)}, bf16[10,128,128]{2,1,0:T(8,128)(2,1)S(1)}, bf16[10,128,128]{2,1,0:T(8,128)(2,1)S(1)}, bf16[10,128,128]{2,1,0:T(8,128)(2,1)S(1)}) custom-call(s32[64]{0:T(128)S(1)} %get-tuple-element.70.s_index.index, bf16[8,128,128]{2,1,0:T(8,128)(2,1)S(1)} %collective-permute-done.7.far_halo, ...), custom_call_target="tpu_custom_call" | custom-call | flops 150994944 | bytes 4194304 | tf_op jit(solution)/shard_map/pallas_call | solution.py:282
  36.6 1.2 %collective-permute-start.9 = (bf16[10,128,128]{2,1,0:T(8,128)(2,1)S(1)}, bf16[10,128,128]{2,1,0:T(8,128)(2,1)S(1)}, u32[]{:S(2)}, u32[]{:S(2)}) collective-permute-start(bf16[10,128,128]{2,1,0:T(8,128)(2,1)S(1)} %get-tuple-element.56), channel_id=1, source_target_pairs={{0,16},{8,24},{16,32},{24,40},{32,48},{40,56},{48,0},{56,8},{64,80... | collective-permute-start | bytes 983048 | tf_op jit(solution)/shard_map/ppermute | solution.py:378
  37.8 2.1 %collective-permute-start.10 = (bf16[10,128,128]{2,1,0:T(8,128)(2,1)S(1)}, bf16[10,128,128]{2,1,0:T(8,128)(2,1)S(1)}, u32[]{:S(2)}, u32[]{:S(2)}) collective-permute-start(bf16[10,128,128]{2,1,0:T(8,128)(2,1)S(1)} %get-tuple-element.57), channel_id=1, source_target_pairs={{0,48},{8,56},{16,0},{24,8},{32,16},{40,24},{48,32},{56,40},{64,11... | collective-permute-start | bytes 983048 | tf_op jit(solution)/shard_map/ppermute | solution.py:378
  40.2 6.8 %collective-permute-done.9.refs_5_ = bf16[10,128,128]{2,1,0:T(8,128)(2,1)S(1)} collective-permute-done((bf16[10,128,128]{2,1,0:T(8,128)(2,1)S(1)}, bf16[10,128,128]{2,1,0:T(8,128)(2,1)S(1)}, u32[]{:S(2)}, u32[]{:S(2)}) %collective-permute-start.9) | collective-permute-done | bytes 327712 | tf_op jit(solution)/shard_map/ppermute | solution.py:378
  46.9 6.6 %collective-permute-done.10.refs_6_ = bf16[10,128,128]{2,1,0:T(8,128)(2,1)S(1)} collective-permute-done((bf16[10,128,128]{2,1,0:T(8,128)(2,1)S(1)}, bf16[10,128,128]{2,1,0:T(8,128)(2,1)S(1)}, u32[]{:S(2)}, u32[]{:S(2)}) %collective-permute-start.10) | collective-permute-done | bytes 327712 | tf_op jit(solution)/shard_map/ppermute | solution.py:378
  53.5 1.6 %collective-permute-done.11.refs_7_ = bf16[10,128,128]{2,1,0:T(8,128)(2,1)S(1)} collective-permute-done((bf16[10,128,128]{2,1,0:T(8,128)(2,1)S(1)}, bf16[10,128,128]{2,1,0:T(8,128)(2,1)S(1)}, u32[]{:S(2)}, u32[]{:S(2)}) %collective-permute-start.11) | collective-permute-done | bytes 327712 | tf_op jit(solution)/shard_map/ppermute | solution.py:378
  55.1 1.1 %shard_map.70 = (f32[256,256]{1,0:T(8,128)S(1)}, bf16[256,256]{1,0:T(8,128)(2,1)S(1)}, bf16[256,256]{1,0:T(8,128)(2,1)S(1)}, bf16[256,256]{1,0:T(8,128)(2,1)S(1)...) custom-call(bf16[8,128,128]{2,1,0:T(8,128)(2,1)S(1)} %get-tuple-elem, ...), custom_call_target="tpu_custom_call" | custom-call | flops 536870912 | bytes 8388608 | tf_op jit(solution)/shard_map/pallas_call | solution.py:324
  56.3 1.6 %collective-permute-start.13 = (bf16[256,256]{1,0:T(8,128)(2,1)S(1)}, bf16[256,256]{1,0:T(8,128)(2,1)S(1)}, u32[]{:S(2)}, u32[]{:S(2)}) collective-permute-start(bf16[256,256]{1,0:T(8,128)(2,1)S(1)} %get-tuple-element.61), channel_id=1, source_target_pairs={{0,64},{8,72},{16,80},{24,88},{32,96},{40,104},{48,112},{56,120},{... | collective-permute-start | bytes 393224 | tf_op jit(solution)/shard_map/ppermute | solution.py:361
  57.9 2.1 %collective-permute-start.14 = (bf16[256,256]{1,0:T(8,128)(2,1)S(1)}, bf16[256,256]{1,0:T(8,128)(2,1)S(1)}, u32[]{:S(2)}, u32[]{:S(2)}) collective-permute-start(bf16[256,256]{1,0:T(8,128)(2,1)S(1)} %get-tuple-element.62), channel_id=1, source_target_pairs={{0,192},{8,200},{16,208},{24,216},{32,224},{40,232},{48,240},{56,2... | collective-permute-start | bytes 393224 | tf_op jit(solution)/shard_map/ppermute | solution.py:361
  60.6 2.7 %collective-permute-start.16 = (bf16[256,256]{1,0:T(8,128)(2,1)S(1)}, bf16[256,256]{1,0:T(8,128)(2,1)S(1)}, u32[]{:S(2)}, u32[]{:S(2)}) collective-permute-start(bf16[256,256]{1,0:T(8,128)(2,1)S(1)} %get-tuple-element.64), channel_id=1, source_target_pairs={{0,72},{8,64},{16,88},{24,80},{32,104},{40,96},{48,120},{56,112},{... | collective-permute-start | bytes 393224 | tf_op jit(solution)/shard_map/ppermute | solution.py:361
  63.4 1.6 %collective-permute-start.17 = (bf16[256,256]{1,0:T(8,128)(2,1)S(1)}, bf16[256,256]{1,0:T(8,128)(2,1)S(1)}, u32[]{:S(2)}, u32[]{:S(2)}) collective-permute-start(bf16[256,256]{1,0:T(8,128)(2,1)S(1)} %get-tuple-element.65), channel_id=1, source_target_pairs={{0,200},{8,192},{16,216},{24,208},{32,232},{40,224},{48,248},{56,2... | collective-permute-start | bytes 393224 | tf_op jit(solution)/shard_map/ppermute | solution.py:361
  65.0 2.0 %collective-permute-start.18 = (bf16[256,256]{1,0:T(8,128)(2,1)S(1)}, bf16[256,256]{1,0:T(8,128)(2,1)S(1)}, u32[]{:S(2)}, u32[]{:S(2)}) collective-permute-start(bf16[256,256]{1,0:T(8,128)(2,1)S(1)} %get-tuple-element.66), channel_id=1, source_target_pairs={{0,136},{8,128},{16,152},{24,144},{32,168},{40,160},{48,184},{56,1... | collective-permute-start | bytes 393224 | tf_op jit(solution)/shard_map/ppermute | solution.py:361
  67.0 1.9 %collective-permute-done.15.refs_4_ = bf16[256,256]{1,0:T(8,128)(2,1)S(1)} collective-permute-done((bf16[256,256]{1,0:T(8,128)(2,1)S(1)}, bf16[256,256]{1,0:T(8,128)(2,1)S(1)}, u32[]{:S(2)}, u32[]{:S(2)}) %collective-permute-start.15) | collective-permute-done | bytes 131104 | tf_op jit(solution)/shard_map/ppermute | solution.py:361
  68.9 3.0 %collective-permute-done.17.refs_6_ = bf16[256,256]{1,0:T(8,128)(2,1)S(1)} collective-permute-done((bf16[256,256]{1,0:T(8,128)(2,1)S(1)}, bf16[256,256]{1,0:T(8,128)(2,1)S(1)}, u32[]{:S(2)}, u32[]{:S(2)}) %collective-permute-start.17) | collective-permute-done | bytes 131104 | tf_op jit(solution)/shard_map/ppermute | solution.py:361
  72.0 1.5 %collective-permute-done.18.refs_7_ = bf16[256,256]{1,0:T(8,128)(2,1)S(1)} collective-permute-done((bf16[256,256]{1,0:T(8,128)(2,1)S(1)}, bf16[256,256]{1,0:T(8,128)(2,1)S(1)}, u32[]{:S(2)}, u32[]{:S(2)}) %collective-permute-start.18) | collective-permute-done | bytes 131104 | tf_op jit(solution)/shard_map/ppermute | solution.py:361
  73.5 0.8 %shard_map.71 = f32[1,256,256]{2,1,0:T(8,128)} custom-call(f32[256,256]{1,0:T(8,128)S(1)} %get-tuple-element.59.refs_0_, bf16[256,256]{1,0:T(8,128)(2,1)S(1)} %collective-permute-done.12.refs_1_, bf16[256,256]{1,0:T(8,128)(2,1)S(1)} %collective-permute-done.13.refs_2_, bf16[256,256]{1,0:T(8,128)(2,1)S(1)} %collective-permute-done.14.refs_3_, ...), custom_call_target="tpu_custom_call" | custom-call | flops 524288 | bytes 1048576 | tf_op jit(solution)/shard_map/pallas_call | solution.py:345
  (18 shorter events, 1.5 us)
Async XLA Ops:
  1.1 11.2 %collective-permute-start = (bf16[8,128,128]{2,1,0:T(8,128)(2,1)S(1)}, bf16[8,128,128]{2,1,0:T(8,128)(2,1)S(1)}, u32[]{:S(2)}, u32[]{:S(2)}) collective-permute-start(bf16[8,128,128]{2,1,0:T(8,128)(2,1)S(1)} %bitcast.17), channel_id=1, source_target_pairs={{0,7},{1,2},{2,1},{3,4},{4,3},{5,6},{6,5},{7,0},{8,15},{9,10},{10,... | collective-permute-start | bytes 786440 | tf_op jit(solution)/shard_map/ppermute | solution.py:368
  1.2 11.1 %collective-permute-start.1 = (bf16[8,128,128]{2,1,0:T(8,128)(2,1)S(1)}, bf16[8,128,128]{2,1,0:T(8,128)(2,1)S(1)}, u32[]{:S(2)}, u32[]{:S(2)}) collective-permute-start(bf16[8,128,128]{2,1,0:T(8,128)(2,1)S(1)} %bitcast.16), channel_id=1, source_target_pairs={{0,1},{1,0},{2,3},{3,2},{4,5},{5,4},{6,7},{7,6},{8,9},{9,8},{10,11... | collective-permute-start | bytes 786440 | tf_op jit(solution)/shard_map/ppermute | solution.py:368
  13.4 11.0 %collective-permute-start.5 = (bf16[8,128,128]{2,1,0:T(8,128)(2,1)S(1)}, bf16[8,128,128]{2,1,0:T(8,128)(2,1)S(1)}, u32[]{:S(2)}, u32[]{:S(2)}) collective-permute-start(bf16[8,128,128]{2,1,0:T(8,128)(2,1)S(1)} %get-tuple-element.38.far.f_far), channel_id=1, source_target_pairs={{0,7},{1,2},{2,1},{3,4},{4,3},{5,6},{6,5},{7,0},{8,15},{9,10},{10,... | collective-permute-start | bytes 786440 | tf_op jit(solution)/shard_map/ppermute | solution.py:368
  14.4 10.0 %collective-permute-start.6 = (bf16[8,128,128]{2,1,0:T(8,128)(2,1)S(1)}, bf16[8,128,128]{2,1,0:T(8,128)(2,1)S(1)}, u32[]{:S(2)}, u32[]{:S(2)}) collective-permute-start(bf16[8,128,128]{2,1,0:T(8,128)(2,1)S(1)} %get-tuple-element.39.near.f_near), channel_id=1, source_target_pairs={{0,1},{1,0},{2,3},{3,2},{4,5},{5,4},{6,7},{7,6},{8,9},{9,8},{10,11... | collective-permute-start | bytes 786440 | tf_op jit(solution)/shard_map/ppermute | solution.py:368
  19.1 10.8 %collective-permute-start.2 = (bf16[8,128,128]{2,1,0:T(8,128)(2,1)S(1)}, bf16[8,128,128]{2,1,0:T(8,128)(2,1)S(1)}, u32[]{:S(2)}, u32[]{:S(2)}) collective-permute-start(bf16[8,128,128]{2,1,0:T(8,128)(2,1)S(1)} %get-tuple-element.46), channel_id=1, source_target_pairs={{0,16},{8,24},{16,32},{24,40},{32,48},{40,56},{48,0},{56,8},{64,80... | collective-permute-start | bytes 786440 | tf_op jit(solution)/shard_map/ppermute | solution.py:378
  20.7 12.9 %collective-permute-start.3 = (bf16[8,128,128]{2,1,0:T(8,128)(2,1)S(1)}, bf16[8,128,128]{2,1,0:T(8,128)(2,1)S(1)}, u32[]{:S(2)}, u32[]{:S(2)}) collective-permute-start(bf16[8,128,128]{2,1,0:T(8,128)(2,1)S(1)} %get-tuple-element.47), channel_id=1, source_target_pairs={{0,48},{8,56},{16,0},{24,8},{32,16},{40,24},{48,32},{56,40},{64,11... | collective-permute-start | bytes 786440 | tf_op jit(solution)/shard_map/ppermute | solution.py:378
  22.4 13.0 %collective-permute-start.4 = (bf16[8,128,128]{2,1,0:T(8,128)(2,1)S(1)}, bf16[8,128,128]{2,1,0:T(8,128)(2,1)S(1)}, u32[]{:S(2)}, u32[]{:S(2)}) collective-permute-start(bf16[8,128,128]{2,1,0:T(8,128)(2,1)S(1)} %get-tuple-element.48), channel_id=1, source_target_pairs={{0,32},{8,40},{16,48},{24,56},{32,0},{40,8},{48,16},{56,24},{64,96... | collective-permute-start | bytes 786440 | tf_op jit(solution)/shard_map/ppermute | solution.py:378
  25.5 10.0 %copy-start = (f32[128]{0:T(128)S(1)}, f32[128]{0:T(128)}, u32[]{:S(2)}) copy-start(f32[128]{0:T(128)} %param.7) | copy-start | bytes 1540
  25.5 9.9 %collective-permute-start.7 = (bf16[8,128,128]{2,1,0:T(8,128)(2,1)S(1)}, bf16[8,128,128]{2,1,0:T(8,128)(2,1)S(1)}, u32[]{:S(2)}, u32[]{:S(2)}) collective-permute-start(bf16[8,128,128]{2,1,0:T(8,128)(2,1)S(1)} %get-tuple-element.51.far), channel_id=1, source_target_pairs={{0,7},{1,2},{2,1},{3,4},{4,3},{5,6},{6,5},{7,0},{8,15},{9,10},{10,... | collective-permute-start | bytes 786440 | tf_op jit(solution)/shard_map/ppermute | solution.py:368
  25.9 9.5 %collective-permute-start.8 = (bf16[8,128,128]{2,1,0:T(8,128)(2,1)S(1)}, bf16[8,128,128]{2,1,0:T(8,128)(2,1)S(1)}, u32[]{:S(2)}, u32[]{:S(2)}) collective-permute-start(bf16[8,128,128]{2,1,0:T(8,128)(2,1)S(1)} %get-tuple-element.52.near), channel_id=1, source_target_pairs={{0,1},{1,0},{2,3},{3,2},{4,5},{5,4},{6,7},{7,6},{8,9},{9,8},{10,11... | collective-permute-start | bytes 786440 | tf_op jit(solution)/shard_map/ppermute | solution.py:368
  36.6 10.3 %collective-permute-start.9 = (bf16[10,128,128]{2,1,0:T(8,128)(2,1)S(1)}, bf16[10,128,128]{2,1,0:T(8,128)(2,1)S(1)}, u32[]{:S(2)}, u32[]{:S(2)}) collective-permute-start(bf16[10,128,128]{2,1,0:T(8,128)(2,1)S(1)} %get-tuple-element.56), channel_id=1, source_target_pairs={{0,16},{8,24},{16,32},{24,40},{32,48},{40,56},{48,0},{56,8},{64,80... | collective-permute-start | bytes 983048 | tf_op jit(solution)/shard_map/ppermute | solution.py:378
  37.8 15.7 %collective-permute-start.10 = (bf16[10,128,128]{2,1,0:T(8,128)(2,1)S(1)}, bf16[10,128,128]{2,1,0:T(8,128)(2,1)S(1)}, u32[]{:S(2)}, u32[]{:S(2)}) collective-permute-start(bf16[10,128,128]{2,1,0:T(8,128)(2,1)S(1)} %get-tuple-element.57), channel_id=1, source_target_pairs={{0,48},{8,56},{16,0},{24,8},{32,16},{40,24},{48,32},{56,40},{64,11... | collective-permute-start | bytes 983048 | tf_op jit(solution)/shard_map/ppermute | solution.py:378
  39.9 15.2 %collective-permute-start.11 = (bf16[10,128,128]{2,1,0:T(8,128)(2,1)S(1)}, bf16[10,128,128]{2,1,0:T(8,128)(2,1)S(1)}, u32[]{:S(2)}, u32[]{:S(2)}) collective-permute-start(bf16[10,128,128]{2,1,0:T(8,128)(2,1)S(1)} %get-tuple-element.58), channel_id=1, source_target_pairs={{0,32},{8,40},{16,48},{24,56},{32,0},{40,8},{48,16},{56,24},{64,96... | collective-permute-start | bytes 983048 | tf_op jit(solution)/shard_map/ppermute | solution.py:378
  56.2 7.1 %collective-permute-start.12 = (bf16[256,256]{1,0:T(8,128)(2,1)S(1)}, bf16[256,256]{1,0:T(8,128)(2,1)S(1)}, u32[]{:S(2)}, u32[]{:S(2)}) collective-permute-start(bf16[256,256]{1,0:T(8,128)(2,1)S(1)} %get-tuple-element.60), channel_id=1, source_target_pairs={{0,8},{8,0},{16,24},{24,16},{32,40},{40,32},{48,56},{56,48},{64,72... | collective-permute-start | bytes 393224 | tf_op jit(solution)/shard_map/ppermute | solution.py:361
  56.3 8.7 %collective-permute-start.13 = (bf16[256,256]{1,0:T(8,128)(2,1)S(1)}, bf16[256,256]{1,0:T(8,128)(2,1)S(1)}, u32[]{:S(2)}, u32[]{:S(2)}) collective-permute-start(bf16[256,256]{1,0:T(8,128)(2,1)S(1)} %get-tuple-element.61), channel_id=1, source_target_pairs={{0,64},{8,72},{16,80},{24,88},{32,96},{40,104},{48,112},{56,120},{... | collective-permute-start | bytes 393224 | tf_op jit(solution)/shard_map/ppermute | solution.py:361
  57.9 9.1 %collective-permute-start.14 = (bf16[256,256]{1,0:T(8,128)(2,1)S(1)}, bf16[256,256]{1,0:T(8,128)(2,1)S(1)}, u32[]{:S(2)}, u32[]{:S(2)}) collective-permute-start(bf16[256,256]{1,0:T(8,128)(2,1)S(1)} %get-tuple-element.62), channel_id=1, source_target_pairs={{0,192},{8,200},{16,208},{24,216},{32,224},{40,232},{48,240},{56,2... | collective-permute-start | bytes 393224 | tf_op jit(solution)/shard_map/ppermute | solution.py:361
  60.0 8.9 %collective-permute-start.15 = (bf16[256,256]{1,0:T(8,128)(2,1)S(1)}, bf16[256,256]{1,0:T(8,128)(2,1)S(1)}, u32[]{:S(2)}, u32[]{:S(2)}) collective-permute-start(bf16[256,256]{1,0:T(8,128)(2,1)S(1)} %get-tuple-element.63), channel_id=1, source_target_pairs={{0,128},{8,136},{16,144},{24,152},{32,160},{40,168},{48,176},{56,1... | collective-permute-start | bytes 393224 | tf_op jit(solution)/shard_map/ppermute | solution.py:361
  60.6 8.3 %collective-permute-start.16 = (bf16[256,256]{1,0:T(8,128)(2,1)S(1)}, bf16[256,256]{1,0:T(8,128)(2,1)S(1)}, u32[]{:S(2)}, u32[]{:S(2)}) collective-permute-start(bf16[256,256]{1,0:T(8,128)(2,1)S(1)} %get-tuple-element.64), channel_id=1, source_target_pairs={{0,72},{8,64},{16,88},{24,80},{32,104},{40,96},{48,120},{56,112},{... | collective-permute-start | bytes 393224 | tf_op jit(solution)/shard_map/ppermute | solution.py:361
  63.4 8.6 %collective-permute-start.17 = (bf16[256,256]{1,0:T(8,128)(2,1)S(1)}, bf16[256,256]{1,0:T(8,128)(2,1)S(1)}, u32[]{:S(2)}, u32[]{:S(2)}) collective-permute-start(bf16[256,256]{1,0:T(8,128)(2,1)S(1)} %get-tuple-element.65), channel_id=1, source_target_pairs={{0,200},{8,192},{16,216},{24,208},{32,232},{40,224},{48,248},{56,2... | collective-permute-start | bytes 393224 | tf_op jit(solution)/shard_map/ppermute | solution.py:361
  65.0 8.5 %collective-permute-start.18 = (bf16[256,256]{1,0:T(8,128)(2,1)S(1)}, bf16[256,256]{1,0:T(8,128)(2,1)S(1)}, u32[]{:S(2)}, u32[]{:S(2)}) collective-permute-start(bf16[256,256]{1,0:T(8,128)(2,1)S(1)} %get-tuple-element.66), channel_id=1, source_target_pairs={{0,136},{8,128},{16,152},{24,144},{32,168},{40,160},{48,184},{56,1... | collective-permute-start | bytes 393224 | tf_op jit(solution)/shard_map/ppermute | solution.py:361

commit v4 on v3

--- a/solution.py
+++ b/solution.py
@@ -41,15 +41,24 @@
 
 
 def positions(index, first_row):
-    rows = lax.broadcasted_iota(jnp.int32, (ROWS,), 0)
-    distance = index[:, 1] - (first_row + rows)
+    rows = lax.broadcasted_iota(jnp.int32, (1, ROWS), 1)
+    named = index.T[1:]
+    distance = named - (first_row + rows)
     distance = jnp.where(distance >= NBLK // 2, distance - NBLK, distance)
     distance = jnp.where(distance < -(NBLK // 2), distance + NBLK, distance)
-    return jnp.where(index[:, 1] >= 0, rows + distance, -NBLK)
+    return jnp.where(named >= 0, rows + distance, -NBLK)
+
+
+def as_column(values):
+    here = lax.broadcasted_iota(jnp.int32, (ROWS, ROWS), 0) == lax.broadcasted_iota(
+        jnp.int32, (ROWS, ROWS), 1
+    )
+    column = jnp.sum(jnp.where(here, values, 0), axis=1, keepdims=True)
+    return jnp.broadcast_to(column, (ROWS, BS))
 
 
 def neighbour(index_ref, row):
-    other = index_ref[row]
+    other = jnp.max(index_ref[pl.ds(row, 1), 0:1])
     live = other > -NBLK
     return jnp.where(live, other, row), live
 
@@ -86,8 +95,8 @@
 
 
 def inner_kernel(
-    s_index, v_index, c_hbm, s_hbm, v_hbm,
-    first, second, layer1, c_edge, s_edge, v_edge, v_mid, s_mid, s_out,
+    s_row, v_row, c_hbm, s_hbm, v_hbm,
+    s_index, v_index, first, second, layer1, c_edge, s_edge, v_edge, v_mid, s_mid, s_out,
     c, s, v, sems,
 ):
     def load(k, source, target, at, to, count):
@@ -108,6 +117,8 @@
         copies.append(load(len(copies), source, target, 56 - at, 8, 8))
     for copy in copies[:5]:
         copy.start()
+    s_index[...] = as_column(s_row[...])
+    v_index[...] = as_column(v_row[...])
     copies[0].wait()
 
     def one(row):
@@ -136,11 +147,12 @@
 
 def inner(s_index, v_index, c, s, v):
     stored = jax.ShapeDtypeStruct((16, 2, BS, BS), BF)
+    column = jax.ShapeDtypeStruct((ROWS, BS), jnp.int32)
     return pl.pallas_call(
         inner_kernel,
-        out_shape=[blocks_of(48), blocks_of(32), blocks_of(16), blocks_of(32)] + [stored] * 5,
-        in_specs=[SMEM, SMEM, HBM, HBM, HBM],
-        out_specs=[VMEM] * 9,
+        out_shape=[column] * 2 + [blocks_of(48), blocks_of(32), blocks_of(16), blocks_of(32)] + [stored] * 5,
+        in_specs=[VMEM, VMEM, HBM, HBM, HBM],
+        out_specs=[VMEM] * 11,
         scratch_shapes=[
             pltpu.VMEM((64, BS, BS), BF),
             pltpu.VMEM((48, 2, BS, BS), BF),
@@ -185,7 +197,7 @@
     return pl.pallas_call(
         kernel,
         out_shape=[blocks_of(8)] * 2,
-        in_specs=[SMEM] + [VMEM] * (len(operands) - 1),
+        in_specs=[VMEM] + [VMEM] * (len(operands) - 1),
         out_specs=[VMEM] * 2,
         scratch_shapes=[pltpu.VMEM((48, BS, BS), BF)],
         compiler_params=params(4),
@@ -218,7 +230,7 @@
     return pl.pallas_call(
         middle_kernel,
         out_shape=[blocks_of(8)] * 6,
-        in_specs=[SMEM, SMEM] + [VMEM] * 7,
+        in_specs=[VMEM, VMEM] + [VMEM] * 7,
         out_specs=[VMEM] * 6,
         scratch_shapes=[pltpu.VMEM((48, BS, BS), BF), pltpu.VMEM((48, BS, BS), BF)],
         compiler_params=params(4),
@@ -245,7 +257,7 @@
     return pl.pallas_call(
         outer_kernel,
         out_shape=blocks_of(16),
-        in_specs=[SMEM] + [VMEM] * 6,
+        in_specs=[VMEM] + [VMEM] * 6,
         out_specs=VMEM,
         scratch_shapes=[pltpu.VMEM((48, BS, BS), BF)],
         compiler_params=params(4),
@@ -282,7 +294,7 @@
     return pl.pallas_call(
         last_kernel,
         out_shape=[blocks_of(10)] * 4,
-        in_specs=[SMEM] + [VMEM] * 12,
+        in_specs=[VMEM] + [VMEM] * 12,
         out_specs=[VMEM] * 4,
         scratch_shapes=[pltpu.VMEM((48, BS, BS), BF)],
         compiler_params=params(4),
@@ -383,12 +395,13 @@
     c = coefficients.reshape(ROWS, BS, BS)
     s, v = metric_blocks, coulomb_blocks
     first_row = lax.axis_index("sec") * ROWS
-    s_index, v_index = positions(metric_index, first_row), positions(coulomb_index, first_row)
+    s_row, v_row = positions(metric_index, first_row), positions(coulomb_index, first_row)
     gaps = energy_gaps.reshape(1, BS)
 
     odd = lax.axis_index("sec") % 2 == 1
     c_far, c_near = halo(jnp.where(odd, c[56:], c[:8]), jnp.where(odd, c[:8], c[56:]))
-    first, second, layer1, c_edge, s_edge, v_edge, v_mid, s_mid, s_out = inner(s_index, v_index, c, s, v)
+    s_index, v_index, first, second, layer1, *edges_of = inner(s_row, v_row, c, s, v)
+    c_edge, s_edge, v_edge, v_mid, s_mid, s_out = edges_of
     f_sends = edges(first_edges_kernel, s_index, c_far, c_near, c_edge, s_edge)
     f_halos = halo(*f_sends)
     e_low, e_high, *inside = middle(s_index, v_index, *f_sends, first, second, layer1, v_mid, s_mid)

time: 74.9 us -> 73.3 us (0.979)
  Pallas kernels: 13.8 us -> 10.6 us
  starting transfers between devices: 31.6 us -> 32.7 us
    pallas_call x6, Pallas kernels: 11.9 us -> 8.73 us  [the longest x1 5.22 us: inner(): pl.pallas_call(inner_kernel, out_shape=[column] * 2 + [blocks_of(48), blo...]
    ppermute x3, starting transfers between devices: 10.5 us -> 11.6 us  [halo(): lax.ppermute(near, 'sec', near_pairs)]
  transfers between devices with their start and end apart: 19 -> 19, of which waited for: 8 -> 8; matrix products, arithmetic and copies ran while one was open for 1% -> 1% of each run, Pallas kernels for 13% -> 10%
where the time goes in v4:
time: 73.3 us; the launch traced here: 72.2 us
  starting transfers between devices  32.7 us (45%)
  waiting for transfers between devices  27 us (37%)
  Pallas kernels  10.6 us (14%)
  other arithmetic  1.77 us (2%)
    ppermute x6, waiting for transfers between devices, spread_y(): out[d] = lax.ppermute(parts[d], 'grp', pairs)  20.7 us
    ppermute x3, starting transfers between devices, halo(): lax.ppermute(near, 'sec', near_pairs)  11.6 us
    ppermute x7, starting transfers between devices, swap(): return lax.ppermute(value, 'grp', pairs)  10.8 us
    ppermute x6, starting transfers between devices, spread_y(): out[d] = lax.ppermute(parts[d], 'grp', pairs)  8.85 us
    ppermute x7, waiting for transfers between devices, swap(): return lax.ppermute(value, 'grp', pairs)  6.27 us
    pallas_call x1, Pallas kernels, inner(): pl.pallas_call(inner_kernel, out_shape=[column] * 2 + [blocks_of(48), blo...  5.22 us
    ppermute x3, starting transfers between devices, halo(): lax.ppermute(far, 'sec', far_pairs)  1.52 us
  transfers between devices with their start and end apart: 19, of which 8 were waited for; matrix products, arithmetic and copies ran while one was open for 1% of the time, Pallas kernels for 10%

profile of v4, /device:TPU:64, one launch (start us, length us, event | category | flops | bytes accessed | tf_op | source)
XLA Modules:
  0.0 72.2 jit_solution(4917676793238879585)
XLA Ops:
  0.0 1.1 %broadcast_select_fusion = (bf16[1024,128]{1,0:T(8,128)(2,1)S(1)}, bf16[1024,128]{1,0:T(8,128)(2,1)S(1)}) fusion(pred[]{:T(512)S(6)} %eq.5, bf16[8192,128]{1,0:T(8,128)(2,1)} %param.6), kind=kLoop, calls=%fused_computation | loop fusion | flops 262144 | bytes 1048577 | tf_op jit(solution)/shard_map/jit(_where)/select_n | solution.py:402
  1.2 4.6 %collective-permute-start.1 = (bf16[8,128,128]{2,1,0:T(8,128)(2,1)S(1)}, bf16[8,128,128]{2,1,0:T(8,128)(2,1)S(1)}, u32[]{:S(2)}, u32[]{:S(2)}) collective-permute-start(bf16[8,128,128]{2,1,0:T(8,128)(2,1)S(1)} %bitcast.8), channel_id=1, source_target_pairs={{0,1},{1,0},{2,3},{3,2},{4,5},{5,4},{6,7},{7,6},{8,9},{9,8},{10,11... | collective-permute-start | bytes 786440 | tf_op jit(solution)/shard_map/ppermute | solution.py:380
  5.8 0.7 compare_select_fusion.4
  6.5 5.2 %shard_map.64 = (s32[64,128]{1,0:T(8,128)S(1)}, s32[64,128]{1,0:T(8,128)S(1)}, bf16[48,128,128]{2,1,0:T(8,128)(2,1)S(1)}, bf16[32,128,128]{2,1,0:T(8,128)(2,1)S(...) custom-call(s32[1,64]{1,0:T(1,128)S(1)} %get-tuple-element.74.s_row,, ...), custom_call_target="tpu_custom_call" | custom-call | flops 805306368 | bytes 14680064 | tf_op jit(solution)/shard_map/pallas_call | solution.py:151
  12.3 1.0 %collective-permute-start.5 = (bf16[8,128,128]{2,1,0:T(8,128)(2,1)S(1)}, bf16[8,128,128]{2,1,0:T(8,128)(2,1)S(1)}, u32[]{:S(2)}, u32[]{:S(2)}) collective-permute-start(bf16[8,128,128]{2,1,0:T(8,128)(2,1)S(1)} %get-tuple-element.42.far.f_far), channel_id=1, source_target_pairs={{0,7},{1,2},{2,1},{3,4},{4,3},{5,6},{6,5},{7,0},{8,15},{9,10},{10,... | collective-permute-start | bytes 786440 | tf_op jit(solution)/shard_map/ppermute | solution.py:380
  13.3 3.6 %collective-permute-start.6 = (bf16[8,128,128]{2,1,0:T(8,128)(2,1)S(1)}, bf16[8,128,128]{2,1,0:T(8,128)(2,1)S(1)}, u32[]{:S(2)}, u32[]{:S(2)}) collective-permute-start(bf16[8,128,128]{2,1,0:T(8,128)(2,1)S(1)} %get-tuple-element.43.near.f_near), channel_id=1, source_target_pairs={{0,1},{1,0},{2,3},{3,2},{4,5},{5,4},{6,7},{7,6},{8,9},{9,8},{10,11... | collective-permute-start | bytes 786440 | tf_op jit(solution)/shard_map/ppermute | solution.py:380
  16.9 1.1 %shard_map.66 = (bf16[8,128,128]{2,1,0:T(8,128)(2,1)S(1)}, bf16[8,128,128]{2,1,0:T(8,128)(2,1)S(1)}, bf16[8,128,128]{2,1,0:T(8,128)(2,1)S(1)}, bf16[8,128,128]{2...) custom-call(s32[64,128]{1,0:T(8,128)S(1)} %get-tuple-element.38.index.s_index, ...), custom_call_target="tpu_custom_call" | custom-call | flops 268435456 | bytes 8388608 | tf_op jit(solution)/shard_map/pallas_call | solution.py:230
  18.0 1.7 %collective-permute-start.2 = (bf16[8,128,128]{2,1,0:T(8,128)(2,1)S(1)}, bf16[8,128,128]{2,1,0:T(8,128)(2,1)S(1)}, u32[]{:S(2)}, u32[]{:S(2)}) collective-permute-start(bf16[8,128,128]{2,1,0:T(8,128)(2,1)S(1)} %get-tuple-element.50), channel_id=1, source_target_pairs={{0,16},{8,24},{16,32},{24,40},{32,48},{40,56},{48,0},{56,8},{64,80... | collective-permute-start | bytes 786440 | tf_op jit(solution)/shard_map/ppermute | solution.py:390
  19.6 1.7 %collective-permute-start.3 = (bf16[8,128,128]{2,1,0:T(8,128)(2,1)S(1)}, bf16[8,128,128]{2,1,0:T(8,128)(2,1)S(1)}, u32[]{:S(2)}, u32[]{:S(2)}) collective-permute-start(bf16[8,128,128]{2,1,0:T(8,128)(2,1)S(1)} %get-tuple-element.51), channel_id=1, source_target_pairs={{0,48},{8,56},{16,0},{24,8},{32,16},{40,24},{48,32},{56,40},{64,11... | collective-permute-start | bytes 786440 | tf_op jit(solution)/shard_map/ppermute | solution.py:390
  21.3 2.0 %collective-permute-start.4 = (bf16[8,128,128]{2,1,0:T(8,128)(2,1)S(1)}, bf16[8,128,128]{2,1,0:T(8,128)(2,1)S(1)}, u32[]{:S(2)}, u32[]{:S(2)}) collective-permute-start(bf16[8,128,128]{2,1,0:T(8,128)(2,1)S(1)} %get-tuple-element.52), channel_id=1, source_target_pairs={{0,32},{8,40},{16,48},{24,56},{32,0},{40,8},{48,16},{56,24},{64,96... | collective-permute-start | bytes 786440 | tf_op jit(solution)/shard_map/ppermute | solution.py:390
  23.3 0.6 shard_map.67
  24.3 3.4 %collective-permute-start.8 = (bf16[8,128,128]{2,1,0:T(8,128)(2,1)S(1)}, bf16[8,128,128]{2,1,0:T(8,128)(2,1)S(1)}, u32[]{:S(2)}, u32[]{:S(2)}) collective-permute-start(bf16[8,128,128]{2,1,0:T(8,128)(2,1)S(1)} %get-tuple-element.56.near), channel_id=1, source_target_pairs={{0,1},{1,0},{2,3},{3,2},{4,5},{5,4},{6,7},{7,6},{8,9},{9,8},{10,11... | collective-permute-start | bytes 786440 | tf_op jit(solution)/shard_map/ppermute | solution.py:380
  27.7 0.6 shard_map.68.layer3
  28.4 4.2 %collective-permute-done.3.after2.refs_2_ = bf16[8,128,128]{2,1,0:T(8,128)(2,1)S(1)} collective-permute-done((bf16[8,128,128]{2,1,0:T(8,128)(2,1)S(1)}, bf16[8,128,128]{2,1,0:T(8,128)(2,1)S(1)}, u32[]{:S(2)}, u32[]{:S(2)}) %collective-permute-start.3) | collective-permute-done | bytes 262176 | tf_op jit(solution)/shard_map/ppermute | solution.py:390
  32.5 1.8 %collective-permute-done.4.after3.refs_3_ = bf16[8,128,128]{2,1,0:T(8,128)(2,1)S(1)} collective-permute-done((bf16[8,128,128]{2,1,0:T(8,128)(2,1)S(1)}, bf16[8,128,128]{2,1,0:T(8,128)(2,1)S(1)}, u32[]{:S(2)}, u32[]{:S(2)}) %collective-permute-start.4) | collective-permute-done | bytes 262176 | tf_op jit(solution)/shard_map/ppermute | solution.py:390
  34.4 0.6 shard_map.69
  35.0 1.2 %collective-permute-start.9 = (bf16[10,128,128]{2,1,0:T(8,128)(2,1)S(1)}, bf16[10,128,128]{2,1,0:T(8,128)(2,1)S(1)}, u32[]{:S(2)}, u32[]{:S(2)}) collective-permute-start(bf16[10,128,128]{2,1,0:T(8,128)(2,1)S(1)} %get-tuple-element.60), channel_id=1, source_target_pairs={{0,16},{8,24},{16,32},{24,40},{32,48},{40,56},{48,0},{56,8},{64,80... | collective-permute-start | bytes 983048 | tf_op jit(solution)/shard_map/ppermute | solution.py:390
  36.2 2.1 %collective-permute-start.10 = (bf16[10,128,128]{2,1,0:T(8,128)(2,1)S(1)}, bf16[10,128,128]{2,1,0:T(8,128)(2,1)S(1)}, u32[]{:S(2)}, u32[]{:S(2)}) collective-permute-start(bf16[10,128,128]{2,1,0:T(8,128)(2,1)S(1)} %get-tuple-element.61), channel_id=1, source_target_pairs={{0,48},{8,56},{16,0},{24,8},{32,16},{40,24},{48,32},{56,40},{64,11... | collective-permute-start | bytes 983048 | tf_op jit(solution)/shard_map/ppermute | solution.py:390
  38.6 6.5 %collective-permute-done.9.refs_5_ = bf16[10,128,128]{2,1,0:T(8,128)(2,1)S(1)} collective-permute-done((bf16[10,128,128]{2,1,0:T(8,128)(2,1)S(1)}, bf16[10,128,128]{2,1,0:T(8,128)(2,1)S(1)}, u32[]{:S(2)}, u32[]{:S(2)}) %collective-permute-start.9) | collective-permute-done | bytes 327712 | tf_op jit(solution)/shard_map/ppermute | solution.py:390
  45.1 6.6 %collective-permute-done.10.refs_6_ = bf16[10,128,128]{2,1,0:T(8,128)(2,1)S(1)} collective-permute-done((bf16[10,128,128]{2,1,0:T(8,128)(2,1)S(1)}, bf16[10,128,128]{2,1,0:T(8,128)(2,1)S(1)}, u32[]{:S(2)}, u32[]{:S(2)}) %collective-permute-start.10) | collective-permute-done | bytes 327712 | tf_op jit(solution)/shard_map/ppermute | solution.py:390
  51.6 1.6 %collective-permute-done.11.refs_7_ = bf16[10,128,128]{2,1,0:T(8,128)(2,1)S(1)} collective-permute-done((bf16[10,128,128]{2,1,0:T(8,128)(2,1)S(1)}, bf16[10,128,128]{2,1,0:T(8,128)(2,1)S(1)}, u32[]{:S(2)}, u32[]{:S(2)}) %collective-permute-start.11) | collective-permute-done | bytes 327712 | tf_op jit(solution)/shard_map/ppermute | solution.py:390
  53.2 1.1 %shard_map.70 = (f32[256,256]{1,0:T(8,128)S(1)}, bf16[256,256]{1,0:T(8,128)(2,1)S(1)}, bf16[256,256]{1,0:T(8,128)(2,1)S(1)}, bf16[256,256]{1,0:T(8,128)(2,1)S(1)...) custom-call(bf16[8,128,128]{2,1,0:T(8,128)(2,1)S(1)} %get-tuple-elem, ...), custom_call_target="tpu_custom_call" | custom-call | flops 536870912 | bytes 8388608 | tf_op jit(solution)/shard_map/pallas_call | solution.py:336
  54.4 1.6 %collective-permute-start.13 = (bf16[256,256]{1,0:T(8,128)(2,1)S(1)}, bf16[256,256]{1,0:T(8,128)(2,1)S(1)}, u32[]{:S(2)}, u32[]{:S(2)}) collective-permute-start(bf16[256,256]{1,0:T(8,128)(2,1)S(1)} %get-tuple-element.65), channel_id=1, source_target_pairs={{0,64},{8,72},{16,80},{24,88},{32,96},{40,104},{48,112},{56,120},{... | collective-permute-start | bytes 393224 | tf_op jit(solution)/shard_map/ppermute | solution.py:373
  56.0 2.1 %collective-permute-start.14 = (bf16[256,256]{1,0:T(8,128)(2,1)S(1)}, bf16[256,256]{1,0:T(8,128)(2,1)S(1)}, u32[]{:S(2)}, u32[]{:S(2)}) collective-permute-start(bf16[256,256]{1,0:T(8,128)(2,1)S(1)} %get-tuple-element.66), channel_id=1, source_target_pairs={{0,192},{8,200},{16,208},{24,216},{32,224},{40,232},{48,240},{56,2... | collective-permute-start | bytes 393224 | tf_op jit(solution)/shard_map/ppermute | solution.py:373
  58.1 0.6 collective-permute-start.15
  58.8 2.7 %collective-permute-start.16 = (bf16[256,256]{1,0:T(8,128)(2,1)S(1)}, bf16[256,256]{1,0:T(8,128)(2,1)S(1)}, u32[]{:S(2)}, u32[]{:S(2)}) collective-permute-start(bf16[256,256]{1,0:T(8,128)(2,1)S(1)} %get-tuple-element.68), channel_id=1, source_target_pairs={{0,72},{8,64},{16,88},{24,80},{32,104},{40,96},{48,120},{56,112},{... | collective-permute-start | bytes 393224 | tf_op jit(solution)/shard_map/ppermute | solution.py:373
  61.5 1.6 %collective-permute-start.17 = (bf16[256,256]{1,0:T(8,128)(2,1)S(1)}, bf16[256,256]{1,0:T(8,128)(2,1)S(1)}, u32[]{:S(2)}, u32[]{:S(2)}) collective-permute-start(bf16[256,256]{1,0:T(8,128)(2,1)S(1)} %get-tuple-element.69), channel_id=1, source_target_pairs={{0,200},{8,192},{16,216},{24,208},{32,232},{40,224},{48,248},{56,2... | collective-permute-start | bytes 393224 | tf_op jit(solution)/shard_map/ppermute | solution.py:373
  63.1 2.0 %collective-permute-start.18 = (bf16[256,256]{1,0:T(8,128)(2,1)S(1)}, bf16[256,256]{1,0:T(8,128)(2,1)S(1)}, u32[]{:S(2)}, u32[]{:S(2)}) collective-permute-start(bf16[256,256]{1,0:T(8,128)(2,1)S(1)} %get-tuple-element.70), channel_id=1, source_target_pairs={{0,136},{8,128},{16,152},{24,144},{32,168},{40,160},{48,184},{56,1... | collective-permute-start | bytes 393224 | tf_op jit(solution)/shard_map/ppermute | solution.py:373
  65.1 3.7 %collective-permute-done.15.refs_4_ = bf16[256,256]{1,0:T(8,128)(2,1)S(1)} collective-permute-done((bf16[256,256]{1,0:T(8,128)(2,1)S(1)}, bf16[256,256]{1,0:T(8,128)(2,1)S(1)}, u32[]{:S(2)}, u32[]{:S(2)}) %collective-permute-start.15) | collective-permute-done | bytes 131104 | tf_op jit(solution)/shard_map/ppermute | solution.py:373
  68.9 1.1 %collective-permute-done.17.refs_6_ = bf16[256,256]{1,0:T(8,128)(2,1)S(1)} collective-permute-done((bf16[256,256]{1,0:T(8,128)(2,1)S(1)}, bf16[256,256]{1,0:T(8,128)(2,1)S(1)}, u32[]{:S(2)}, u32[]{:S(2)}) %collective-permute-start.17) | collective-permute-done | bytes 131104 | tf_op jit(solution)/shard_map/ppermute | solution.py:373
  69.9 1.5 %collective-permute-done.18.refs_7_ = bf16[256,256]{1,0:T(8,128)(2,1)S(1)} collective-permute-done((bf16[256,256]{1,0:T(8,128)(2,1)S(1)}, bf16[256,256]{1,0:T(8,128)(2,1)S(1)}, u32[]{:S(2)}, u32[]{:S(2)}) %collective-permute-start.18) | collective-permute-done | bytes 131104 | tf_op jit(solution)/shard_map/ppermute | solution.py:373
  71.4 0.8 %shard_map.71 = f32[1,256,256]{2,1,0:T(8,128)} custom-call(f32[256,256]{1,0:T(8,128)S(1)} %get-tuple-element.63.refs_0_, bf16[256,256]{1,0:T(8,128)(2,1)S(1)} %collective-permute-done.12.refs_1_, bf16[256,256]{1,0:T(8,128)(2,1)S(1)} %collective-permute-done.13.refs_2_, bf16[256,256]{1,0:T(8,128)(2,1)S(1)} %collective-permute-done.14.refs_3_, ...), custom_call_target="tpu_custom_call" | custom-call | flops 524288 | bytes 1048576 | tf_op jit(solution)/shard_map/pallas_call | solution.py:357
  (18 shorter events, 1.5 us)
Async XLA Ops:
  1.1 10.6 %collective-permute-start = (bf16[8,128,128]{2,1,0:T(8,128)(2,1)S(1)}, bf16[8,128,128]{2,1,0:T(8,128)(2,1)S(1)}, u32[]{:S(2)}, u32[]{:S(2)}) collective-permute-start(bf16[8,128,128]{2,1,0:T(8,128)(2,1)S(1)} %bitcast.9), channel_id=1, source_target_pairs={{0,7},{1,2},{2,1},{3,4},{4,3},{5,6},{6,5},{7,0},{8,15},{9,10},{10,... | collective-permute-start | bytes 786440 | tf_op jit(solution)/shard_map/ppermute | solution.py:380
  1.2 10.5 %collective-permute-start.1 = (bf16[8,128,128]{2,1,0:T(8,128)(2,1)S(1)}, bf16[8,128,128]{2,1,0:T(8,128)(2,1)S(1)}, u32[]{:S(2)}, u32[]{:S(2)}) collective-permute-start(bf16[8,128,128]{2,1,0:T(8,128)(2,1)S(1)} %bitcast.8), channel_id=1, source_target_pairs={{0,1},{1,0},{2,3},{3,2},{4,5},{5,4},{6,7},{7,6},{8,9},{9,8},{10,11... | collective-permute-start | bytes 786440 | tf_op jit(solution)/shard_map/ppermute | solution.py:380
  12.3 11.0 %collective-permute-start.5 = (bf16[8,128,128]{2,1,0:T(8,128)(2,1)S(1)}, bf16[8,128,128]{2,1,0:T(8,128)(2,1)S(1)}, u32[]{:S(2)}, u32[]{:S(2)}) collective-permute-start(bf16[8,128,128]{2,1,0:T(8,128)(2,1)S(1)} %get-tuple-element.42.far.f_far), channel_id=1, source_target_pairs={{0,7},{1,2},{2,1},{3,4},{4,3},{5,6},{6,5},{7,0},{8,15},{9,10},{10,... | collective-permute-start | bytes 786440 | tf_op jit(solution)/shard_map/ppermute | solution.py:380
  13.3 10.0 %collective-permute-start.6 = (bf16[8,128,128]{2,1,0:T(8,128)(2,1)S(1)}, bf16[8,128,128]{2,1,0:T(8,128)(2,1)S(1)}, u32[]{:S(2)}, u32[]{:S(2)}) collective-permute-start(bf16[8,128,128]{2,1,0:T(8,128)(2,1)S(1)} %get-tuple-element.43.near.f_near), channel_id=1, source_target_pairs={{0,1},{1,0},{2,3},{3,2},{4,5},{5,4},{6,7},{7,6},{8,9},{9,8},{10,11... | collective-permute-start | bytes 786440 | tf_op jit(solution)/shard_map/ppermute | solution.py:380
  18.0 10.4 %collective-permute-start.2 = (bf16[8,128,128]{2,1,0:T(8,128)(2,1)S(1)}, bf16[8,128,128]{2,1,0:T(8,128)(2,1)S(1)}, u32[]{:S(2)}, u32[]{:S(2)}) collective-permute-start(bf16[8,128,128]{2,1,0:T(8,128)(2,1)S(1)} %get-tuple-element.50), channel_id=1, source_target_pairs={{0,16},{8,24},{16,32},{24,40},{32,48},{40,56},{48,0},{56,8},{64,80... | collective-permute-start | bytes 786440 | tf_op jit(solution)/shard_map/ppermute | solution.py:390
  19.6 12.9 %collective-permute-start.3 = (bf16[8,128,128]{2,1,0:T(8,128)(2,1)S(1)}, bf16[8,128,128]{2,1,0:T(8,128)(2,1)S(1)}, u32[]{:S(2)}, u32[]{:S(2)}) collective-permute-start(bf16[8,128,128]{2,1,0:T(8,128)(2,1)S(1)} %get-tuple-element.51), channel_id=1, source_target_pairs={{0,48},{8,56},{16,0},{24,8},{32,16},{40,24},{48,32},{56,40},{64,11... | collective-permute-start | bytes 786440 | tf_op jit(solution)/shard_map/ppermute | solution.py:390
  21.3 13.0 %collective-permute-start.4 = (bf16[8,128,128]{2,1,0:T(8,128)(2,1)S(1)}, bf16[8,128,128]{2,1,0:T(8,128)(2,1)S(1)}, u32[]{:S(2)}, u32[]{:S(2)}) collective-permute-start(bf16[8,128,128]{2,1,0:T(8,128)(2,1)S(1)} %get-tuple-element.52), channel_id=1, source_target_pairs={{0,32},{8,40},{16,48},{24,56},{32,0},{40,8},{48,16},{56,24},{64,96... | collective-permute-start | bytes 786440 | tf_op jit(solution)/shard_map/ppermute | solution.py:390
  23.9 10.5 %copy-start = (f32[128]{0:T(128)S(1)}, f32[128]{0:T(128)}, u32[]{:S(2)}) copy-start(f32[128]{0:T(128)} %param.7) | copy-start | bytes 1540
  23.9 10.5 %collective-permute-start.7 = (bf16[8,128,128]{2,1,0:T(8,128)(2,1)S(1)}, bf16[8,128,128]{2,1,0:T(8,128)(2,1)S(1)}, u32[]{:S(2)}, u32[]{:S(2)}) collective-permute-start(bf16[8,128,128]{2,1,0:T(8,128)(2,1)S(1)} %get-tuple-element.55.far), channel_id=1, source_target_pairs={{0,7},{1,2},{2,1},{3,4},{4,3},{5,6},{6,5},{7,0},{8,15},{9,10},{10,... | collective-permute-start | bytes 786440 | tf_op jit(solution)/shard_map/ppermute | solution.py:380
  24.3 10.0 %collective-permute-start.8 = (bf16[8,128,128]{2,1,0:T(8,128)(2,1)S(1)}, bf16[8,128,128]{2,1,0:T(8,128)(2,1)S(1)}, u32[]{:S(2)}, u32[]{:S(2)}) collective-permute-start(bf16[8,128,128]{2,1,0:T(8,128)(2,1)S(1)} %get-tuple-element.56.near), channel_id=1, source_target_pairs={{0,1},{1,0},{2,3},{3,2},{4,5},{5,4},{6,7},{7,6},{8,9},{9,8},{10,11... | collective-permute-start | bytes 786440 | tf_op jit(solution)/shard_map/ppermute | solution.py:380
  35.0 10.1 %collective-permute-start.9 = (bf16[10,128,128]{2,1,0:T(8,128)(2,1)S(1)}, bf16[10,128,128]{2,1,0:T(8,128)(2,1)S(1)}, u32[]{:S(2)}, u32[]{:S(2)}) collective-permute-start(bf16[10,128,128]{2,1,0:T(8,128)(2,1)S(1)} %get-tuple-element.60), channel_id=1, source_target_pairs={{0,16},{8,24},{16,32},{24,40},{32,48},{40,56},{48,0},{56,8},{64,80... | collective-permute-start | bytes 983048 | tf_op jit(solution)/shard_map/ppermute | solution.py:390
  36.2 15.4 %collective-permute-start.10 = (bf16[10,128,128]{2,1,0:T(8,128)(2,1)S(1)}, bf16[10,128,128]{2,1,0:T(8,128)(2,1)S(1)}, u32[]{:S(2)}, u32[]{:S(2)}) collective-permute-start(bf16[10,128,128]{2,1,0:T(8,128)(2,1)S(1)} %get-tuple-element.61), channel_id=1, source_target_pairs={{0,48},{8,56},{16,0},{24,8},{32,16},{40,24},{48,32},{56,40},{64,11... | collective-permute-start | bytes 983048 | tf_op jit(solution)/shard_map/ppermute | solution.py:390
  38.3 14.9 %collective-permute-start.11 = (bf16[10,128,128]{2,1,0:T(8,128)(2,1)S(1)}, bf16[10,128,128]{2,1,0:T(8,128)(2,1)S(1)}, u32[]{:S(2)}, u32[]{:S(2)}) collective-permute-start(bf16[10,128,128]{2,1,0:T(8,128)(2,1)S(1)} %get-tuple-element.62), channel_id=1, source_target_pairs={{0,32},{8,40},{16,48},{24,56},{32,0},{40,8},{48,16},{56,24},{64,96... | collective-permute-start | bytes 983048 | tf_op jit(solution)/shard_map/ppermute | solution.py:390
  54.3 7.1 %collective-permute-start.12 = (bf16[256,256]{1,0:T(8,128)(2,1)S(1)}, bf16[256,256]{1,0:T(8,128)(2,1)S(1)}, u32[]{:S(2)}, u32[]{:S(2)}) collective-permute-start(bf16[256,256]{1,0:T(8,128)(2,1)S(1)} %get-tuple-element.64), channel_id=1, source_target_pairs={{0,8},{8,0},{16,24},{24,16},{32,40},{40,32},{48,56},{56,48},{64,72... | collective-permute-start | bytes 393224 | tf_op jit(solution)/shard_map/ppermute | solution.py:373
  54.4 8.7 %collective-permute-start.13 = (bf16[256,256]{1,0:T(8,128)(2,1)S(1)}, bf16[256,256]{1,0:T(8,128)(2,1)S(1)}, u32[]{:S(2)}, u32[]{:S(2)}) collective-permute-start(bf16[256,256]{1,0:T(8,128)(2,1)S(1)} %get-tuple-element.65), channel_id=1, source_target_pairs={{0,64},{8,72},{16,80},{24,88},{32,96},{40,104},{48,112},{56,120},{... | collective-permute-start | bytes 393224 | tf_op jit(solution)/shard_map/ppermute | solution.py:373
  56.0 9.1 %collective-permute-start.14 = (bf16[256,256]{1,0:T(8,128)(2,1)S(1)}, bf16[256,256]{1,0:T(8,128)(2,1)S(1)}, u32[]{:S(2)}, u32[]{:S(2)}) collective-permute-start(bf16[256,256]{1,0:T(8,128)(2,1)S(1)} %get-tuple-element.66), channel_id=1, source_target_pairs={{0,192},{8,200},{16,208},{24,216},{32,224},{40,232},{48,240},{56,2... | collective-permute-start | bytes 393224 | tf_op jit(solution)/shard_map/ppermute | solution.py:373
  58.1 10.7 %collective-permute-start.15 = (bf16[256,256]{1,0:T(8,128)(2,1)S(1)}, bf16[256,256]{1,0:T(8,128)(2,1)S(1)}, u32[]{:S(2)}, u32[]{:S(2)}) collective-permute-start(bf16[256,256]{1,0:T(8,128)(2,1)S(1)} %get-tuple-element.67), channel_id=1, source_target_pairs={{0,128},{8,136},{16,144},{24,152},{32,160},{40,168},{48,176},{56,1... | collective-permute-start | bytes 393224 | tf_op jit(solution)/shard_map/ppermute | solution.py:373
  58.8 10.1 %collective-permute-start.16 = (bf16[256,256]{1,0:T(8,128)(2,1)S(1)}, bf16[256,256]{1,0:T(8,128)(2,1)S(1)}, u32[]{:S(2)}, u32[]{:S(2)}) collective-permute-start(bf16[256,256]{1,0:T(8,128)(2,1)S(1)} %get-tuple-element.68), channel_id=1, source_target_pairs={{0,72},{8,64},{16,88},{24,80},{32,104},{40,96},{48,120},{56,112},{... | collective-permute-start | bytes 393224 | tf_op jit(solution)/shard_map/ppermute | solution.py:373
  61.5 8.4 %collective-permute-start.17 = (bf16[256,256]{1,0:T(8,128)(2,1)S(1)}, bf16[256,256]{1,0:T(8,128)(2,1)S(1)}, u32[]{:S(2)}, u32[]{:S(2)}) collective-permute-start(bf16[256,256]{1,0:T(8,128)(2,1)S(1)} %get-tuple-element.69), channel_id=1, source_target_pairs={{0,200},{8,192},{16,216},{24,208},{32,232},{40,224},{48,248},{56,2... | collective-permute-start | bytes 393224 | tf_op jit(solution)/shard_map/ppermute | solution.py:373
  63.1 8.3 %collective-permute-start.18 = (bf16[256,256]{1,0:T(8,128)(2,1)S(1)}, bf16[256,256]{1,0:T(8,128)(2,1)S(1)}, u32[]{:S(2)}, u32[]{:S(2)}) collective-permute-start(bf16[256,256]{1,0:T(8,128)(2,1)S(1)} %get-tuple-element.70), channel_id=1, source_target_pairs={{0,136},{8,128},{16,152},{24,144},{32,168},{40,160},{48,184},{56,1... | collective-permute-start | bytes 393224 | tf_op jit(solution)/shard_map/ppermute | solution.py:373

commit v5 on v4

--- a/solution.py
+++ b/solution.py
@@ -13,6 +13,8 @@
 NX, NY, NZ = 4, 4, 2
 
 frequency_sq = 1.0
+
+DIRECT = ((1, 0), (3, 0), (1, 1), (3, 1))
 
 VMEM = pl.BlockSpec(memory_space=pltpu.VMEM)
 SMEM = pl.BlockSpec(memory_space=pltpu.SMEM)
@@ -302,66 +304,86 @@
     )(*operands)
 
 
+def chunk(inside, outside, to, half):
+    _, y, _ = coords()
+    near = jnp.where(to == 2, 0, jnp.where(to == 1, 1, jnp.where(to == 3, 2, 3)))
+    away = jnp.where(to == 1, 0, jnp.where(to == 2, 1, jnp.where(to == 0, 2, 3)))
+    layer = jnp.where(y < 2, near, away)
+    rows = pl.ds(4 * (layer % 2) + 2 * half, 2)
+    left = [
+        jnp.where(layer < 2, inner_part[rows], outer_part[rows]).reshape(QC, BS)
+        for inner_part, outer_part in zip(inside, outside)
+    ]
+    right = [part[8:10].reshape(QC, BS) for part in outside]
+    return lax.dot_general(
+        jnp.concatenate(left, axis=1),
+        jnp.concatenate(right, axis=1),
+        (((1,), (1,)), ((), ())),
+        preferred_element_type=F32,
+    )
+
+
+def across_kernel(*refs):
+    inside, outside, out = refs[:4], refs[4:8], refs[8]
+    x, _, z = coords()
+    out[0] = chunk(inside, outside, x, z ^ 1).astype(BF)
+    out[1] = chunk(inside, outside, x ^ 2, z ^ 1).astype(BF)
+
+
 def product_kernel(*refs):
     inside, outside = refs[:4], refs[4:8]
-    own, outs, b, w = refs[8], refs[9:16], refs[16], refs[17]
-    for source in range(4):
-        lanes = slice(source * BS, (source + 1) * BS)
-        for k in range(2):
-            b[k, :, lanes] = inside[source][4 * k : 4 * k + 4].reshape(4 * BS, BS)
-            b[2 + k, :, lanes] = outside[source][4 * k : 4 * k + 4].reshape(4 * BS, BS)
-        w[:, lanes] = outside[source][8:10].reshape(QC, BS)
-    x, y, z = coords()
-    for step in range(NX):
-        to = x ^ step
-        near = jnp.where(to == 2, 0, jnp.where(to == 1, 1, jnp.where(to == 3, 2, 3)))
-        away = jnp.where(to == 1, 0, jnp.where(to == 2, 1, jnp.where(to == 0, 2, 3)))
-        layer = jnp.where(y < 2, near, away)
-        for flip in range(NZ):
-            half = z ^ flip
-            tile = lax.dot_general(
-                b[layer, pl.ds(pl.multiple_of(half * QC, QC), QC), :],
-                w[...],
-                (((1,), (1,)), ((), ())),
-                preferred_element_type=F32,
-            )
-            if step == 0 and flip == 0:
-                own[...] = tile
-            else:
-                outs[step * NZ + flip - 1][...] = tile.astype(BF)
-
-
-def product(*operands):
-    tile = jax.ShapeDtypeStruct((QC, QC), BF)
-    return pl.pallas_call(
-        product_kernel,
-        out_shape=[jax.ShapeDtypeStruct((QC, QC), F32)] + [tile] * 7,
-        in_specs=[VMEM] * 8,
-        out_specs=[VMEM] * 8,
-        scratch_shapes=[pltpu.VMEM((4, 4 * BS, 4 * BS), BF), pltpu.VMEM((QC, 4 * BS), BF)],
+    own, passed, outs = refs[9], refs[10], refs[11:]
+    x, _, z = coords()
+    for out, (step, flip) in zip(outs, DIRECT):
+        out[...] = chunk(inside, outside, x ^ step, z ^ flip).astype(BF)
+    passed[...] = chunk(inside, outside, x ^ 2, z)
+    own[...] = chunk(inside, outside, x, z)
+
+
+def product(kernel, tiles, out_shape, *operands):
+    return pl.pallas_call(
+        kernel,
+        out_shape=out_shape,
+        in_specs=[VMEM] * len(operands),
+        out_specs=jax.tree.map(lambda _: VMEM, out_shape),
         compiler_params=params(8),
         cost_estimate=pl.CostEstimate(
-            flops=2 * 2048 * 512 * 256, bytes_accessed=8 * 2**20, transcendentals=0
+            flops=2 * tiles * QC * QC * 512, bytes_accessed=2**20 * tiles, transcendentals=0
         ),
     )(*operands)
 
 
-def add_kernel(*refs):
-    total = refs[0][...]
-    for ref in refs[1:8]:
+def pass_kernel(passed, arrived, out):
+    out[...] = (passed[...] + arrived[1].astype(F32)).astype(BF)
+
+
+def pass_on(passed, arrived):
+    return pl.pallas_call(
+        pass_kernel,
+        out_shape=jax.ShapeDtypeStruct((QC, QC), BF),
+        in_specs=[VMEM] * 2,
+        out_specs=VMEM,
+        compiler_params=params(4),
+        cost_estimate=pl.CostEstimate(flops=QC * QC, bytes_accessed=2**19, transcendentals=0),
+    )(passed, arrived)
+
+
+def add_kernel(own, arrived, *refs):
+    total = own[...] + arrived[0].astype(F32)
+    for ref in refs[:-1]:
         total += ref[...].astype(F32)
-    refs[8][0] = total
-
-
-def add_up(own, others):
+    refs[-1][0] = total
+
+
+def add_up(*operands):
     return pl.pallas_call(
         add_kernel,
         out_shape=jax.ShapeDtypeStruct((1, QC, QC), F32),
-        in_specs=[VMEM] * 8,
+        in_specs=[VMEM] * len(operands),
         out_specs=VMEM,
-        compiler_params=params(8),
+        compiler_params=params(4),
         cost_estimate=pl.CostEstimate(flops=8 * QC * QC, bytes_accessed=2**20, transcendentals=0),
-    )(own, *others)
+    )(*operands)
 
 
 def swap(value, dx, dy, dz):
@@ -413,9 +435,16 @@
         s_index, *e_halos, *e_sends, e_low, e_high, s_edge, gaps, layer3, *inside[1:]
     )
     outside = spread_y(outside)
-    own, *others = product(*inside, *outside)
-    sent = [swap(others[step * NZ + flip - 1], step, 0, flip) for step, flip in ((0, 1), (1, 0), (3, 0), (2, 0), (1, 1), (3, 1), (2, 1))]
-    return add_up(own, sent)
+    tile = jax.ShapeDtypeStruct((QC, QC), BF)
+    whole = jax.ShapeDtypeStruct((QC, QC), F32)
+    across = product(across_kernel, 2, jax.ShapeDtypeStruct((2, QC, QC), BF), *inside, *outside)
+    arrived = swap(across, 0, 0, 1)
+    own, passed, *direct = product(
+        product_kernel, 6, [whole] * 2 + [tile] * len(DIRECT), *inside, *outside, across
+    )
+    direct = [swap(part, step, 0, flip) for part, (step, flip) in zip(direct, DIRECT)]
+    last_tile = swap(pass_on(passed, arrived), 2, 0, 0)
+    return add_up(own, arrived, *direct, last_tile)
 
 
 def solution(mesh):

time: 73.3 us -> 71.6 us (0.977); the launches traced: 72.2 us -> 71.3 us
  starting transfers between devices: 32.7 us -> 31.4 us
    ppermute x7 -> x6, starting transfers between devices: 10.8 us -> 9.46 us  [swap(): return lax.ppermute(value, 'grp', pairs)]
    ppermute x7 -> x6, waiting for transfers between devices: 6.27 us -> 6.77 us  [swap(): return lax.ppermute(value, 'grp', pairs)]
  transfers between devices with their start and end apart: 19 -> 18, of which waited for: 8 -> 9; matrix products, arithmetic and copies ran while one was open for 1% -> 1% of each run, Pallas kernels for 10% -> 11%
where the time goes in v5:
time: 71.6 us; the launch traced here: 71.3 us
  starting transfers between devices  31.4 us (44%)
  waiting for transfers between devices  27.5 us (38%)
  Pallas kernels  10.5 us (15%)
  other arithmetic  1.77 us (2%)
    ppermute x6, waiting for transfers between devices, spread_y(): out[d] = lax.ppermute(parts[d], 'grp', pairs)  20.7 us
    ppermute x3, starting transfers between devices, halo(): lax.ppermute(near, 'sec', near_pairs)  11.6 us
    ppermute x6, starting transfers between devices, swap(): return lax.ppermute(value, 'grp', pairs)  9.46 us
    ppermute x6, starting transfers between devices, spread_y(): out[d] = lax.ppermute(parts[d], 'grp', pairs)  8.85 us
    ppermute x6, waiting for transfers between devices, swap(): return lax.ppermute(value, 'grp', pairs)  6.77 us
    pallas_call x1, Pallas kernels, inner(): pl.pallas_call(inner_kernel, out_shape=[column] * 2 + [blocks_of(48), blo...  5.22 us
    ppermute x3, starting transfers between devices, halo(): lax.ppermute(far, 'sec', far_pairs)  1.52 us
  transfers between devices with their start and end apart: 18, of which 9 were waited for; matrix products, arithmetic and copies ran while one was open for 1% of the time, Pallas kernels for 11%

profile of v5, /device:TPU:64, one launch (start us, length us, event | category | flops | bytes accessed | tf_op | source)
XLA Modules:
  0.0 71.3 jit_solution(1974392666559720224)
XLA Ops:
  0.0 1.1 %broadcast_select_fusion = (bf16[1024,128]{1,0:T(8,128)(2,1)S(1)}, bf16[1024,128]{1,0:T(8,128)(2,1)S(1)}) fusion(pred[]{:T(512)S(6)} %eq.5, bf16[8192,128]{1,0:T(8,128)(2,1)} %param.6), kind=kLoop, calls=%fused_computation | loop fusion | flops 262144 | bytes 1048577 | tf_op jit(solution)/shard_map/jit(_where)/select_n | solution.py:424
  1.2 4.6 %collective-permute-start.1 = (bf16[8,128,128]{2,1,0:T(8,128)(2,1)S(1)}, bf16[8,128,128]{2,1,0:T(8,128)(2,1)S(1)}, u32[]{:S(2)}, u32[]{:S(2)}) collective-permute-start(bf16[8,128,128]{2,1,0:T(8,128)(2,1)S(1)} %bitcast.8), channel_id=1, source_target_pairs={{0,1},{1,0},{2,3},{3,2},{4,5},{5,4},{6,7},{7,6},{8,9},{9,8},{10,11... | collective-permute-start | bytes 786440 | tf_op jit(solution)/shard_map/ppermute | solution.py:402
  5.8 0.7 compare_select_fusion.4
  6.5 5.2 %shard_map.64 = (s32[64,128]{1,0:T(8,128)S(1)}, s32[64,128]{1,0:T(8,128)S(1)}, bf16[48,128,128]{2,1,0:T(8,128)(2,1)S(1)}, bf16[32,128,128]{2,1,0:T(8,128)(2,1)S(...) custom-call(s32[1,64]{1,0:T(1,128)S(1)} %get-tuple-element.70.s_row,, ...), custom_call_target="tpu_custom_call" | custom-call | flops 805306368 | bytes 14680064 | tf_op jit(solution)/shard_map/pallas_call | solution.py:153
  11.7 0.6 shard_map.65
  12.3 1.0 %collective-permute-start.5 = (bf16[8,128,128]{2,1,0:T(8,128)(2,1)S(1)}, bf16[8,128,128]{2,1,0:T(8,128)(2,1)S(1)}, u32[]{:S(2)}, u32[]{:S(2)}) collective-permute-start(bf16[8,128,128]{2,1,0:T(8,128)(2,1)S(1)} %get-tuple-element.40.far.f_far), channel_id=1, source_target_pairs={{0,7},{1,2},{2,1},{3,4},{4,3},{5,6},{6,5},{7,0},{8,15},{9,10},{10,... | collective-permute-start | bytes 786440 | tf_op jit(solution)/shard_map/ppermute | solution.py:402
  13.3 3.6 %collective-permute-start.6 = (bf16[8,128,128]{2,1,0:T(8,128)(2,1)S(1)}, bf16[8,128,128]{2,1,0:T(8,128)(2,1)S(1)}, u32[]{:S(2)}, u32[]{:S(2)}) collective-permute-start(bf16[8,128,128]{2,1,0:T(8,128)(2,1)S(1)} %get-tuple-element.41.near.f_near), channel_id=1, source_target_pairs={{0,1},{1,0},{2,3},{3,2},{4,5},{5,4},{6,7},{7,6},{8,9},{9,8},{10,11... | collective-permute-start | bytes 786440 | tf_op jit(solution)/shard_map/ppermute | solution.py:402
  16.9 1.1 %shard_map.66 = (bf16[8,128,128]{2,1,0:T(8,128)(2,1)S(1)}, bf16[8,128,128]{2,1,0:T(8,128)(2,1)S(1)}, bf16[8,128,128]{2,1,0:T(8,128)(2,1)S(1)}, bf16[8,128,128]{2...) custom-call(s32[64,128]{1,0:T(8,128)S(1)} %get-tuple-element.36.index.s_index, ...), custom_call_target="tpu_custom_call" | custom-call | flops 268435456 | bytes 8388608 | tf_op jit(solution)/shard_map/pallas_call | solution.py:232
  18.0 1.7 %collective-permute-start.2 = (bf16[8,128,128]{2,1,0:T(8,128)(2,1)S(1)}, bf16[8,128,128]{2,1,0:T(8,128)(2,1)S(1)}, u32[]{:S(2)}, u32[]{:S(2)}) collective-permute-start(bf16[8,128,128]{2,1,0:T(8,128)(2,1)S(1)} %get-tuple-element.48), channel_id=1, source_target_pairs={{0,16},{8,24},{16,32},{24,40},{32,48},{40,56},{48,0},{56,8},{64,80... | collective-permute-start | bytes 786440 | tf_op jit(solution)/shard_map/ppermute | solution.py:412
  19.6 1.7 %collective-permute-start.3 = (bf16[8,128,128]{2,1,0:T(8,128)(2,1)S(1)}, bf16[8,128,128]{2,1,0:T(8,128)(2,1)S(1)}, u32[]{:S(2)}, u32[]{:S(2)}) collective-permute-start(bf16[8,128,128]{2,1,0:T(8,128)(2,1)S(1)} %get-tuple-element.49), channel_id=1, source_target_pairs={{0,48},{8,56},{16,0},{24,8},{32,16},{40,24},{48,32},{56,40},{64,11... | collective-permute-start | bytes 786440 | tf_op jit(solution)/shard_map/ppermute | solution.py:412
  21.3 2.0 %collective-permute-start.4 = (bf16[8,128,128]{2,1,0:T(8,128)(2,1)S(1)}, bf16[8,128,128]{2,1,0:T(8,128)(2,1)S(1)}, u32[]{:S(2)}, u32[]{:S(2)}) collective-permute-start(bf16[8,128,128]{2,1,0:T(8,128)(2,1)S(1)} %get-tuple-element.50), channel_id=1, source_target_pairs={{0,32},{8,40},{16,48},{24,56},{32,0},{40,8},{48,16},{56,24},{64,96... | collective-permute-start | bytes 786440 | tf_op jit(solution)/shard_map/ppermute | solution.py:412
  23.3 0.6 shard_map.67
  24.3 3.4 %collective-permute-start.8 = (bf16[8,128,128]{2,1,0:T(8,128)(2,1)S(1)}, bf16[8,128,128]{2,1,0:T(8,128)(2,1)S(1)}, u32[]{:S(2)}, u32[]{:S(2)}) collective-permute-start(bf16[8,128,128]{2,1,0:T(8,128)(2,1)S(1)} %get-tuple-element.54.near), channel_id=1, source_target_pairs={{0,1},{1,0},{2,3},{3,2},{4,5},{5,4},{6,7},{7,6},{8,9},{9,8},{10,11... | collective-permute-start | bytes 786440 | tf_op jit(solution)/shard_map/ppermute | solution.py:402
  27.7 0.6 shard_map.68.layer3
  28.4 4.2 %collective-permute-done.3.after2.refs_2_ = bf16[8,128,128]{2,1,0:T(8,128)(2,1)S(1)} collective-permute-done((bf16[8,128,128]{2,1,0:T(8,128)(2,1)S(1)}, bf16[8,128,128]{2,1,0:T(8,128)(2,1)S(1)}, u32[]{:S(2)}, u32[]{:S(2)}) %collective-permute-start.3) | collective-permute-done | bytes 262176 | tf_op jit(solution)/shard_map/ppermute | solution.py:412
  32.5 1.8 %collective-permute-done.4.after3.refs_3_ = bf16[8,128,128]{2,1,0:T(8,128)(2,1)S(1)} collective-permute-done((bf16[8,128,128]{2,1,0:T(8,128)(2,1)S(1)}, bf16[8,128,128]{2,1,0:T(8,128)(2,1)S(1)}, u32[]{:S(2)}, u32[]{:S(2)}) %collective-permute-start.4) | collective-permute-done | bytes 262176 | tf_op jit(solution)/shard_map/ppermute | solution.py:412
  34.4 0.7 shard_map.69
  35.0 1.2 %collective-permute-start.9 = (bf16[10,128,128]{2,1,0:T(8,128)(2,1)S(1)}, bf16[10,128,128]{2,1,0:T(8,128)(2,1)S(1)}, u32[]{:S(2)}, u32[]{:S(2)}) collective-permute-start(bf16[10,128,128]{2,1,0:T(8,128)(2,1)S(1)} %get-tuple-element.58), channel_id=1, source_target_pairs={{0,16},{8,24},{16,32},{24,40},{32,48},{40,56},{48,0},{56,8},{64,80... | collective-permute-start | bytes 983048 | tf_op jit(solution)/shard_map/ppermute | solution.py:412
  36.2 2.1 %collective-permute-start.10 = (bf16[10,128,128]{2,1,0:T(8,128)(2,1)S(1)}, bf16[10,128,128]{2,1,0:T(8,128)(2,1)S(1)}, u32[]{:S(2)}, u32[]{:S(2)}) collective-permute-start(bf16[10,128,128]{2,1,0:T(8,128)(2,1)S(1)} %get-tuple-element.59), channel_id=1, source_target_pairs={{0,48},{8,56},{16,0},{24,8},{32,16},{40,24},{48,32},{56,40},{64,11... | collective-permute-start | bytes 983048 | tf_op jit(solution)/shard_map/ppermute | solution.py:412
  38.6 6.5 %collective-permute-done.9.refs_5_ = bf16[10,128,128]{2,1,0:T(8,128)(2,1)S(1)} collective-permute-done((bf16[10,128,128]{2,1,0:T(8,128)(2,1)S(1)}, bf16[10,128,128]{2,1,0:T(8,128)(2,1)S(1)}, u32[]{:S(2)}, u32[]{:S(2)}) %collective-permute-start.9) | collective-permute-done | bytes 327712 | tf_op jit(solution)/shard_map/ppermute | solution.py:412
  45.1 6.6 %collective-permute-done.10.refs_6_ = bf16[10,128,128]{2,1,0:T(8,128)(2,1)S(1)} collective-permute-done((bf16[10,128,128]{2,1,0:T(8,128)(2,1)S(1)}, bf16[10,128,128]{2,1,0:T(8,128)(2,1)S(1)}, u32[]{:S(2)}, u32[]{:S(2)}) %collective-permute-start.10) | collective-permute-done | bytes 327712 | tf_op jit(solution)/shard_map/ppermute | solution.py:412
  51.6 1.6 %collective-permute-done.11.refs_7_ = bf16[10,128,128]{2,1,0:T(8,128)(2,1)S(1)} collective-permute-done((bf16[10,128,128]{2,1,0:T(8,128)(2,1)S(1)}, bf16[10,128,128]{2,1,0:T(8,128)(2,1)S(1)}, u32[]{:S(2)}, u32[]{:S(2)}) %collective-permute-start.11) | collective-permute-done | bytes 327712 | tf_op jit(solution)/shard_map/ppermute | solution.py:412
  53.7 0.6 shard_map.71
  54.3 1.6 %collective-permute-start.13 = (bf16[256,256]{1,0:T(8,128)(2,1)S(1)}, bf16[256,256]{1,0:T(8,128)(2,1)S(1)}, u32[]{:S(2)}, u32[]{:S(2)}) collective-permute-start(bf16[256,256]{1,0:T(8,128)(2,1)S(1)} %get-tuple-element.62), channel_id=1, source_target_pairs={{0,64},{8,72},{16,80},{24,88},{32,96},{40,104},{48,112},{56,120},{... | collective-permute-start | bytes 393224 | tf_op jit(solution)/shard_map/ppermute | solution.py:395
  55.9 2.1 %collective-permute-start.14 = (bf16[256,256]{1,0:T(8,128)(2,1)S(1)}, bf16[256,256]{1,0:T(8,128)(2,1)S(1)}, u32[]{:S(2)}, u32[]{:S(2)}) collective-permute-start(bf16[256,256]{1,0:T(8,128)(2,1)S(1)} %get-tuple-element.63), channel_id=1, source_target_pairs={{0,192},{8,200},{16,208},{24,216},{32,224},{40,232},{48,240},{56,2... | collective-permute-start | bytes 393224 | tf_op jit(solution)/shard_map/ppermute | solution.py:395
  58.0 2.0 %collective-permute-start.15 = (bf16[256,256]{1,0:T(8,128)(2,1)S(1)}, bf16[256,256]{1,0:T(8,128)(2,1)S(1)}, u32[]{:S(2)}, u32[]{:S(2)}) collective-permute-start(bf16[256,256]{1,0:T(8,128)(2,1)S(1)} %get-tuple-element.64), channel_id=1, source_target_pairs={{0,72},{8,64},{16,88},{24,80},{32,104},{40,96},{48,120},{56,112},{... | collective-permute-start | bytes 393224 | tf_op jit(solution)/shard_map/ppermute | solution.py:395
  60.1 0.5 collective-permute-start.16
  60.6 2.3 %collective-permute-done.12.arrived = bf16[2,256,256]{2,1,0:T(8,128)(2,1)S(1)} collective-permute-done((bf16[2,256,256]{2,1,0:T(8,128)(2,1)S(1)}, bf16[2,256,256]{2,1,0:T(8,128)(2,1)S(1)}, u32[]{:S(2)}, u32[]{:S(2)}) %collective-permute-start.12) | collective-permute-done | bytes 262176 | tf_op jit(solution)/shard_map/ppermute | solution.py:395
  63.0 3.1 %collective-permute-start.17 = (bf16[256,256]{1,0:T(8,128)(2,1)S(1)}, bf16[256,256]{1,0:T(8,128)(2,1)S(1)}, u32[]{:S(2)}, u32[]{:S(2)}) collective-permute-start(bf16[256,256]{1,0:T(8,128)(2,1)S(1)} %shard_map.72), channel_id=1, source_target_pairs={{0,128},{8,136},{16,144},{24,152},{32,160},{40,168},{48,176},{56,1... | collective-permute-start | bytes 393224 | tf_op jit(solution)/shard_map/ppermute | solution.py:395
  66.1 0.5 collective-permute-done.15.refs_2_
  66.5 3.6 %collective-permute-done.16.refs_3_ = bf16[256,256]{1,0:T(8,128)(2,1)S(1)} collective-permute-done((bf16[256,256]{1,0:T(8,128)(2,1)S(1)}, bf16[256,256]{1,0:T(8,128)(2,1)S(1)}, u32[]{:S(2)}, u32[]{:S(2)}) %collective-permute-start.16) | collective-permute-done | bytes 131104 | tf_op jit(solution)/shard_map/ppermute | solution.py:395
  70.5 0.8 %shard_map.73 = f32[1,256,256]{2,1,0:T(8,128)} custom-call(f32[256,256]{1,0:T(8,128)S(1)} %get-tuple-element.61.own, bf16[2,256,256]{2,1,0:T(8,128)(2,1)S(1)} %collective-permute-done.12.arrived, bf16[256,256]{1,0:T(8,128)(2,1)S(1)} %collective-permute-done.13.refs_0_, bf16[256,256]{1,0:T(8,128)(2,1)S(1)} %collective-permute-done.14.refs_1_, ...), custom_call_target="tpu_custom_call" | custom-call | flops 524288 | bytes 1048576 | tf_op jit(solution)/shard_map/pallas_call | solution.py:379
  (18 shorter events, 1.7 us)
Async XLA Ops:
  1.1 10.6 %collective-permute-start = (bf16[8,128,128]{2,1,0:T(8,128)(2,1)S(1)}, bf16[8,128,128]{2,1,0:T(8,128)(2,1)S(1)}, u32[]{:S(2)}, u32[]{:S(2)}) collective-permute-start(bf16[8,128,128]{2,1,0:T(8,128)(2,1)S(1)} %bitcast.9), channel_id=1, source_target_pairs={{0,7},{1,2},{2,1},{3,4},{4,3},{5,6},{6,5},{7,0},{8,15},{9,10},{10,... | collective-permute-start | bytes 786440 | tf_op jit(solution)/shard_map/ppermute | solution.py:402
  1.2 10.5 %collective-permute-start.1 = (bf16[8,128,128]{2,1,0:T(8,128)(2,1)S(1)}, bf16[8,128,128]{2,1,0:T(8,128)(2,1)S(1)}, u32[]{:S(2)}, u32[]{:S(2)}) collective-permute-start(bf16[8,128,128]{2,1,0:T(8,128)(2,1)S(1)} %bitcast.8), channel_id=1, source_target_pairs={{0,1},{1,0},{2,3},{3,2},{4,5},{5,4},{6,7},{7,6},{8,9},{9,8},{10,11... | collective-permute-start | bytes 786440 | tf_op jit(solution)/shard_map/ppermute | solution.py:402
  12.3 11.0 %collective-permute-start.5 = (bf16[8,128,128]{2,1,0:T(8,128)(2,1)S(1)}, bf16[8,128,128]{2,1,0:T(8,128)(2,1)S(1)}, u32[]{:S(2)}, u32[]{:S(2)}) collective-permute-start(bf16[8,128,128]{2,1,0:T(8,128)(2,1)S(1)} %get-tuple-element.40.far.f_far), channel_id=1, source_target_pairs={{0,7},{1,2},{2,1},{3,4},{4,3},{5,6},{6,5},{7,0},{8,15},{9,10},{10,... | collective-permute-start | bytes 786440 | tf_op jit(solution)/shard_map/ppermute | solution.py:402
  13.3 10.0 %collective-permute-start.6 = (bf16[8,128,128]{2,1,0:T(8,128)(2,1)S(1)}, bf16[8,128,128]{2,1,0:T(8,128)(2,1)S(1)}, u32[]{:S(2)}, u32[]{:S(2)}) collective-permute-start(bf16[8,128,128]{2,1,0:T(8,128)(2,1)S(1)} %get-tuple-element.41.near.f_near), channel_id=1, source_target_pairs={{0,1},{1,0},{2,3},{3,2},{4,5},{5,4},{6,7},{7,6},{8,9},{9,8},{10,11... | collective-permute-start | bytes 786440 | tf_op jit(solution)/shard_map/ppermute | solution.py:402
  18.0 10.4 %collective-permute-start.2 = (bf16[8,128,128]{2,1,0:T(8,128)(2,1)S(1)}, bf16[8,128,128]{2,1,0:T(8,128)(2,1)S(1)}, u32[]{:S(2)}, u32[]{:S(2)}) collective-permute-start(bf16[8,128,128]{2,1,0:T(8,128)(2,1)S(1)} %get-tuple-element.48), channel_id=1, source_target_pairs={{0,16},{8,24},{16,32},{24,40},{32,48},{40,56},{48,0},{56,8},{64,80... | collective-permute-start | bytes 786440 | tf_op jit(solution)/shard_map/ppermute | solution.py:412
  19.6 12.9 %collective-permute-start.3 = (bf16[8,128,128]{2,1,0:T(8,128)(2,1)S(1)}, bf16[8,128,128]{2,1,0:T(8,128)(2,1)S(1)}, u32[]{:S(2)}, u32[]{:S(2)}) collective-permute-start(bf16[8,128,128]{2,1,0:T(8,128)(2,1)S(1)} %get-tuple-element.49), channel_id=1, source_target_pairs={{0,48},{8,56},{16,0},{24,8},{32,16},{40,24},{48,32},{56,40},{64,11... | collective-permute-start | bytes 786440 | tf_op jit(solution)/shard_map/ppermute | solution.py:412
  21.3 13.0 %collective-permute-start.4 = (bf16[8,128,128]{2,1,0:T(8,128)(2,1)S(1)}, bf16[8,128,128]{2,1,0:T(8,128)(2,1)S(1)}, u32[]{:S(2)}, u32[]{:S(2)}) collective-permute-start(bf16[8,128,128]{2,1,0:T(8,128)(2,1)S(1)} %get-tuple-element.50), channel_id=1, source_target_pairs={{0,32},{8,40},{16,48},{24,56},{32,0},{40,8},{48,16},{56,24},{64,96... | collective-permute-start | bytes 786440 | tf_op jit(solution)/shard_map/ppermute | solution.py:412
  23.9 10.5 %copy-start = (f32[128]{0:T(128)S(1)}, f32[128]{0:T(128)}, u32[]{:S(2)}) copy-start(f32[128]{0:T(128)} %param.7) | copy-start | bytes 1540
  23.9 10.5 %collective-permute-start.7 = (bf16[8,128,128]{2,1,0:T(8,128)(2,1)S(1)}, bf16[8,128,128]{2,1,0:T(8,128)(2,1)S(1)}, u32[]{:S(2)}, u32[]{:S(2)}) collective-permute-start(bf16[8,128,128]{2,1,0:T(8,128)(2,1)S(1)} %get-tuple-element.53.far), channel_id=1, source_target_pairs={{0,7},{1,2},{2,1},{3,4},{4,3},{5,6},{6,5},{7,0},{8,15},{9,10},{10,... | collective-permute-start | bytes 786440 | tf_op jit(solution)/shard_map/ppermute | solution.py:402
  24.3 10.0 %collective-permute-start.8 = (bf16[8,128,128]{2,1,0:T(8,128)(2,1)S(1)}, bf16[8,128,128]{2,1,0:T(8,128)(2,1)S(1)}, u32[]{:S(2)}, u32[]{:S(2)}) collective-permute-start(bf16[8,128,128]{2,1,0:T(8,128)(2,1)S(1)} %get-tuple-element.54.near), channel_id=1, source_target_pairs={{0,1},{1,0},{2,3},{3,2},{4,5},{5,4},{6,7},{7,6},{8,9},{9,8},{10,11... | collective-permute-start | bytes 786440 | tf_op jit(solution)/shard_map/ppermute | solution.py:402
  35.0 10.1 %collective-permute-start.9 = (bf16[10,128,128]{2,1,0:T(8,128)(2,1)S(1)}, bf16[10,128,128]{2,1,0:T(8,128)(2,1)S(1)}, u32[]{:S(2)}, u32[]{:S(2)}) collective-permute-start(bf16[10,128,128]{2,1,0:T(8,128)(2,1)S(1)} %get-tuple-element.58), channel_id=1, source_target_pairs={{0,16},{8,24},{16,32},{24,40},{32,48},{40,56},{48,0},{56,8},{64,80... | collective-permute-start | bytes 983048 | tf_op jit(solution)/shard_map/ppermute | solution.py:412
  36.2 15.4 %collective-permute-start.10 = (bf16[10,128,128]{2,1,0:T(8,128)(2,1)S(1)}, bf16[10,128,128]{2,1,0:T(8,128)(2,1)S(1)}, u32[]{:S(2)}, u32[]{:S(2)}) collective-permute-start(bf16[10,128,128]{2,1,0:T(8,128)(2,1)S(1)} %get-tuple-element.59), channel_id=1, source_target_pairs={{0,48},{8,56},{16,0},{24,8},{32,16},{40,24},{48,32},{56,40},{64,11... | collective-permute-start | bytes 983048 | tf_op jit(solution)/shard_map/ppermute | solution.py:412
  38.3 14.9 %collective-permute-start.11 = (bf16[10,128,128]{2,1,0:T(8,128)(2,1)S(1)}, bf16[10,128,128]{2,1,0:T(8,128)(2,1)S(1)}, u32[]{:S(2)}, u32[]{:S(2)}) collective-permute-start(bf16[10,128,128]{2,1,0:T(8,128)(2,1)S(1)} %get-tuple-element.60), channel_id=1, source_target_pairs={{0,32},{8,40},{16,48},{24,56},{32,0},{40,8},{48,16},{56,24},{64,96... | collective-permute-start | bytes 983048 | tf_op jit(solution)/shard_map/ppermute | solution.py:412
  53.6 9.3 %collective-permute-start.12 = (bf16[2,256,256]{2,1,0:T(8,128)(2,1)S(1)}, bf16[2,256,256]{2,1,0:T(8,128)(2,1)S(1)}, u32[]{:S(2)}, u32[]{:S(2)}) collective-permute-start(bf16[2,256,256]{2,1,0:T(8,128)(2,1)S(1)} %shard_map.70.refs_8_), channel_id=1, source_target_pairs={{0,8},{8,0},{16,24},{24,16},{32,40},{40,32},{48,56},{56,48},{64,72... | collective-permute-start | bytes 786440 | tf_op jit(solution)/shard_map/ppermute | solution.py:395
  54.3 11.7 %collective-permute-start.13 = (bf16[256,256]{1,0:T(8,128)(2,1)S(1)}, bf16[256,256]{1,0:T(8,128)(2,1)S(1)}, u32[]{:S(2)}, u32[]{:S(2)}) collective-permute-start(bf16[256,256]{1,0:T(8,128)(2,1)S(1)} %get-tuple-element.62), channel_id=1, source_target_pairs={{0,64},{8,72},{16,80},{24,88},{32,96},{40,104},{48,112},{56,120},{... | collective-permute-start | bytes 393224 | tf_op jit(solution)/shard_map/ppermute | solution.py:395
  55.9 10.2 %collective-permute-start.14 = (bf16[256,256]{1,0:T(8,128)(2,1)S(1)}, bf16[256,256]{1,0:T(8,128)(2,1)S(1)}, u32[]{:S(2)}, u32[]{:S(2)}) collective-permute-start(bf16[256,256]{1,0:T(8,128)(2,1)S(1)} %get-tuple-element.63), channel_id=1, source_target_pairs={{0,192},{8,200},{16,208},{24,216},{32,224},{40,232},{48,240},{56,2... | collective-permute-start | bytes 393224 | tf_op jit(solution)/shard_map/ppermute | solution.py:395
  58.0 8.5 %collective-permute-start.15 = (bf16[256,256]{1,0:T(8,128)(2,1)S(1)}, bf16[256,256]{1,0:T(8,128)(2,1)S(1)}, u32[]{:S(2)}, u32[]{:S(2)}) collective-permute-start(bf16[256,256]{1,0:T(8,128)(2,1)S(1)} %get-tuple-element.64), channel_id=1, source_target_pairs={{0,72},{8,64},{16,88},{24,80},{32,104},{40,96},{48,120},{56,112},{... | collective-permute-start | bytes 393224 | tf_op jit(solution)/shard_map/ppermute | solution.py:395
  60.1 10.0 %collective-permute-start.16 = (bf16[256,256]{1,0:T(8,128)(2,1)S(1)}, bf16[256,256]{1,0:T(8,128)(2,1)S(1)}, u32[]{:S(2)}, u32[]{:S(2)}) collective-permute-start(bf16[256,256]{1,0:T(8,128)(2,1)S(1)} %get-tuple-element.65), channel_id=1, source_target_pairs={{0,200},{8,192},{16,216},{24,208},{32,232},{40,224},{48,248},{56,2... | collective-permute-start | bytes 393224 | tf_op jit(solution)/shard_map/ppermute | solution.py:395
  63.0 7.5 %collective-permute-start.17 = (bf16[256,256]{1,0:T(8,128)(2,1)S(1)}, bf16[256,256]{1,0:T(8,128)(2,1)S(1)}, u32[]{:S(2)}, u32[]{:S(2)}) collective-permute-start(bf16[256,256]{1,0:T(8,128)(2,1)S(1)} %shard_map.72), channel_id=1, source_target_pairs={{0,128},{8,136},{16,144},{24,152},{32,160},{40,168},{48,176},{56,1... | collective-permute-start | bytes 393224 | tf_op jit(solution)/shard_map/ppermute | solution.py:395

commit v6 on v5

--- a/solution.py
+++ b/solution.py
@@ -1,3 +1,5 @@
+import functools
+
 import jax
 import jax.numpy as jnp
 from jax import lax
@@ -172,53 +174,77 @@
     ref[pl.ds(jnp.where(odd == 1, head_at, tail_at), 8)] = near[...]
 
 
-def edge_rows(index, ext, x, far, near):
+def edge_side(far):
     odd = lax.axis_index("sec") % 2
-    for out, high in ((far, odd), (near, 1 - odd)):
-        for k in range(8):
-            out[k] = row_product(x[8 * high + k], ext, 32 * high - 8, 56 * high + k, index)
-
-
-def first_edges_kernel(index, far_halo, near_halo, c, x, far, near, ext):
-    place(ext, far_halo, near_halo, 0, 40)
-    ext[8:40] = c[...]
-    edge_rows(index, ext, x, far, near)
-
-
-def second_edges_kernel(
-    index, far_halo, near_halo, f_far, f_near, first, x, after, far, near, ext
-):
-    place(ext, far_halo, near_halo, 0, 40)
-    place(ext, f_far, f_near, 8, 32)
-    ext[16:24] = first[0:8]
-    ext[24:32] = first[40:48]
-    edge_rows(index, ext, x, far, near)
-
-
-def edges(kernel, *operands):
+    return odd if far else 1 - odd
+
+
+def edge_rows(index, ext, x, high, emit):
+    for k in range(8):
+        emit(k, row_product(x[8 * high + k], ext, 56 * high - 8, 56 * high + k, index))
+
+
+def first_edge_kernel(far, index, halo, c, x, after, out, ext):
+    high = edge_side(far)
+    ext[pl.ds(16 * high, 8)] = halo[...]
+    ext[pl.ds(8 - 8 * high, 16)] = c[pl.ds(16 * high, 16)]
+
+    def emit(k, value):
+        out[k] = value
+
+    edge_rows(index, ext, x, high, emit)
+
+
+def fill_ext(ext, high, halo, edge, inside, inside_at):
+    ext[pl.ds(16 * high, 8)] = halo[...]
+    ext[8:16] = edge[...]
+    ext[pl.ds(16 - 16 * high, 8)] = inside[pl.ds(inside_at * high, 8)]
+
+
+def second_edge_kernel(far, index, halo, edge, first, x, after, out, ext):
+    high = edge_side(far)
+    fill_ext(ext, high, halo, edge, first, 40)
+
+    def emit(k, value):
+        out[k] = value
+
+    edge_rows(index, ext, x, high, emit)
+
+
+def near_kernel(index, halo, edge, mid, x, out, ext):
+    high = edge_side(False)
+    fill_ext(ext, high, halo, edge, mid, 8)
+
+    def emit(k, value):
+        out[k] = value
+
+    edge_rows(index, ext, x, high, emit)
+
+
+def edge(kernel, *operands):
     return pl.pallas_call(
         kernel,
-        out_shape=[blocks_of(8)] * 2,
+        out_shape=blocks_of(8),
         in_specs=[VMEM] + [VMEM] * (len(operands) - 1),
-        out_specs=[VMEM] * 2,
-        scratch_shapes=[pltpu.VMEM((48, BS, BS), BF)],
-        compiler_params=params(4),
-        cost_estimate=cost(16, 3 * 2**20),
+        out_specs=VMEM,
+        scratch_shapes=[pltpu.VMEM((24, BS, BS), BF)],
+        compiler_params=params(4),
+        cost_estimate=cost(8, 2 * 2**20),
     )(*operands)
 
 
 def middle_kernel(
-    s_index, v_index, far, near, first, second, layer1, v, s, low_out, high_out, b0, b1, b2, b3, f, e
+    s_index, v_index, far, near, first, second, layer1, v, s, mid, b0, b1, b2, b3, f, e
 ):
     place(f, far, near, 0, 40)
     f[8:24] = first[0:16]
     f[24:40] = first[32:48]
     for k in range(8):
-        low_out[k] = row_product(v[k], f, 0, 8 + k, v_index)
-        high_out[k] = row_product(v[8 + k], f, 16, 48 + k, v_index)
-    e[0:8] = low_out[...]
+        mid[k] = row_product(v[k], f, 0, 8 + k, v_index)
+        mid[8 + k] = row_product(v[8 + k], f, 16, 48 + k, v_index)
+    e[0:8] = mid[0:8]
     e[8:40] = second[...]
-    e[40:48] = high_out[...]
+    e[40:48] = mid[8:16]
     _, y, _ = coords()
     for step, out in enumerate((b0, b1, b2, b3)):
         out[0:4] = layer1[4 * step : 4 * step + 4]
@@ -231,21 +257,21 @@
 def middle(*operands):
     return pl.pallas_call(
         middle_kernel,
-        out_shape=[blocks_of(8)] * 6,
+        out_shape=[blocks_of(16)] + [blocks_of(8)] * 4,
         in_specs=[VMEM, VMEM] + [VMEM] * 7,
-        out_specs=[VMEM] * 6,
+        out_specs=[VMEM] * 5,
         scratch_shapes=[pltpu.VMEM((48, BS, BS), BF), pltpu.VMEM((48, BS, BS), BF)],
         compiler_params=params(4),
         cost_estimate=cost(32, 8 * 2**20),
     )(*operands)
 
 
-def outer_kernel(index, far, near, low, high, second, s, layer3, e):
+def outer_kernel(index, far, near, mid, second, s, layer3, e):
     place(e, far, near, 0, 40)
-    e[8:16] = low[...]
+    e[8:16] = mid[0:8]
     e[16:24] = second[0:8]
     e[24:32] = second[24:32]
-    e[32:40] = high[...]
+    e[32:40] = mid[8:16]
     _, y, _ = coords()
     for step in range(NY):
         start = layer_start(3, (y + step) % NY)
@@ -259,7 +285,7 @@
     return pl.pallas_call(
         outer_kernel,
         out_shape=blocks_of(16),
-        in_specs=[VMEM] + [VMEM] * 6,
+        in_specs=[VMEM] + [VMEM] * 5,
         out_specs=VMEM,
         scratch_shapes=[pltpu.VMEM((48, BS, BS), BF)],
         compiler_params=params(4),
@@ -268,39 +294,35 @@
 
 
 def last_kernel(
-    index, far_halo, near_halo, far, near, low, high, s, gaps, layer3, after1, after2, after3,
-    b0, b1, b2, b3, e,
+    index, halo, edge, mid, x, near_rows, gaps, layer3, after1, after2, after3, b0, b1, b2, b3, ext, rows
 ):
-    place(e, far_halo, near_halo, 0, 40)
-    place(e, far, near, 8, 32)
-    e[16:24] = low[...]
-    e[24:32] = high[...]
+    high = edge_side(True)
+    rows[pl.ds(8 - 8 * high, 8)] = near_rows[...]
+    fill_ext(ext, high, halo, edge, mid, 8)
+
+    def emit(k, value):
+        rows[8 * high + k] = value
+
+    edge_rows(index, ext, x, high, emit)
     gap = gaps[...]
     weight = 4.0 * gap / (gap * gap + frequency_sq)
+    weighted = (rows[0:2].astype(F32) * weight[None]).astype(BF)
     _, y, _ = coords()
-    for k in range(2):
-        value = row_product(s[k], e, -8, k, index)
-        weighted = (value.astype(F32) * weight).astype(BF)
-        for out in (b0, b1, b2, b3):
-            out[8 + k] = weighted
     for step, out in enumerate((b0, b1, b2, b3)):
         out[0:4] = layer3[4 * step : 4 * step + 4]
-        start = layer_start(4, (y + step) % NY)
-        slot = stored_slot(4, start)
-        base = jnp.where(start < 32, -8, 24)
-        for k in range(4):
-            out[4 + k] = row_product(s[slot + k], e, base, start + k, index)
+        out[4:8] = rows[pl.ds(4 * ((y + step) % NY), 4)]
+        out[8:10] = weighted
 
 
 def last(*operands):
     return pl.pallas_call(
         last_kernel,
         out_shape=[blocks_of(10)] * 4,
-        in_specs=[VMEM] + [VMEM] * 12,
+        in_specs=[VMEM] + [VMEM] * 10,
         out_specs=[VMEM] * 4,
-        scratch_shapes=[pltpu.VMEM((48, BS, BS), BF)],
-        compiler_params=params(4),
-        cost_estimate=cost(18, 4 * 2**20),
+        scratch_shapes=[pltpu.VMEM((24, BS, BS), BF), pltpu.VMEM((16, BS, BS), BF)],
+        compiler_params=params(4),
+        cost_estimate=cost(8, 4 * 2**20),
     )(*operands)
 
 
@@ -335,7 +357,7 @@
     own, passed, outs = refs[9], refs[10], refs[11:]
     x, _, z = coords()
     for out, (step, flip) in zip(outs, DIRECT):
-        out[...] = chunk(inside, outside, x ^ step, z ^ flip).astype(BF)
+        out[...] = chunk(inside, outside, (x + step) % NX, z ^ flip).astype(BF)
     passed[...] = chunk(inside, outside, x ^ 2, z)
     own[...] = chunk(inside, outside, x, z)
 
@@ -386,12 +408,12 @@
     )(*operands)
 
 
-def swap(value, dx, dy, dz):
+def shift(value, dx, dy, dz):
     pairs = []
     for x in range(NX):
         for y in range(NY):
             for z in range(NZ):
-                pairs.append(((x * NY + y) * NZ + z, ((x ^ dx) * NY + (y ^ dy)) * NZ + (z ^ dz)))
+                pairs.append(((x * NY + y) * NZ + z, ((x + dx) % NX * NY + (y ^ dy)) * NZ + (z ^ dz)))
     return lax.ppermute(value, "grp", pairs)
 
 
@@ -424,26 +446,31 @@
     c_far, c_near = halo(jnp.where(odd, c[56:], c[:8]), jnp.where(odd, c[:8], c[56:]))
     s_index, v_index, first, second, layer1, *edges_of = inner(s_row, v_row, c, s, v)
     c_edge, s_edge, v_edge, v_mid, s_mid, s_out = edges_of
-    f_sends = edges(first_edges_kernel, s_index, c_far, c_near, c_edge, s_edge)
-    f_halos = halo(*f_sends)
-    e_low, e_high, *inside = middle(s_index, v_index, *f_sends, first, second, layer1, v_mid, s_mid)
+    first_far, first_near = (functools.partial(first_edge_kernel, far) for far in (True, False))
+    second_far, second_near = (functools.partial(second_edge_kernel, far) for far in (True, False))
+    f_near = edge(first_near, s_index, c_near, c_edge, s_edge, layer1)
+    f_far = edge(first_far, s_index, c_far, c_edge, s_edge, f_near)
+    f_far_halo, f_near_halo = halo(f_far, f_near)
+    mid, *inside = middle(s_index, v_index, f_far, f_near, first, second, layer1, v_mid, s_mid)
     inside = spread_y(inside)
-    e_sends = edges(second_edges_kernel, v_index, *f_halos, *f_sends, first, v_edge, e_low)
-    e_halos = halo(*e_sends)
-    layer3 = outer(s_index, *e_sends, e_low, e_high, second, s_out)
+    e_near = edge(second_near, v_index, f_near_halo, f_near, first, v_edge, mid)
+    e_far = edge(second_far, v_index, f_far_halo, f_far, first, v_edge, e_near)
+    e_far_halo, e_near_halo = halo(e_far, e_near)
+    layer3 = outer(s_index, e_far, e_near, mid, second, s_out)
+    b_near = edge(near_kernel, s_index, e_near_halo, e_near, mid, s_edge)
     outside = last(
-        s_index, *e_halos, *e_sends, e_low, e_high, s_edge, gaps, layer3, *inside[1:]
+        s_index, e_far_halo, e_far, mid, s_edge, b_near, gaps, layer3, *inside[1:]
     )
     outside = spread_y(outside)
     tile = jax.ShapeDtypeStruct((QC, QC), BF)
     whole = jax.ShapeDtypeStruct((QC, QC), F32)
     across = product(across_kernel, 2, jax.ShapeDtypeStruct((2, QC, QC), BF), *inside, *outside)
-    arrived = swap(across, 0, 0, 1)
+    arrived = shift(across, 0, 0, 1)
     own, passed, *direct = product(
         product_kernel, 6, [whole] * 2 + [tile] * len(DIRECT), *inside, *outside, across
     )
-    direct = [swap(part, step, 0, flip) for part, (step, flip) in zip(direct, DIRECT)]
-    last_tile = swap(pass_on(passed, arrived), 2, 0, 0)
+    direct = [shift(part, step, 0, flip) for part, (step, flip) in zip(direct, DIRECT)]
+    last_tile = shift(pass_on(passed, arrived), 2, 0, 0)
     return add_up(own, arrived, *direct, last_tile)
 
 

time: 71.6 us -> 70.9 us (level)
  the two profiles are of different devices: /device:TPU:64 before, /device:TPU:75 now
where the time goes in v6:
time: 70.9 us; the launch traced here: 70.7 us
  waiting for transfers between devices  30.8 us (43%)
  starting transfers between devices  27.1 us (38%)
  Pallas kernels  10.9 us (15%)
  other arithmetic  1.77 us (2%)
    ppermute x6, waiting for transfers between devices, spread_y(): out[d] = lax.ppermute(parts[d], 'grp', pairs)  17.3 us
    ppermute x3, starting transfers between devices, halo(): lax.ppermute(far, 'sec', far_pairs)  11.5 us
    ppermute x6, waiting for transfers between devices, shift(): return lax.ppermute(value, 'grp', pairs)  10.2 us
    ppermute x6, starting transfers between devices, shift(): return lax.ppermute(value, 'grp', pairs)  7.56 us
    ppermute x6, starting transfers between devices, spread_y(): out[d] = lax.ppermute(parts[d], 'grp', pairs)  7.31 us
    pallas_call x1, Pallas kernels, inner(): pl.pallas_call(inner_kernel, out_shape=[column] * 2 + [blocks_of(48), blo...  5.22 us
    ppermute x3, waiting for transfers between devices, halo(): lax.ppermute(far, 'sec', far_pairs)  3.25 us
    pallas_call x5, Pallas kernels, edge(): pl.pallas_call(kernel, out_shape=blocks_of(8), in_specs=[VMEM] + [VMEM] *...  1.83 us
  transfers between devices with their start and end apart: 18, of which 9 were waited for; matrix products, arithmetic and copies ran while one was open for 1% of the time, Pallas kernels for 13%

profile of v6, /device:TPU:75, one launch (start us, length us, event | category | flops | bytes accessed | tf_op | source)
XLA Modules:
  0.0 70.7 jit_solution(9859447261451458152)
XLA Ops:
  0.0 1.1 %broadcast_select_fusion = (bf16[1024,128]{1,0:T(8,128)(2,1)S(1)}, bf16[1024,128]{1,0:T(8,128)(2,1)S(1)}) fusion(pred[]{:T(512)S(6)} %eq.5, bf16[8192,128]{1,0:T(8,128)(2,1)} %param.6), kind=kLoop, calls=%fused_computation | loop fusion | flops 262144 | bytes 1048577 | tf_op jit(solution)/shard_map/jit(_where)/select_n | solution.py:446
  1.1 4.8 %collective-permute-start = (bf16[8,128,128]{2,1,0:T(8,128)(2,1)S(1)}, bf16[8,128,128]{2,1,0:T(8,128)(2,1)S(1)}, u32[]{:S(2)}, u32[]{:S(2)}) collective-permute-start(bf16[8,128,128]{2,1,0:T(8,128)(2,1)S(1)} %bitcast.8), channel_id=1, source_target_pairs={{0,7},{1,2},{2,1},{3,4},{4,3},{5,6},{6,5},{7,0},{8,15},{9,10},{10,... | collective-permute-start | bytes 786440 | tf_op jit(solution)/shard_map/ppermute | solution.py:424
  5.9 0.7 compare_select_fusion.4
  6.6 5.2 %shard_map.64 = (s32[64,128]{1,0:T(8,128)S(1)}, s32[64,128]{1,0:T(8,128)S(1)}, bf16[48,128,128]{2,1,0:T(8,128)(2,1)S(1)}, bf16[32,128,128]{2,1,0:T(8,128)(2,1)S(...) custom-call(s32[1,64]{1,0:T(1,128)S(1)} %get-tuple-element.60.s_row,, ...), custom_call_target="tpu_custom_call" | custom-call | flops 805306368 | bytes 14680064 | tf_op jit(solution)/shard_map/pallas_call | solution.py:155
  11.9 0.4 shard_map.65.after.near.edge
  12.2 0.6 collective-permute-start.6
  12.8 0.4 shard_map.66.far.edge
  13.2 3.6 %collective-permute-start.5 = (bf16[8,128,128]{2,1,0:T(8,128)(2,1)S(1)}, bf16[8,128,128]{2,1,0:T(8,128)(2,1)S(1)}, u32[]{:S(2)}, u32[]{:S(2)}) collective-permute-start(bf16[8,128,128]{2,1,0:T(8,128)(2,1)S(1)} %shard_map.66.far.edge), channel_id=1, source_target_pairs={{0,7},{1,2},{2,1},{3,4},{4,3},{5,6},{6,5},{7,0},{8,15},{9,10},{10,... | collective-permute-start | bytes 786440 | tf_op jit(solution)/shard_map/ppermute | solution.py:424
  16.8 1.1 %shard_map.67 = (bf16[16,128,128]{2,1,0:T(8,128)(2,1)S(1)}, bf16[8,128,128]{2,1,0:T(8,128)(2,1)S(1)}, bf16[8,128,128]{2,1,0:T(8,128)(2,1)S(1)}, bf16[8,128,128]{2,1,0:T(8,128)(2,1)S(1)}, bf16[8,128,128]{2,1,0:T(8,128)(2,1)S(1)}) custom-call(s32[64,128]{1,0:T(8,128)S(1)} %get-tuple-element.31.index.s_index, s32[64,128]{1,0:T(8,128)S(1)} %get-tuple-element.32.v_index.index, ...), custom_call_target="tpu_custom_call" | custom-call | flops 268435456 | bytes 8388608 | tf_op jit(solution)/shard_map/pallas_call | solution.py:258
  17.9 1.4 %collective-permute-start.2 = (bf16[8,128,128]{2,1,0:T(8,128)(2,1)S(1)}, bf16[8,128,128]{2,1,0:T(8,128)(2,1)S(1)}, u32[]{:S(2)}, u32[]{:S(2)}) collective-permute-start(bf16[8,128,128]{2,1,0:T(8,128)(2,1)S(1)} %get-tuple-element.41), channel_id=1, source_target_pairs={{0,16},{8,24},{16,32},{24,40},{32,48},{40,56},{48,0},{56,8},{64,80... | collective-permute-start | bytes 786440 | tf_op jit(solution)/shard_map/ppermute | solution.py:434
  19.9 2.1 %collective-permute-start.4 = (bf16[8,128,128]{2,1,0:T(8,128)(2,1)S(1)}, bf16[8,128,128]{2,1,0:T(8,128)(2,1)S(1)}, u32[]{:S(2)}, u32[]{:S(2)}) collective-permute-start(bf16[8,128,128]{2,1,0:T(8,128)(2,1)S(1)} %get-tuple-element.43), channel_id=1, source_target_pairs={{0,32},{8,40},{16,48},{24,56},{32,0},{40,8},{48,16},{56,24},{64,96... | collective-permute-start | bytes 786440 | tf_op jit(solution)/shard_map/ppermute | solution.py:434
  22.1 1.9 %collective-permute-done.5.halo = bf16[8,128,128]{2,1,0:T(8,128)(2,1)S(1)} collective-permute-done((bf16[8,128,128]{2,1,0:T(8,128)(2,1)S(1)}, bf16[8,128,128]{2,1,0:T(8,128)(2,1)S(1)}, u32[]{:S(2)}, u32[]{:S(2)}) %collective-permute-start.5) | collective-permute-done | bytes 262176 | tf_op jit(solution)/shard_map/ppermute | solution.py:424
  24.4 3.1 %collective-permute-start.7 = (bf16[8,128,128]{2,1,0:T(8,128)(2,1)S(1)}, bf16[8,128,128]{2,1,0:T(8,128)(2,1)S(1)}, u32[]{:S(2)}, u32[]{:S(2)}) collective-permute-start(bf16[8,128,128]{2,1,0:T(8,128)(2,1)S(1)} %shard_map.69.far.edge), channel_id=1, source_target_pairs={{0,7},{1,2},{2,1},{3,4},{4,3},{5,6},{6,5},{7,0},{8,15},{9,10},{10,... | collective-permute-start | bytes 786440 | tf_op jit(solution)/shard_map/ppermute | solution.py:424
  27.5 0.6 shard_map.71.layer3
  28.5 3.4 %collective-permute-done.4.after3.refs_3_ = bf16[8,128,128]{2,1,0:T(8,128)(2,1)S(1)} collective-permute-done((bf16[8,128,128]{2,1,0:T(8,128)(2,1)S(1)}, bf16[8,128,128]{2,1,0:T(8,128)(2,1)S(1)}, u32[]{:S(2)}, u32[]{:S(2)}) %collective-permute-start.4) | collective-permute-done | bytes 262176 | tf_op jit(solution)/shard_map/ppermute | solution.py:434
  31.8 1.3 %collective-permute-done.7.halo = bf16[8,128,128]{2,1,0:T(8,128)(2,1)S(1)} collective-permute-done((bf16[8,128,128]{2,1,0:T(8,128)(2,1)S(1)}, bf16[8,128,128]{2,1,0:T(8,128)(2,1)S(1)}, u32[]{:S(2)}, u32[]{:S(2)}) %collective-permute-start.7) | collective-permute-done | bytes 262176 | tf_op jit(solution)/shard_map/ppermute | solution.py:424
  33.1 0.4 shard_map.72
  33.5 1.9 %collective-permute-start.9 = (bf16[10,128,128]{2,1,0:T(8,128)(2,1)S(1)}, bf16[10,128,128]{2,1,0:T(8,128)(2,1)S(1)}, u32[]{:S(2)}, u32[]{:S(2)}) collective-permute-start(bf16[10,128,128]{2,1,0:T(8,128)(2,1)S(1)} %get-tuple-element.48), channel_id=1, source_target_pairs={{0,16},{8,24},{16,32},{24,40},{32,48},{40,56},{48,0},{56,8},{64,80... | collective-permute-start | bytes 983048 | tf_op jit(solution)/shard_map/ppermute | solution.py:434
  35.5 1.8 %collective-permute-start.11 = (bf16[10,128,128]{2,1,0:T(8,128)(2,1)S(1)}, bf16[10,128,128]{2,1,0:T(8,128)(2,1)S(1)}, u32[]{:S(2)}, u32[]{:S(2)}) collective-permute-start(bf16[10,128,128]{2,1,0:T(8,128)(2,1)S(1)} %get-tuple-element.50), channel_id=1, source_target_pairs={{0,32},{8,40},{16,48},{24,56},{32,0},{40,8},{48,16},{56,24},{64,96... | collective-permute-start | bytes 983048 | tf_op jit(solution)/shard_map/ppermute | solution.py:434
  37.2 6.3 %collective-permute-done.9.refs_5_ = bf16[10,128,128]{2,1,0:T(8,128)(2,1)S(1)} collective-permute-done((bf16[10,128,128]{2,1,0:T(8,128)(2,1)S(1)}, bf16[10,128,128]{2,1,0:T(8,128)(2,1)S(1)}, u32[]{:S(2)}, u32[]{:S(2)}) %collective-permute-start.9) | collective-permute-done | bytes 327712 | tf_op jit(solution)/shard_map/ppermute | solution.py:434
  43.5 7.6 %collective-permute-done.11.refs_7_ = bf16[10,128,128]{2,1,0:T(8,128)(2,1)S(1)} collective-permute-done((bf16[10,128,128]{2,1,0:T(8,128)(2,1)S(1)}, bf16[10,128,128]{2,1,0:T(8,128)(2,1)S(1)}, u32[]{:S(2)}, u32[]{:S(2)}) %collective-permute-start.11) | collective-permute-done | bytes 327712 | tf_op jit(solution)/shard_map/ppermute | solution.py:434
  51.5 1.7 %collective-permute-start.12 = (bf16[2,256,256]{2,1,0:T(8,128)(2,1)S(1)}, bf16[2,256,256]{2,1,0:T(8,128)(2,1)S(1)}, u32[]{:S(2)}, u32[]{:S(2)}) collective-permute-start(bf16[2,256,256]{2,1,0:T(8,128)(2,1)S(1)} %shard_map.73.refs_8_), channel_id=1, source_target_pairs={{0,8},{8,0},{16,24},{24,16},{32,40},{40,32},{48,56},{56,48},{64,72... | collective-permute-start | bytes 786440 | tf_op jit(solution)/shard_map/ppermute | solution.py:417
  53.3 0.6 shard_map.74
  53.9 1.3 %collective-permute-start.13 = (bf16[256,256]{1,0:T(8,128)(2,1)S(1)}, bf16[256,256]{1,0:T(8,128)(2,1)S(1)}, u32[]{:S(2)}, u32[]{:S(2)}) collective-permute-start(bf16[256,256]{1,0:T(8,128)(2,1)S(1)} %get-tuple-element.52), channel_id=1, source_target_pairs={{0,64},{8,72},{16,80},{24,88},{32,96},{40,104},{48,112},{56,120},{... | collective-permute-start | bytes 393224 | tf_op jit(solution)/shard_map/ppermute | solution.py:417
  55.4 1.0 %collective-permute-start.15 = (bf16[256,256]{1,0:T(8,128)(2,1)S(1)}, bf16[256,256]{1,0:T(8,128)(2,1)S(1)}, u32[]{:S(2)}, u32[]{:S(2)}) collective-permute-start(bf16[256,256]{1,0:T(8,128)(2,1)S(1)} %get-tuple-element.54), channel_id=1, source_target_pairs={{0,72},{8,64},{16,88},{24,80},{32,104},{40,96},{48,120},{56,112},{... | collective-permute-start | bytes 393224 | tf_op jit(solution)/shard_map/ppermute | solution.py:417
  56.4 1.4 %collective-permute-start.16 = (bf16[256,256]{1,0:T(8,128)(2,1)S(1)}, bf16[256,256]{1,0:T(8,128)(2,1)S(1)}, u32[]{:S(2)}, u32[]{:S(2)}) collective-permute-start(bf16[256,256]{1,0:T(8,128)(2,1)S(1)} %get-tuple-element.55), channel_id=1, source_target_pairs={{0,200},{8,192},{16,216},{24,208},{32,232},{40,224},{48,248},{56,2... | collective-permute-start | bytes 393224 | tf_op jit(solution)/shard_map/ppermute | solution.py:417
  57.8 2.3 %collective-permute-done.12.arrived = bf16[2,256,256]{2,1,0:T(8,128)(2,1)S(1)} collective-permute-done((bf16[2,256,256]{2,1,0:T(8,128)(2,1)S(1)}, bf16[2,256,256]{2,1,0:T(8,128)(2,1)S(1)}, u32[]{:S(2)}, u32[]{:S(2)}) %collective-permute-start.12) | collective-permute-done | bytes 262176 | tf_op jit(solution)/shard_map/ppermute | solution.py:417
  60.2 1.9 %collective-permute-start.17 = (bf16[256,256]{1,0:T(8,128)(2,1)S(1)}, bf16[256,256]{1,0:T(8,128)(2,1)S(1)}, u32[]{:S(2)}, u32[]{:S(2)}) collective-permute-start(bf16[256,256]{1,0:T(8,128)(2,1)S(1)} %shard_map.75), channel_id=1, source_target_pairs={{0,128},{8,136},{16,144},{24,152},{32,160},{40,168},{48,176},{56,1... | collective-permute-start | bytes 393224 | tf_op jit(solution)/shard_map/ppermute | solution.py:417
  62.1 0.7 %collective-permute-done.15.refs_2_ = bf16[256,256]{1,0:T(8,128)(2,1)S(1)} collective-permute-done((bf16[256,256]{1,0:T(8,128)(2,1)S(1)}, bf16[256,256]{1,0:T(8,128)(2,1)S(1)}, u32[]{:S(2)}, u32[]{:S(2)}) %collective-permute-start.15) | collective-permute-done | bytes 131104 | tf_op jit(solution)/shard_map/ppermute | solution.py:417
  62.8 3.8 %collective-permute-done.16.refs_3_ = bf16[256,256]{1,0:T(8,128)(2,1)S(1)} collective-permute-done((bf16[256,256]{1,0:T(8,128)(2,1)S(1)}, bf16[256,256]{1,0:T(8,128)(2,1)S(1)}, u32[]{:S(2)}, u32[]{:S(2)}) %collective-permute-start.16) | collective-permute-done | bytes 131104 | tf_op jit(solution)/shard_map/ppermute | solution.py:417
  66.6 3.3 %collective-permute-done.17.refs_4_ = bf16[256,256]{1,0:T(8,128)(2,1)S(1)} collective-permute-done((bf16[256,256]{1,0:T(8,128)(2,1)S(1)}, bf16[256,256]{1,0:T(8,128)(2,1)S(1)}, u32[]{:S(2)}, u32[]{:S(2)}) %collective-permute-start.17) | collective-permute-done | bytes 131104 | tf_op jit(solution)/shard_map/ppermute | solution.py:417
  69.9 0.8 %shard_map.76 = f32[1,256,256]{2,1,0:T(8,128)} custom-call(f32[256,256]{1,0:T(8,128)S(1)} %get-tuple-element.51.own, bf16[2,256,256]{2,1,0:T(8,128)(2,1)S(1)} %collective-permute-done.12.arrived, bf16[256,256]{1,0:T(8,128)(2,1)S(1)} %collective-permute-done.13.refs_0_, bf16[256,256]{1,0:T(8,128)(2,1)S(1)} %collective-permute-done.14.refs_1_, ...), custom_call_target="tpu_custom_call" | custom-call | flops 524288 | bytes 1048576 | tf_op jit(solution)/shard_map/pallas_call | solution.py:401
  (21 shorter events, 2.0 us)
Async XLA Ops:
  1.1 11.8 %collective-permute-start = (bf16[8,128,128]{2,1,0:T(8,128)(2,1)S(1)}, bf16[8,128,128]{2,1,0:T(8,128)(2,1)S(1)}, u32[]{:S(2)}, u32[]{:S(2)}) collective-permute-start(bf16[8,128,128]{2,1,0:T(8,128)(2,1)S(1)} %bitcast.8), channel_id=1, source_target_pairs={{0,7},{1,2},{2,1},{3,4},{4,3},{5,6},{6,5},{7,0},{8,15},{9,10},{10,... | collective-permute-start | bytes 786440 | tf_op jit(solution)/shard_map/ppermute | solution.py:424
  5.9 5.9 %collective-permute-start.1 = (bf16[8,128,128]{2,1,0:T(8,128)(2,1)S(1)}, bf16[8,128,128]{2,1,0:T(8,128)(2,1)S(1)}, u32[]{:S(2)}, u32[]{:S(2)}) collective-permute-start(bf16[8,128,128]{2,1,0:T(8,128)(2,1)S(1)} %bitcast.9), channel_id=1, source_target_pairs={{0,1},{1,0},{2,3},{3,2},{4,5},{5,4},{6,7},{7,6},{8,9},{9,8},{10,11... | collective-permute-start | bytes 786440 | tf_op jit(solution)/shard_map/ppermute | solution.py:424
  12.2 7.2 %collective-permute-start.6 = (bf16[8,128,128]{2,1,0:T(8,128)(2,1)S(1)}, bf16[8,128,128]{2,1,0:T(8,128)(2,1)S(1)}, u32[]{:S(2)}, u32[]{:S(2)}) collective-permute-start(bf16[8,128,128]{2,1,0:T(8,128)(2,1)S(1)} %shard_map.65.after.near.edge), channel_id=1, source_target_pairs={{0,1},{1,0},{2,3},{3,2},{4,5},{5,4},{6,7},{7,6},{8,9},{9,8},{10,11... | collective-permute-start | bytes 786440 | tf_op jit(solution)/shard_map/ppermute | solution.py:424
  13.2 10.8 %collective-permute-start.5 = (bf16[8,128,128]{2,1,0:T(8,128)(2,1)S(1)}, bf16[8,128,128]{2,1,0:T(8,128)(2,1)S(1)}, u32[]{:S(2)}, u32[]{:S(2)}) collective-permute-start(bf16[8,128,128]{2,1,0:T(8,128)(2,1)S(1)} %shard_map.66.far.edge), channel_id=1, source_target_pairs={{0,7},{1,2},{2,1},{3,4},{4,3},{5,6},{6,5},{7,0},{8,15},{9,10},{10,... | collective-permute-start | bytes 786440 | tf_op jit(solution)/shard_map/ppermute | solution.py:424
  17.9 10.5 %collective-permute-start.2 = (bf16[8,128,128]{2,1,0:T(8,128)(2,1)S(1)}, bf16[8,128,128]{2,1,0:T(8,128)(2,1)S(1)}, u32[]{:S(2)}, u32[]{:S(2)}) collective-permute-start(bf16[8,128,128]{2,1,0:T(8,128)(2,1)S(1)} %get-tuple-element.41), channel_id=1, source_target_pairs={{0,16},{8,24},{16,32},{24,40},{32,48},{40,56},{48,0},{56,8},{64,80... | collective-permute-start | bytes 786440 | tf_op jit(solution)/shard_map/ppermute | solution.py:434
  19.3 9.2 %collective-permute-start.3 = (bf16[8,128,128]{2,1,0:T(8,128)(2,1)S(1)}, bf16[8,128,128]{2,1,0:T(8,128)(2,1)S(1)}, u32[]{:S(2)}, u32[]{:S(2)}) collective-permute-start(bf16[8,128,128]{2,1,0:T(8,128)(2,1)S(1)} %get-tuple-element.42), channel_id=1, source_target_pairs={{0,48},{8,56},{16,0},{24,8},{32,16},{40,24},{48,32},{56,40},{64,11... | collective-permute-start | bytes 786440 | tf_op jit(solution)/shard_map/ppermute | solution.py:434
  19.8 8.2 %collective-permute-start.8 = (bf16[8,128,128]{2,1,0:T(8,128)(2,1)S(1)}, bf16[8,128,128]{2,1,0:T(8,128)(2,1)S(1)}, u32[]{:S(2)}, u32[]{:S(2)}) collective-permute-start(bf16[8,128,128]{2,1,0:T(8,128)(2,1)S(1)} %shard_map.68.after.edge.near), channel_id=1, source_target_pairs={{0,1},{1,0},{2,3},{3,2},{4,5},{5,4},{6,7},{7,6},{8,9},{9,8},{10,11... | collective-permute-start | bytes 786440 | tf_op jit(solution)/shard_map/ppermute | solution.py:424
  19.9 11.9 %collective-permute-start.4 = (bf16[8,128,128]{2,1,0:T(8,128)(2,1)S(1)}, bf16[8,128,128]{2,1,0:T(8,128)(2,1)S(1)}, u32[]{:S(2)}, u32[]{:S(2)}) collective-permute-start(bf16[8,128,128]{2,1,0:T(8,128)(2,1)S(1)} %get-tuple-element.43), channel_id=1, source_target_pairs={{0,32},{8,40},{16,48},{24,56},{32,0},{40,8},{48,16},{56,24},{64,96... | collective-permute-start | bytes 786440 | tf_op jit(solution)/shard_map/ppermute | solution.py:434
  24.4 8.8 %collective-permute-start.7 = (bf16[8,128,128]{2,1,0:T(8,128)(2,1)S(1)}, bf16[8,128,128]{2,1,0:T(8,128)(2,1)S(1)}, u32[]{:S(2)}, u32[]{:S(2)}) collective-permute-start(bf16[8,128,128]{2,1,0:T(8,128)(2,1)S(1)} %shard_map.69.far.edge), channel_id=1, source_target_pairs={{0,7},{1,2},{2,1},{3,4},{4,3},{5,6},{6,5},{7,0},{8,15},{9,10},{10,... | collective-permute-start | bytes 786440 | tf_op jit(solution)/shard_map/ppermute | solution.py:424
  28.1 5.1 %copy-start = (f32[128]{0:T(128)S(1)}, f32[128]{0:T(128)}, u32[]{:S(2)}) copy-start(f32[128]{0:T(128)} %param.7) | copy-start | bytes 1540
  33.5 10.0 %collective-permute-start.9 = (bf16[10,128,128]{2,1,0:T(8,128)(2,1)S(1)}, bf16[10,128,128]{2,1,0:T(8,128)(2,1)S(1)}, u32[]{:S(2)}, u32[]{:S(2)}) collective-permute-start(bf16[10,128,128]{2,1,0:T(8,128)(2,1)S(1)} %get-tuple-element.48), channel_id=1, source_target_pairs={{0,16},{8,24},{16,32},{24,40},{32,48},{40,56},{48,0},{56,8},{64,80... | collective-permute-start | bytes 983048 | tf_op jit(solution)/shard_map/ppermute | solution.py:434
  35.5 8.1 %collective-permute-start.10 = (bf16[10,128,128]{2,1,0:T(8,128)(2,1)S(1)}, bf16[10,128,128]{2,1,0:T(8,128)(2,1)S(1)}, u32[]{:S(2)}, u32[]{:S(2)}) collective-permute-start(bf16[10,128,128]{2,1,0:T(8,128)(2,1)S(1)} %get-tuple-element.49), channel_id=1, source_target_pairs={{0,48},{8,56},{16,0},{24,8},{32,16},{40,24},{48,32},{56,40},{64,11... | collective-permute-start | bytes 983048 | tf_op jit(solution)/shard_map/ppermute | solution.py:434
  35.5 15.7 %collective-permute-start.11 = (bf16[10,128,128]{2,1,0:T(8,128)(2,1)S(1)}, bf16[10,128,128]{2,1,0:T(8,128)(2,1)S(1)}, u32[]{:S(2)}, u32[]{:S(2)}) collective-permute-start(bf16[10,128,128]{2,1,0:T(8,128)(2,1)S(1)} %get-tuple-element.50), channel_id=1, source_target_pairs={{0,32},{8,40},{16,48},{24,56},{32,0},{40,8},{48,16},{56,24},{64,96... | collective-permute-start | bytes 983048 | tf_op jit(solution)/shard_map/ppermute | solution.py:434
  51.5 8.6 %collective-permute-start.12 = (bf16[2,256,256]{2,1,0:T(8,128)(2,1)S(1)}, bf16[2,256,256]{2,1,0:T(8,128)(2,1)S(1)}, u32[]{:S(2)}, u32[]{:S(2)}) collective-permute-start(bf16[2,256,256]{2,1,0:T(8,128)(2,1)S(1)} %shard_map.73.refs_8_), channel_id=1, source_target_pairs={{0,8},{8,0},{16,24},{24,16},{32,40},{40,32},{48,56},{56,48},{64,72... | collective-permute-start | bytes 786440 | tf_op jit(solution)/shard_map/ppermute | solution.py:417
  53.9 8.2 %collective-permute-start.13 = (bf16[256,256]{1,0:T(8,128)(2,1)S(1)}, bf16[256,256]{1,0:T(8,128)(2,1)S(1)}, u32[]{:S(2)}, u32[]{:S(2)}) collective-permute-start(bf16[256,256]{1,0:T(8,128)(2,1)S(1)} %get-tuple-element.52), channel_id=1, source_target_pairs={{0,64},{8,72},{16,80},{24,88},{32,96},{40,104},{48,112},{56,120},{... | collective-permute-start | bytes 393224 | tf_op jit(solution)/shard_map/ppermute | solution.py:417
  55.2 6.9 %collective-permute-start.14 = (bf16[256,256]{1,0:T(8,128)(2,1)S(1)}, bf16[256,256]{1,0:T(8,128)(2,1)S(1)}, u32[]{:S(2)}, u32[]{:S(2)}) collective-permute-start(bf16[256,256]{1,0:T(8,128)(2,1)S(1)} %get-tuple-element.53), channel_id=1, source_target_pairs={{0,192},{8,200},{16,208},{24,216},{32,224},{40,232},{48,240},{56,2... | collective-permute-start | bytes 393224 | tf_op jit(solution)/shard_map/ppermute | solution.py:417
  55.4 7.4 %collective-permute-start.15 = (bf16[256,256]{1,0:T(8,128)(2,1)S(1)}, bf16[256,256]{1,0:T(8,128)(2,1)S(1)}, u32[]{:S(2)}, u32[]{:S(2)}) collective-permute-start(bf16[256,256]{1,0:T(8,128)(2,1)S(1)} %get-tuple-element.54), channel_id=1, source_target_pairs={{0,72},{8,64},{16,88},{24,80},{32,104},{40,96},{48,120},{56,112},{... | collective-permute-start | bytes 393224 | tf_op jit(solution)/shard_map/ppermute | solution.py:417
  56.4 10.3 %collective-permute-start.16 = (bf16[256,256]{1,0:T(8,128)(2,1)S(1)}, bf16[256,256]{1,0:T(8,128)(2,1)S(1)}, u32[]{:S(2)}, u32[]{:S(2)}) collective-permute-start(bf16[256,256]{1,0:T(8,128)(2,1)S(1)} %get-tuple-element.55), channel_id=1, source_target_pairs={{0,200},{8,192},{16,216},{24,208},{32,232},{40,224},{48,248},{56,2... | collective-permute-start | bytes 393224 | tf_op jit(solution)/shard_map/ppermute | solution.py:417
  60.2 9.8 %collective-permute-start.17 = (bf16[256,256]{1,0:T(8,128)(2,1)S(1)}, bf16[256,256]{1,0:T(8,128)(2,1)S(1)}, u32[]{:S(2)}, u32[]{:S(2)}) collective-permute-start(bf16[256,256]{1,0:T(8,128)(2,1)S(1)} %shard_map.75), channel_id=1, source_target_pairs={{0,128},{8,136},{16,144},{24,152},{32,160},{40,168},{48,176},{56,1... | collective-permute-start | bytes 393224 | tf_op jit(solution)/shard_map/ppermute | solution.py:417

commit v7 on v6

--- a/solution.py
+++ b/solution.py
@@ -16,7 +16,7 @@
 
 frequency_sq = 1.0
 
-DIRECT = ((1, 0), (3, 0), (1, 1), (3, 1))
+DIRECT = ((1, 0), (3, 0), (3, 1), (1, 1))
 
 VMEM = pl.BlockSpec(memory_space=pltpu.VMEM)
 SMEM = pl.BlockSpec(memory_space=pltpu.SMEM)

time: 70.9 us -> 71.1 us (level)
  the two profiles are of different devices: /device:TPU:75 before, /device:TPU:64 now
where the time goes in v7:
time: 71.1 us; the launch traced here: 70.3 us
  starting transfers between devices  29.1 us (41%)
  waiting for transfers between devices  28.3 us (40%)
  Pallas kernels  11 us (15%)
  other arithmetic  1.77 us (2%)
    ppermute x6, waiting for transfers between devices, spread_y(): out[d] = lax.ppermute(parts[d], 'grp', pairs)  21.3 us
    ppermute x6, starting transfers between devices, shift(): return lax.ppermute(value, 'grp', pairs)  10.3 us
    ppermute x6, starting transfers between devices, spread_y(): out[d] = lax.ppermute(parts[d], 'grp', pairs)  8.65 us
    ppermute x3, starting transfers between devices, halo(): lax.ppermute(near, 'sec', near_pairs)  7.45 us
    ppermute x6, waiting for transfers between devices, shift(): return lax.ppermute(value, 'grp', pairs)  6.61 us
    pallas_call x1, Pallas kernels, inner(): pl.pallas_call(inner_kernel, out_shape=[column] * 2 + [blocks_of(48), blo...  5.22 us
    ppermute x3, starting transfers between devices, halo(): lax.ppermute(far, 'sec', far_pairs)  2.65 us
    pallas_call x5, Pallas kernels, edge(): pl.pallas_call(kernel, out_shape=blocks_of(8), in_specs=[VMEM] + [VMEM] *...  1.84 us
  transfers between devices with their start and end apart: 18, of which 7 were waited for; matrix products, arithmetic and copies ran while one was open for 1% of the time, Pallas kernels for 13%

profile of v7, /device:TPU:64, one launch (start us, length us, event | category | flops | bytes accessed | tf_op | source)
XLA Modules:
  0.0 70.3 jit_solution(12769794903433350921)
XLA Ops:
  0.0 1.1 %broadcast_select_fusion = (bf16[1024,128]{1,0:T(8,128)(2,1)S(1)}, bf16[1024,128]{1,0:T(8,128)(2,1)S(1)}) fusion(pred[]{:T(512)S(6)} %eq.5, bf16[8192,128]{1,0:T(8,128)(2,1)} %param.6), kind=kLoop, calls=%fused_computation | loop fusion | flops 262144 | bytes 1048577 | tf_op jit(solution)/shard_map/jit(_where)/select_n | solution.py:446
  1.2 4.6 %collective-permute-start.1 = (bf16[8,128,128]{2,1,0:T(8,128)(2,1)S(1)}, bf16[8,128,128]{2,1,0:T(8,128)(2,1)S(1)}, u32[]{:S(2)}, u32[]{:S(2)}) collective-permute-start(bf16[8,128,128]{2,1,0:T(8,128)(2,1)S(1)} %bitcast.9), channel_id=1, source_target_pairs={{0,1},{1,0},{2,3},{3,2},{4,5},{5,4},{6,7},{7,6},{8,9},{9,8},{10,11... | collective-permute-start | bytes 786440 | tf_op jit(solution)/shard_map/ppermute | solution.py:424
  5.8 0.7 %compare_select_fusion.4 = (s32[1,64]{1,0:T(1,128)S(1)}, s32[1,64]{1,0:T(1,128)S(1)}) fusion(s32[2,64]{1,0:T(2,128)} %bitcast.10, s32[]{:T(128)S(6)} %mul.3, s32[2,64]{1,0:T(2,128)} %bitcast.11), kind=kLoop, calls=%fused_computation.6 | loop fusion | flops 1344 | bytes 1028 | tf_op jit(solution)/shard_map/jit(_where)/select_n | solution.py:53
  6.5 5.2 %shard_map.64 = (s32[64,128]{1,0:T(8,128)S(1)}, s32[64,128]{1,0:T(8,128)S(1)}, bf16[48,128,128]{2,1,0:T(8,128)(2,1)S(1)}, bf16[32,128,128]{2,1,0:T(8,128)(2,1)S(...) custom-call(s32[1,64]{1,0:T(1,128)S(1)} %get-tuple-element.60.s_row,, ...), custom_call_target="tpu_custom_call" | custom-call | flops 805306368 | bytes 14680064 | tf_op jit(solution)/shard_map/pallas_call | solution.py:155
  11.7 0.4 shard_map.65.after.near.edge
  12.2 0.4 shard_map.66.far.edge
  12.6 1.0 %collective-permute-start.5 = (bf16[8,128,128]{2,1,0:T(8,128)(2,1)S(1)}, bf16[8,128,128]{2,1,0:T(8,128)(2,1)S(1)}, u32[]{:S(2)}, u32[]{:S(2)}) collective-permute-start(bf16[8,128,128]{2,1,0:T(8,128)(2,1)S(1)} %shard_map.66.far.edge), channel_id=1, source_target_pairs={{0,7},{1,2},{2,1},{3,4},{4,3},{5,6},{6,5},{7,0},{8,15},{9,10},{10,... | collective-permute-start | bytes 786440 | tf_op jit(solution)/shard_map/ppermute | solution.py:424
  13.6 1.1 %shard_map.67 = (bf16[16,128,128]{2,1,0:T(8,128)(2,1)S(1)}, bf16[8,128,128]{2,1,0:T(8,128)(2,1)S(1)}, bf16[8,128,128]{2,1,0:T(8,128)(2,1)S(1)}, bf16[8,128,128]{2,1,0:T(8,128)(2,1)S(1)}, bf16[8,128,128]{2,1,0:T(8,128)(2,1)S(1)}) custom-call(s32[64,128]{1,0:T(8,128)S(1)} %get-tuple-element.31.index.s_index, s32[64,128]{1,0:T(8,128)S(1)} %get-tuple-element.32.v_index.index, ...), custom_call_target="tpu_custom_call" | custom-call | flops 268435456 | bytes 8388608 | tf_op jit(solution)/shard_map/pallas_call | solution.py:258
  14.7 1.7 %collective-permute-start.2 = (bf16[8,128,128]{2,1,0:T(8,128)(2,1)S(1)}, bf16[8,128,128]{2,1,0:T(8,128)(2,1)S(1)}, u32[]{:S(2)}, u32[]{:S(2)}) collective-permute-start(bf16[8,128,128]{2,1,0:T(8,128)(2,1)S(1)} %get-tuple-element.41), channel_id=1, source_target_pairs={{0,16},{8,24},{16,32},{24,40},{32,48},{40,56},{48,0},{56,8},{64,80... | collective-permute-start | bytes 786440 | tf_op jit(solution)/shard_map/ppermute | solution.py:434
  16.3 1.7 %collective-permute-start.3 = (bf16[8,128,128]{2,1,0:T(8,128)(2,1)S(1)}, bf16[8,128,128]{2,1,0:T(8,128)(2,1)S(1)}, u32[]{:S(2)}, u32[]{:S(2)}) collective-permute-start(bf16[8,128,128]{2,1,0:T(8,128)(2,1)S(1)} %get-tuple-element.42), channel_id=1, source_target_pairs={{0,48},{8,56},{16,0},{24,8},{32,16},{40,24},{48,32},{56,40},{64,11... | collective-permute-start | bytes 786440 | tf_op jit(solution)/shard_map/ppermute | solution.py:434
  18.4 2.8 %collective-permute-start.8 = (bf16[8,128,128]{2,1,0:T(8,128)(2,1)S(1)}, bf16[8,128,128]{2,1,0:T(8,128)(2,1)S(1)}, u32[]{:S(2)}, u32[]{:S(2)}) collective-permute-start(bf16[8,128,128]{2,1,0:T(8,128)(2,1)S(1)} %shard_map.68.after.edge.near), channel_id=1, source_target_pairs={{0,1},{1,0},{2,3},{3,2},{4,5},{5,4},{6,7},{7,6},{8,9},{9,8},{10,11... | collective-permute-start | bytes 786440 | tf_op jit(solution)/shard_map/ppermute | solution.py:424
  21.1 1.8 %collective-permute-start.4 = (bf16[8,128,128]{2,1,0:T(8,128)(2,1)S(1)}, bf16[8,128,128]{2,1,0:T(8,128)(2,1)S(1)}, u32[]{:S(2)}, u32[]{:S(2)}) collective-permute-start(bf16[8,128,128]{2,1,0:T(8,128)(2,1)S(1)} %get-tuple-element.43), channel_id=1, source_target_pairs={{0,32},{8,40},{16,48},{24,56},{32,0},{40,8},{48,16},{56,24},{64,96... | collective-permute-start | bytes 786440 | tf_op jit(solution)/shard_map/ppermute | solution.py:434
  23.0 0.4 shard_map.69.far.edge
  23.4 1.6 %collective-permute-start.7 = (bf16[8,128,128]{2,1,0:T(8,128)(2,1)S(1)}, bf16[8,128,128]{2,1,0:T(8,128)(2,1)S(1)}, u32[]{:S(2)}, u32[]{:S(2)}) collective-permute-start(bf16[8,128,128]{2,1,0:T(8,128)(2,1)S(1)} %shard_map.69.far.edge), channel_id=1, source_target_pairs={{0,7},{1,2},{2,1},{3,4},{4,3},{5,6},{6,5},{7,0},{8,15},{9,10},{10,... | collective-permute-start | bytes 786440 | tf_op jit(solution)/shard_map/ppermute | solution.py:424
  24.9 0.6 shard_map.71.layer3
  25.5 0.4 shard_map.70.near_rows
  25.9 6.0 %collective-permute-done.4.after3.refs_3_ = bf16[8,128,128]{2,1,0:T(8,128)(2,1)S(1)} collective-permute-done((bf16[8,128,128]{2,1,0:T(8,128)(2,1)S(1)}, bf16[8,128,128]{2,1,0:T(8,128)(2,1)S(1)}, u32[]{:S(2)}, u32[]{:S(2)}) %collective-permute-start.4) | collective-permute-done | bytes 262176 | tf_op jit(solution)/shard_map/ppermute | solution.py:434
  31.9 0.4 collective-permute-done.7.halo
  32.3 0.4 shard_map.72
  32.7 0.4 collective-permute-start.9
  33.1 3.1 %collective-permute-start.10 = (bf16[10,128,128]{2,1,0:T(8,128)(2,1)S(1)}, bf16[10,128,128]{2,1,0:T(8,128)(2,1)S(1)}, u32[]{:S(2)}, u32[]{:S(2)}) collective-permute-start(bf16[10,128,128]{2,1,0:T(8,128)(2,1)S(1)} %get-tuple-element.49), channel_id=1, source_target_pairs={{0,48},{8,56},{16,0},{24,8},{32,16},{40,24},{48,32},{56,40},{64,11... | collective-permute-start | bytes 983048 | tf_op jit(solution)/shard_map/ppermute | solution.py:434
  36.2 15.3 %collective-permute-done.9.refs_5_ = bf16[10,128,128]{2,1,0:T(8,128)(2,1)S(1)} collective-permute-done((bf16[10,128,128]{2,1,0:T(8,128)(2,1)S(1)}, bf16[10,128,128]{2,1,0:T(8,128)(2,1)S(1)}, u32[]{:S(2)}, u32[]{:S(2)}) %collective-permute-start.9) | collective-permute-done | bytes 327712 | tf_op jit(solution)/shard_map/ppermute | solution.py:434
  52.0 0.6 shard_map.74
  52.6 1.6 %collective-permute-start.13 = (bf16[256,256]{1,0:T(8,128)(2,1)S(1)}, bf16[256,256]{1,0:T(8,128)(2,1)S(1)}, u32[]{:S(2)}, u32[]{:S(2)}) collective-permute-start(bf16[256,256]{1,0:T(8,128)(2,1)S(1)} %get-tuple-element.52), channel_id=1, source_target_pairs={{0,64},{8,72},{16,80},{24,88},{32,96},{40,104},{48,112},{56,120},{... | collective-permute-start | bytes 393224 | tf_op jit(solution)/shard_map/ppermute | solution.py:417
  54.2 1.7 %collective-permute-start.14 = (bf16[256,256]{1,0:T(8,128)(2,1)S(1)}, bf16[256,256]{1,0:T(8,128)(2,1)S(1)}, u32[]{:S(2)}, u32[]{:S(2)}) collective-permute-start(bf16[256,256]{1,0:T(8,128)(2,1)S(1)} %get-tuple-element.53), channel_id=1, source_target_pairs={{0,192},{8,200},{16,208},{24,216},{32,224},{40,232},{48,240},{56,2... | collective-permute-start | bytes 393224 | tf_op jit(solution)/shard_map/ppermute | solution.py:417
  55.9 3.0 %collective-permute-start.15 = (bf16[256,256]{1,0:T(8,128)(2,1)S(1)}, bf16[256,256]{1,0:T(8,128)(2,1)S(1)}, u32[]{:S(2)}, u32[]{:S(2)}) collective-permute-start(bf16[256,256]{1,0:T(8,128)(2,1)S(1)} %get-tuple-element.54), channel_id=1, source_target_pairs={{0,200},{8,192},{16,216},{24,208},{32,232},{40,224},{48,248},{56,2... | collective-permute-start | bytes 393224 | tf_op jit(solution)/shard_map/ppermute | solution.py:417
  58.9 1.4 %collective-permute-done.12.arrived = bf16[2,256,256]{2,1,0:T(8,128)(2,1)S(1)} collective-permute-done((bf16[2,256,256]{2,1,0:T(8,128)(2,1)S(1)}, bf16[2,256,256]{2,1,0:T(8,128)(2,1)S(1)}, u32[]{:S(2)}, u32[]{:S(2)}) %collective-permute-start.12) | collective-permute-done | bytes 262176 | tf_op jit(solution)/shard_map/ppermute | solution.py:417
  60.3 3.9 %collective-permute-start.17 = (bf16[256,256]{1,0:T(8,128)(2,1)S(1)}, bf16[256,256]{1,0:T(8,128)(2,1)S(1)}, u32[]{:S(2)}, u32[]{:S(2)}) collective-permute-start(bf16[256,256]{1,0:T(8,128)(2,1)S(1)} %shard_map.75), channel_id=1, source_target_pairs={{0,128},{8,136},{16,144},{24,152},{32,160},{40,168},{48,176},{56,1... | collective-permute-start | bytes 393224 | tf_op jit(solution)/shard_map/ppermute | solution.py:417
  64.3 0.6 collective-permute-done.15.refs_2_
  64.9 3.5 %collective-permute-done.16.refs_3_ = bf16[256,256]{1,0:T(8,128)(2,1)S(1)} collective-permute-done((bf16[256,256]{1,0:T(8,128)(2,1)S(1)}, bf16[256,256]{1,0:T(8,128)(2,1)S(1)}, u32[]{:S(2)}, u32[]{:S(2)}) %collective-permute-start.16) | collective-permute-done | bytes 131104 | tf_op jit(solution)/shard_map/ppermute | solution.py:417
  68.4 1.1 %collective-permute-done.17.refs_4_ = bf16[256,256]{1,0:T(8,128)(2,1)S(1)} collective-permute-done((bf16[256,256]{1,0:T(8,128)(2,1)S(1)}, bf16[256,256]{1,0:T(8,128)(2,1)S(1)}, u32[]{:S(2)}, u32[]{:S(2)}) %collective-permute-start.17) | collective-permute-done | bytes 131104 | tf_op jit(solution)/shard_map/ppermute | solution.py:417
  69.5 0.8 %shard_map.76 = f32[1,256,256]{2,1,0:T(8,128)} custom-call(f32[256,256]{1,0:T(8,128)S(1)} %get-tuple-element.51.own, bf16[2,256,256]{2,1,0:T(8,128)(2,1)S(1)} %collective-permute-done.12.arrived, bf16[256,256]{1,0:T(8,128)(2,1)S(1)} %collective-permute-done.13.refs_0_, bf16[256,256]{1,0:T(8,128)(2,1)S(1)} %collective-permute-done.14.refs_1_, ...), custom_call_target="tpu_custom_call" | custom-call | flops 524288 | bytes 1048576 | tf_op jit(solution)/shard_map/pallas_call | solution.py:401
  (21 shorter events, 1.1 us)
Async XLA Ops:
  1.1 11.1 %collective-permute-start = (bf16[8,128,128]{2,1,0:T(8,128)(2,1)S(1)}, bf16[8,128,128]{2,1,0:T(8,128)(2,1)S(1)}, u32[]{:S(2)}, u32[]{:S(2)}) collective-permute-start(bf16[8,128,128]{2,1,0:T(8,128)(2,1)S(1)} %bitcast.8), channel_id=1, source_target_pairs={{0,7},{1,2},{2,1},{3,4},{4,3},{5,6},{6,5},{7,0},{8,15},{9,10},{10,... | collective-permute-start | bytes 786440 | tf_op jit(solution)/shard_map/ppermute | solution.py:424
  1.2 10.5 %collective-permute-start.1 = (bf16[8,128,128]{2,1,0:T(8,128)(2,1)S(1)}, bf16[8,128,128]{2,1,0:T(8,128)(2,1)S(1)}, u32[]{:S(2)}, u32[]{:S(2)}) collective-permute-start(bf16[8,128,128]{2,1,0:T(8,128)(2,1)S(1)} %bitcast.9), channel_id=1, source_target_pairs={{0,1},{1,0},{2,3},{3,2},{4,5},{5,4},{6,7},{7,6},{8,9},{9,8},{10,11... | collective-permute-start | bytes 786440 | tf_op jit(solution)/shard_map/ppermute | solution.py:424
  12.1 5.9 %collective-permute-start.6 = (bf16[8,128,128]{2,1,0:T(8,128)(2,1)S(1)}, bf16[8,128,128]{2,1,0:T(8,128)(2,1)S(1)}, u32[]{:S(2)}, u32[]{:S(2)}) collective-permute-start(bf16[8,128,128]{2,1,0:T(8,128)(2,1)S(1)} %shard_map.65.after.near.edge), channel_id=1, source_target_pairs={{0,1},{1,0},{2,3},{3,2},{4,5},{5,4},{6,7},{7,6},{8,9},{9,8},{10,11... | collective-permute-start | bytes 786440 | tf_op jit(solution)/shard_map/ppermute | solution.py:424
  12.6 10.4 %collective-permute-start.5 = (bf16[8,128,128]{2,1,0:T(8,128)(2,1)S(1)}, bf16[8,128,128]{2,1,0:T(8,128)(2,1)S(1)}, u32[]{:S(2)}, u32[]{:S(2)}) collective-permute-start(bf16[8,128,128]{2,1,0:T(8,128)(2,1)S(1)} %shard_map.66.far.edge), channel_id=1, source_target_pairs={{0,7},{1,2},{2,1},{3,4},{4,3},{5,6},{6,5},{7,0},{8,15},{9,10},{10,... | collective-permute-start | bytes 786440 | tf_op jit(solution)/shard_map/ppermute | solution.py:424
  14.7 11.2 %collective-permute-start.2 = (bf16[8,128,128]{2,1,0:T(8,128)(2,1)S(1)}, bf16[8,128,128]{2,1,0:T(8,128)(2,1)S(1)}, u32[]{:S(2)}, u32[]{:S(2)}) collective-permute-start(bf16[8,128,128]{2,1,0:T(8,128)(2,1)S(1)} %get-tuple-element.41), channel_id=1, source_target_pairs={{0,16},{8,24},{16,32},{24,40},{32,48},{40,56},{48,0},{56,8},{64,80... | collective-permute-start | bytes 786440 | tf_op jit(solution)/shard_map/ppermute | solution.py:434
  16.3 9.6 %collective-permute-start.3 = (bf16[8,128,128]{2,1,0:T(8,128)(2,1)S(1)}, bf16[8,128,128]{2,1,0:T(8,128)(2,1)S(1)}, u32[]{:S(2)}, u32[]{:S(2)}) collective-permute-start(bf16[8,128,128]{2,1,0:T(8,128)(2,1)S(1)} %get-tuple-element.42), channel_id=1, source_target_pairs={{0,48},{8,56},{16,0},{24,8},{32,16},{40,24},{48,32},{56,40},{64,11... | collective-permute-start | bytes 786440 | tf_op jit(solution)/shard_map/ppermute | solution.py:434
  18.4 7.2 %collective-permute-start.8 = (bf16[8,128,128]{2,1,0:T(8,128)(2,1)S(1)}, bf16[8,128,128]{2,1,0:T(8,128)(2,1)S(1)}, u32[]{:S(2)}, u32[]{:S(2)}) collective-permute-start(bf16[8,128,128]{2,1,0:T(8,128)(2,1)S(1)} %shard_map.68.after.edge.near), channel_id=1, source_target_pairs={{0,1},{1,0},{2,3},{3,2},{4,5},{5,4},{6,7},{7,6},{8,9},{9,8},{10,11... | collective-permute-start | bytes 786440 | tf_op jit(solution)/shard_map/ppermute | solution.py:424
  21.1 10.7 %collective-permute-start.4 = (bf16[8,128,128]{2,1,0:T(8,128)(2,1)S(1)}, bf16[8,128,128]{2,1,0:T(8,128)(2,1)S(1)}, u32[]{:S(2)}, u32[]{:S(2)}) collective-permute-start(bf16[8,128,128]{2,1,0:T(8,128)(2,1)S(1)} %get-tuple-element.43), channel_id=1, source_target_pairs={{0,32},{8,40},{16,48},{24,56},{32,0},{40,8},{48,16},{56,24},{64,96... | collective-permute-start | bytes 786440 | tf_op jit(solution)/shard_map/ppermute | solution.py:434
  23.4 8.9 %collective-permute-start.7 = (bf16[8,128,128]{2,1,0:T(8,128)(2,1)S(1)}, bf16[8,128,128]{2,1,0:T(8,128)(2,1)S(1)}, u32[]{:S(2)}, u32[]{:S(2)}) collective-permute-start(bf16[8,128,128]{2,1,0:T(8,128)(2,1)S(1)} %shard_map.69.far.edge), channel_id=1, source_target_pairs={{0,7},{1,2},{2,1},{3,4},{4,3},{5,6},{6,5},{7,0},{8,15},{9,10},{10,... | collective-permute-start | bytes 786440 | tf_op jit(solution)/shard_map/ppermute | solution.py:424
  25.5 6.8 %copy-start = (f32[128]{0:T(128)S(1)}, f32[128]{0:T(128)}, u32[]{:S(2)}) copy-start(f32[128]{0:T(128)} %param.7) | copy-start | bytes 1540
  32.7 18.8 %collective-permute-start.9 = (bf16[10,128,128]{2,1,0:T(8,128)(2,1)S(1)}, bf16[10,128,128]{2,1,0:T(8,128)(2,1)S(1)}, u32[]{:S(2)}, u32[]{:S(2)}) collective-permute-start(bf16[10,128,128]{2,1,0:T(8,128)(2,1)S(1)} %get-tuple-element.48), channel_id=1, source_target_pairs={{0,16},{8,24},{16,32},{24,40},{32,48},{40,56},{48,0},{56,8},{64,80... | collective-permute-start | bytes 983048 | tf_op jit(solution)/shard_map/ppermute | solution.py:434
  33.1 18.4 %collective-permute-start.10 = (bf16[10,128,128]{2,1,0:T(8,128)(2,1)S(1)}, bf16[10,128,128]{2,1,0:T(8,128)(2,1)S(1)}, u32[]{:S(2)}, u32[]{:S(2)}) collective-permute-start(bf16[10,128,128]{2,1,0:T(8,128)(2,1)S(1)} %get-tuple-element.49), channel_id=1, source_target_pairs={{0,48},{8,56},{16,0},{24,8},{32,16},{40,24},{48,32},{56,40},{64,11... | collective-permute-start | bytes 983048 | tf_op jit(solution)/shard_map/ppermute | solution.py:434
  36.2 15.3 %collective-permute-start.11 = (bf16[10,128,128]{2,1,0:T(8,128)(2,1)S(1)}, bf16[10,128,128]{2,1,0:T(8,128)(2,1)S(1)}, u32[]{:S(2)}, u32[]{:S(2)}) collective-permute-start(bf16[10,128,128]{2,1,0:T(8,128)(2,1)S(1)} %get-tuple-element.50), channel_id=1, source_target_pairs={{0,32},{8,40},{16,48},{24,56},{32,0},{40,8},{48,16},{56,24},{64,96... | collective-permute-start | bytes 983048 | tf_op jit(solution)/shard_map/ppermute | solution.py:434
  51.9 8.4 %collective-permute-start.12 = (bf16[2,256,256]{2,1,0:T(8,128)(2,1)S(1)}, bf16[2,256,256]{2,1,0:T(8,128)(2,1)S(1)}, u32[]{:S(2)}, u32[]{:S(2)}) collective-permute-start(bf16[2,256,256]{2,1,0:T(8,128)(2,1)S(1)} %shard_map.73.refs_8_), channel_id=1, source_target_pairs={{0,8},{8,0},{16,24},{24,16},{32,40},{40,32},{48,56},{56,48},{64,72... | collective-permute-start | bytes 786440 | tf_op jit(solution)/shard_map/ppermute | solution.py:417
  52.6 11.7 %collective-permute-start.13 = (bf16[256,256]{1,0:T(8,128)(2,1)S(1)}, bf16[256,256]{1,0:T(8,128)(2,1)S(1)}, u32[]{:S(2)}, u32[]{:S(2)}) collective-permute-start(bf16[256,256]{1,0:T(8,128)(2,1)S(1)} %get-tuple-element.52), channel_id=1, source_target_pairs={{0,64},{8,72},{16,80},{24,88},{32,96},{40,104},{48,112},{56,120},{... | collective-permute-start | bytes 393224 | tf_op jit(solution)/shard_map/ppermute | solution.py:417
  54.2 10.1 %collective-permute-start.14 = (bf16[256,256]{1,0:T(8,128)(2,1)S(1)}, bf16[256,256]{1,0:T(8,128)(2,1)S(1)}, u32[]{:S(2)}, u32[]{:S(2)}) collective-permute-start(bf16[256,256]{1,0:T(8,128)(2,1)S(1)} %get-tuple-element.53), channel_id=1, source_target_pairs={{0,192},{8,200},{16,208},{24,216},{32,224},{40,232},{48,240},{56,2... | collective-permute-start | bytes 393224 | tf_op jit(solution)/shard_map/ppermute | solution.py:417
  55.9 8.9 %collective-permute-start.15 = (bf16[256,256]{1,0:T(8,128)(2,1)S(1)}, bf16[256,256]{1,0:T(8,128)(2,1)S(1)}, u32[]{:S(2)}, u32[]{:S(2)}) collective-permute-start(bf16[256,256]{1,0:T(8,128)(2,1)S(1)} %get-tuple-element.54), channel_id=1, source_target_pairs={{0,200},{8,192},{16,216},{24,208},{32,232},{40,224},{48,248},{56,2... | collective-permute-start | bytes 393224 | tf_op jit(solution)/shard_map/ppermute | solution.py:417
  58.9 9.5 %collective-permute-start.16 = (bf16[256,256]{1,0:T(8,128)(2,1)S(1)}, bf16[256,256]{1,0:T(8,128)(2,1)S(1)}, u32[]{:S(2)}, u32[]{:S(2)}) collective-permute-start(bf16[256,256]{1,0:T(8,128)(2,1)S(1)} %get-tuple-element.55), channel_id=1, source_target_pairs={{0,72},{8,64},{16,88},{24,80},{32,104},{40,96},{48,120},{56,112},{... | collective-permute-start | bytes 393224 | tf_op jit(solution)/shard_map/ppermute | solution.py:417
  60.3 9.2 %collective-permute-start.17 = (bf16[256,256]{1,0:T(8,128)(2,1)S(1)}, bf16[256,256]{1,0:T(8,128)(2,1)S(1)}, u32[]{:S(2)}, u32[]{:S(2)}) collective-permute-start(bf16[256,256]{1,0:T(8,128)(2,1)S(1)} %shard_map.75), channel_id=1, source_target_pairs={{0,128},{8,136},{16,144},{24,152},{32,160},{40,168},{48,176},{56,1... | collective-permute-start | bytes 393224 | tf_op jit(solution)/shard_map/ppermute | solution.py:417
